TPU v7x, 512 devices: a whole 4x4x16 slice. The times are simulated.
512 devices in a mesh: stn: 32 (over z_lo, y), tm: 16 (over z_hi, x, core).
Axes of the slice: x: 4, y: 4, z: 16 (z_hi: 2, z_lo: 8; z = z_hi * 8 + z_lo), core: 2. Of those that a mesh axis runs over, the one named last changes fastest.
Arguments:
- voltages: bfloat16 [2, 128, 393216], P(None, 'stn', 'tm'), may hold values from -20 to 20, as said below
Outputs:
- visibilities: float32 [2, 128, 128, 4096], P(None, 'stn', None, 'tm')
Inputs may be any that keep to these rules, and one draw needn't show every extreme that they name: `voltages`: voltage samples.
All inputs are finite; a program needn't handle non-finite values.
Results may differ from a plain program's by a relative error of at most 0.0018.
Values may be sent and summed in bfloat16 or wider, within the bound.
No kernel may reach another device: no remote copies, remote signals or barrier semaphores. Data moves between devices by JAX's collectives and lax.ppermute only.
A program may use at most 128 MiB of HBM per device.

v0:
```python
import math

import jax
import jax.numpy as jnp
from jax import lax
from jax.sharding import PartitionSpec as P

TAPS = 16
RADIX = 64
NCH = 4096


def passed_along(value, axis, steps):
    count = lax.axis_size(axis)
    leading, last = (max(0, -steps), min(count, count - steps))
    return lax.ppermute(value, axis, [(source, source + steps) for source in range(leading, last)])


def from_behind(x, axis, by):
    count = lax.axis_size(axis)
    return lax.ppermute(x, axis, [(i, (i + by) % count) for i in range(count)])


def prototype():
    total = TAPS * NCH
    index = jnp.arange(total).astype(jnp.float32)
    offset = (index + 0.5 - total / 2.0) / NCH
    window = 0.5 - 0.5 * jnp.cos(2.0 * math.pi * (index + 0.5) / total)
    return (jnp.sinc(offset) * window).reshape(TAPS, NCH)


def rotation_block(order):
    index = jnp.arange(order, dtype=jnp.int32)
    angle = 2.0 * math.pi * (index[:, None] * index[None, :] % order).astype(jnp.float32) / order
    cosine = jnp.cos(angle)
    sine = jnp.sin(angle)
    upper = jnp.concatenate([cosine, -sine], 1)
    lower = jnp.concatenate([sine, cosine], 1)
    return jnp.concatenate([upper, lower], 0)


def transform(filtered):
    inputs_dev = filtered.shape[1]
    frames_dev = filtered.shape[2]
    radix = RADIX
    table = rotation_block(radix)
    index = jnp.arange(radix, dtype=jnp.int32)
    angle = 2.0 * math.pi * (index[:, None] * index[None, :] % NCH).astype(jnp.float32) / NCH
    cos_pair = jnp.concatenate([jnp.cos(angle), jnp.cos(angle)], 1)
    sin_pair = jnp.concatenate([jnp.sin(angle), jnp.sin(angle)], 1)
    values = filtered.astype(jnp.float32).reshape(2, inputs_dev, frames_dev, radix, radix)
    values = jnp.transpose(values, (1, 2, 4, 0, 3)).reshape(
        inputs_dev, frames_dev, radix, 2 * radix
    )
    section = jnp.einsum("ifbk,kl->ifbl", values, table, precision=lax.Precision.HIGHEST)
    swapped = jnp.concatenate([section[..., radix:], -section[..., :radix]], -1)
    twisted = section * cos_pair + swapped * sin_pair
    twisted = twisted.reshape(inputs_dev, frames_dev, radix, 2, radix)
    twisted = jnp.transpose(twisted, (0, 1, 4, 3, 2)).reshape(
        inputs_dev, frames_dev, radix, 2 * radix
    )
    second = jnp.einsum("ifbk,kl->ifbl", twisted, table, precision=lax.Precision.HIGHEST)
    second = second.reshape(inputs_dev, frames_dev, radix, 2, radix)
    second = jnp.transpose(second, (3, 0, 1, 4, 2)).reshape(2, inputs_dev, frames_dev, NCH)
    return (second / radix).astype(jnp.bfloat16)


def shards(voltages):
    taps_table = prototype()
    inputs_dev = voltages.shape[1]
    frames_dev = voltages.shape[2] // NCH
    reach = (TAPS - 2) // frames_dev + 1
    earlier = []
    for distance in range(reach, 0, -1):
        earlier.append(passed_along(voltages, "tm", distance))
    before = jnp.concatenate(earlier, 2)
    history = before[:, :, before.shape[2] - (TAPS - 1) * NCH :]
    joined = jnp.concatenate([history, voltages], 2).astype(jnp.float32)
    joined = joined.reshape(2, inputs_dev, frames_dev + TAPS - 1, NCH)
    filtered = jnp.zeros((2, inputs_dev, frames_dev, NCH), jnp.float32)
    for tap in range(TAPS):
        filtered = filtered + joined[:, :, tap : tap + frames_dev, :] * taps_table[tap]
    spectra = transform(filtered.astype(jnp.bfloat16))
    turned = lax.all_to_all(spectra, "tm", split_axis=3, concat_axis=2, tiled=True)
    frames_all = turned.shape[2]
    width = turned.shape[3]
    count = lax.axis_size("stn")
    here = lax.axis_index("stn")
    zero_at = jnp.zeros((), jnp.int32)
    blank = jnp.zeros((2, inputs_dev, inputs_dev * count, width), jnp.float32)

    def correlate(other):
        products = jnp.einsum("aifc,bjfc->abijc", turned, other, preferred_element_type=jnp.float32)
        real_part = products[0, 0] + products[1, 1]
        imag_part = products[1, 0] - products[0, 1]
        return jnp.stack([real_part, imag_part]) / frames_all

    def place(accum, block, group):
        start = group * inputs_dev
        return lax.dynamic_update_slice(accum, block, (zero_at, zero_at, start, zero_at))

    accum = place(blank, correlate(turned), here)

    def advance_step(step, carry):
        moving, accum = carry
        moving = from_behind(moving, "stn", 1)
        group = (here - step) % count
        return (moving, place(accum, correlate(moving), group))

    moving, accum = lax.fori_loop(1, count, advance_step, (turned, accum))
    return accum


def solution(mesh):
    in_specs = (P(None, "stn", "tm"),)
    out_specs = P(None, "stn", None, "tm")
    return jax.shard_map(shards, mesh=mesh, in_specs=in_specs, out_specs=out_specs, check_vma=False)
```

profile of v0, /device:TPU:2, one launch (start us, length us, event | category | flops | bytes accessed | tf_op | source)
XLA Modules:
  0.0 1016.9 jit_solution(4058024477677042663)
XLA Ops:
  6.0 14.9 %collective-permute-start.3 = (bf16[2,4,24576]{2,1,0:T(4,128)(2,1)}, bf16[2,4,24576]{2,1,0:T(4,128)(2,1)S(1)}, u32[]{:S(2)}, u32[]{:S(2)}) collective-permute-start(bf16[2,4,24576]{2,1,0:T(4,128)(2,1)} %param.3), channel_id=1, source_target_pairs={{0,1},{1,2},{2,3},{3,4},{4,5},{5,6},{6,7},{7,8},{8,9},{9,10},{10,1... | collective-permute-start | bytes 1179656 | tf_op jit(solution)/shard_map/ppermute | solution.py:16
  43.8 14.1 %copy.78 = bf16[2,4,6,64,64]{2,1,0,4,3:T(4,128)(2,1)} copy(bf16[2,4,6,64,64]{3,4,0,2,1:T(8,128)(2,1)S(1)} %fusion.7) | data formatting | bytes 786432 | tf_op jit(solution)/shard_map/convert_element_type | solution.py:65
  58.0 14.3 %reshape.178 = bf16[16,2,6144]{2,1,0:T(2,128)(2,1)} reshape(bf16[4096,2,4,6]{3,2,1,0:T(4,128)(2,1)} %bitcast.66) | data formatting | bytes 786432
  72.3 25.2 %all-to-all-start = ((bf16[16,2,6144]{2,1,0:T(2,128)(2,1)}), bf16[16,2,6144]{2,1,0:T(2,128)(2,1)S(1)}, u32[]{:S(2)}, u32[]{:S(2)}) async-start(bf16[16,2,6144]{2,1,0:T(2,128)(2,1)} %reshape.178), calls=%async_computation | async-start | bytes 786432 | tf_op jit(solution)/shard_map/all_to_all | solution.py:84
  97.5 15.0 %all-to-all-done = bf16[16,2,6144]{2,1,0:T(2,128)(2,1)S(1)} async-done(((bf16[16,2,6144]{2,1,0:T(2,128)(2,1)}), bf16[16,2,6144]{2,1,0:T(2,128)(2,1)S(1)}, u32[]{:S(2)}, u32[]{:S(2)}) %all-to-all-start) | async-done | bytes 393248 | tf_op jit(solution)/shard_map/all_to_all | solution.py:84
  112.5 20.0 %reshape.179 = bf16[4096,2,4,6]{3,2,1,0:T(4,128)(2,1)} reshape(bf16[16,2,6144]{2,1,0:T(2,128)(2,1)S(1)} %all-to-all-done) | data formatting | bytes 786432
  132.5 8.8 copy.79
  142.7 4.7 convolution_bitcast_fusion.1
  149.0 866.9 %while.17 = (s32[]{:T(128)}, bf16[2,4,96,256]{2,1,0,3:T(4,128)(2,1)S(1)}, f32[2,4,128,256]{3,2,1,0:T(8,128)S(1)}, bf16[2,4,96,256]{2,1,0,3:T(4,128)(2,1)S(1)}, s...) while((s32[]{:T(128)}, ...), condition=%wide.region_1.2_spmd, body=%wide.region_0.1_spmd.sunk | while | flops 3170322 | bytes 3440960 | solution.py:110
  152.5 21.8 %collective-permute-done = bf16[2,4,96,256]{2,1,0,3:T(4,128)(2,1)S(1)} collective-permute-done((bf16[2,4,96,256]{2,1,0,3:T(4,128)(2,1)S(1)}, bf16[2,4,96,256]{2,1,0,3:T(4,128)(2,1)S(1)}, u32[]{:S(2)}, u32[]{:S(2)}) %collective-permute-start) | collective-permute-done | bytes 393248 | tf_op jit(solution)/shard_map/while/body/eval_jaxpr/ppermute | solution.py:21
  174.3 4.7 convolution_bitcast_fusion.3
  181.9 22.3 %collective-permute-done = bf16[2,4,96,256]{2,1,0,3:T(4,128)(2,1)S(1)} collective-permute-done((bf16[2,4,96,256]{2,1,0,3:T(4,128)(2,1)S(1)}, bf16[2,4,96,256]{2,1,0,3:T(4,128)(2,1)S(1)}, u32[]{:S(2)}, u32[]{:S(2)}) %collective-permute-start) | collective-permute-done | bytes 393248 | tf_op jit(solution)/shard_map/while/body/eval_jaxpr/ppermute | solution.py:21
  204.2 4.7 convolution_bitcast_fusion.3
  211.8 21.4 %collective-permute-done = bf16[2,4,96,256]{2,1,0,3:T(4,128)(2,1)S(1)} collective-permute-done((bf16[2,4,96,256]{2,1,0,3:T(4,128)(2,1)S(1)}, bf16[2,4,96,256]{2,1,0,3:T(4,128)(2,1)S(1)}, u32[]{:S(2)}, u32[]{:S(2)}) %collective-permute-start) | collective-permute-done | bytes 393248 | tf_op jit(solution)/shard_map/while/body/eval_jaxpr/ppermute | solution.py:21
  233.2 4.7 convolution_bitcast_fusion.3
  238.9 36.5 %collective-permute-start = (bf16[2,4,96,256]{2,1,0,3:T(4,128)(2,1)S(1)}, bf16[2,4,96,256]{2,1,0,3:T(4,128)(2,1)S(1)}, u32[]{:S(2)}, u32[]{:S(2)}) collective-permute-start(bf16[2,4,96,256]{2,1,0,3:T(4,128)(2,1)S(1)} %get-tuple-element.242), channel_id=1, source_target_pairs={{0,16},{16,32},{32,48},{48,64},{64,80},{80,96},{96,112},{112,128},... | collective-permute-start | bytes 1179656 | tf_op jit(solution)/shard_map/while/body/eval_jaxpr/ppermute | solution.py:21
  275.4 9.4 collective-permute-done
  290.4 6.5 collective-permute-start
  297.0 16.5 %collective-permute-done = bf16[2,4,96,256]{2,1,0,3:T(4,128)(2,1)S(1)} collective-permute-done((bf16[2,4,96,256]{2,1,0,3:T(4,128)(2,1)S(1)}, bf16[2,4,96,256]{2,1,0,3:T(4,128)(2,1)S(1)}, u32[]{:S(2)}, u32[]{:S(2)}) %collective-permute-start) | collective-permute-done | bytes 393248 | tf_op jit(solution)/shard_map/while/body/eval_jaxpr/ppermute | solution.py:21
  313.4 4.7 convolution_bitcast_fusion.3
  321.1 20.1 %collective-permute-done = bf16[2,4,96,256]{2,1,0,3:T(4,128)(2,1)S(1)} collective-permute-done((bf16[2,4,96,256]{2,1,0,3:T(4,128)(2,1)S(1)}, bf16[2,4,96,256]{2,1,0,3:T(4,128)(2,1)S(1)}, u32[]{:S(2)}, u32[]{:S(2)}) %collective-permute-start) | collective-permute-done | bytes 393248 | tf_op jit(solution)/shard_map/while/body/eval_jaxpr/ppermute | solution.py:21
  341.2 4.7 convolution_bitcast_fusion.3
  348.8 19.2 %collective-permute-done = bf16[2,4,96,256]{2,1,0,3:T(4,128)(2,1)S(1)} collective-permute-done((bf16[2,4,96,256]{2,1,0,3:T(4,128)(2,1)S(1)}, bf16[2,4,96,256]{2,1,0,3:T(4,128)(2,1)S(1)}, u32[]{:S(2)}, u32[]{:S(2)}) %collective-permute-start) | collective-permute-done | bytes 393248 | tf_op jit(solution)/shard_map/while/body/eval_jaxpr/ppermute | solution.py:21
  368.0 4.7 convolution_bitcast_fusion.3
  375.6 18.3 %collective-permute-done = bf16[2,4,96,256]{2,1,0,3:T(4,128)(2,1)S(1)} collective-permute-done((bf16[2,4,96,256]{2,1,0,3:T(4,128)(2,1)S(1)}, bf16[2,4,96,256]{2,1,0,3:T(4,128)(2,1)S(1)}, u32[]{:S(2)}, u32[]{:S(2)}) %collective-permute-start) | collective-permute-done | bytes 393248 | tf_op jit(solution)/shard_map/while/body/eval_jaxpr/ppermute | solution.py:21
  393.9 4.7 convolution_bitcast_fusion.3
  401.5 17.8 %collective-permute-done = bf16[2,4,96,256]{2,1,0,3:T(4,128)(2,1)S(1)} collective-permute-done((bf16[2,4,96,256]{2,1,0,3:T(4,128)(2,1)S(1)}, bf16[2,4,96,256]{2,1,0,3:T(4,128)(2,1)S(1)}, u32[]{:S(2)}, u32[]{:S(2)}) %collective-permute-start) | collective-permute-done | bytes 393248 | tf_op jit(solution)/shard_map/while/body/eval_jaxpr/ppermute | solution.py:21
  419.3 4.7 convolution_bitcast_fusion.3
  426.9 17.8 %collective-permute-done = bf16[2,4,96,256]{2,1,0,3:T(4,128)(2,1)S(1)} collective-permute-done((bf16[2,4,96,256]{2,1,0,3:T(4,128)(2,1)S(1)}, bf16[2,4,96,256]{2,1,0,3:T(4,128)(2,1)S(1)}, u32[]{:S(2)}, u32[]{:S(2)}) %collective-permute-start) | collective-permute-done | bytes 393248 | tf_op jit(solution)/shard_map/while/body/eval_jaxpr/ppermute | solution.py:21
  444.8 4.7 convolution_bitcast_fusion.3
  452.4 17.8 %collective-permute-done = bf16[2,4,96,256]{2,1,0,3:T(4,128)(2,1)S(1)} collective-permute-done((bf16[2,4,96,256]{2,1,0,3:T(4,128)(2,1)S(1)}, bf16[2,4,96,256]{2,1,0,3:T(4,128)(2,1)S(1)}, u32[]{:S(2)}, u32[]{:S(2)}) %collective-permute-start) | collective-permute-done | bytes 393248 | tf_op jit(solution)/shard_map/while/body/eval_jaxpr/ppermute | solution.py:21
  470.2 4.7 convolution_bitcast_fusion.3
  477.8 17.8 %collective-permute-done = bf16[2,4,96,256]{2,1,0,3:T(4,128)(2,1)S(1)} collective-permute-done((bf16[2,4,96,256]{2,1,0,3:T(4,128)(2,1)S(1)}, bf16[2,4,96,256]{2,1,0,3:T(4,128)(2,1)S(1)}, u32[]{:S(2)}, u32[]{:S(2)}) %collective-permute-start) | collective-permute-done | bytes 393248 | tf_op jit(solution)/shard_map/while/body/eval_jaxpr/ppermute | solution.py:21
  495.6 4.7 convolution_bitcast_fusion.3
  503.2 17.8 %collective-permute-done = bf16[2,4,96,256]{2,1,0,3:T(4,128)(2,1)S(1)} collective-permute-done((bf16[2,4,96,256]{2,1,0,3:T(4,128)(2,1)S(1)}, bf16[2,4,96,256]{2,1,0,3:T(4,128)(2,1)S(1)}, u32[]{:S(2)}, u32[]{:S(2)}) %collective-permute-start) | collective-permute-done | bytes 393248 | tf_op jit(solution)/shard_map/while/body/eval_jaxpr/ppermute | solution.py:21
  521.1 4.7 convolution_bitcast_fusion.3
  528.7 17.8 %collective-permute-done = bf16[2,4,96,256]{2,1,0,3:T(4,128)(2,1)S(1)} collective-permute-done((bf16[2,4,96,256]{2,1,0,3:T(4,128)(2,1)S(1)}, bf16[2,4,96,256]{2,1,0,3:T(4,128)(2,1)S(1)}, u32[]{:S(2)}, u32[]{:S(2)}) %collective-permute-start) | collective-permute-done | bytes 393248 | tf_op jit(solution)/shard_map/while/body/eval_jaxpr/ppermute | solution.py:21
  546.5 4.7 convolution_bitcast_fusion.3
  554.1 17.8 %collective-permute-done = bf16[2,4,96,256]{2,1,0,3:T(4,128)(2,1)S(1)} collective-permute-done((bf16[2,4,96,256]{2,1,0,3:T(4,128)(2,1)S(1)}, bf16[2,4,96,256]{2,1,0,3:T(4,128)(2,1)S(1)}, u32[]{:S(2)}, u32[]{:S(2)}) %collective-permute-start) | collective-permute-done | bytes 393248 | tf_op jit(solution)/shard_map/while/body/eval_jaxpr/ppermute | solution.py:21
  572.0 4.7 convolution_bitcast_fusion.3
  579.6 17.8 %collective-permute-done = bf16[2,4,96,256]{2,1,0,3:T(4,128)(2,1)S(1)} collective-permute-done((bf16[2,4,96,256]{2,1,0,3:T(4,128)(2,1)S(1)}, bf16[2,4,96,256]{2,1,0,3:T(4,128)(2,1)S(1)}, u32[]{:S(2)}, u32[]{:S(2)}) %collective-permute-start) | collective-permute-done | bytes 393248 | tf_op jit(solution)/shard_map/while/body/eval_jaxpr/ppermute | solution.py:21
  597.4 4.7 convolution_bitcast_fusion.3
  605.0 17.8 %collective-permute-done = bf16[2,4,96,256]{2,1,0,3:T(4,128)(2,1)S(1)} collective-permute-done((bf16[2,4,96,256]{2,1,0,3:T(4,128)(2,1)S(1)}, bf16[2,4,96,256]{2,1,0,3:T(4,128)(2,1)S(1)}, u32[]{:S(2)}, u32[]{:S(2)}) %collective-permute-start) | collective-permute-done | bytes 393248 | tf_op jit(solution)/shard_map/while/body/eval_jaxpr/ppermute | solution.py:21
  622.8 4.7 convolution_bitcast_fusion.3
  630.4 17.8 %collective-permute-done = bf16[2,4,96,256]{2,1,0,3:T(4,128)(2,1)S(1)} collective-permute-done((bf16[2,4,96,256]{2,1,0,3:T(4,128)(2,1)S(1)}, bf16[2,4,96,256]{2,1,0,3:T(4,128)(2,1)S(1)}, u32[]{:S(2)}, u32[]{:S(2)}) %collective-permute-start) | collective-permute-done | bytes 393248 | tf_op jit(solution)/shard_map/while/body/eval_jaxpr/ppermute | solution.py:21
  648.3 4.7 convolution_bitcast_fusion.3
  655.9 17.8 %collective-permute-done = bf16[2,4,96,256]{2,1,0,3:T(4,128)(2,1)S(1)} collective-permute-done((bf16[2,4,96,256]{2,1,0,3:T(4,128)(2,1)S(1)}, bf16[2,4,96,256]{2,1,0,3:T(4,128)(2,1)S(1)}, u32[]{:S(2)}, u32[]{:S(2)}) %collective-permute-start) | collective-permute-done | bytes 393248 | tf_op jit(solution)/shard_map/while/body/eval_jaxpr/ppermute | solution.py:21
  673.7 4.7 convolution_bitcast_fusion.3
  681.3 17.8 %collective-permute-done = bf16[2,4,96,256]{2,1,0,3:T(4,128)(2,1)S(1)} collective-permute-done((bf16[2,4,96,256]{2,1,0,3:T(4,128)(2,1)S(1)}, bf16[2,4,96,256]{2,1,0,3:T(4,128)(2,1)S(1)}, u32[]{:S(2)}, u32[]{:S(2)}) %collective-permute-start) | collective-permute-done | bytes 393248 | tf_op jit(solution)/shard_map/while/body/eval_jaxpr/ppermute | solution.py:21
  699.1 4.7 convolution_bitcast_fusion.3
  706.8 18.9 %collective-permute-done = bf16[2,4,96,256]{2,1,0,3:T(4,128)(2,1)S(1)} collective-permute-done((bf16[2,4,96,256]{2,1,0,3:T(4,128)(2,1)S(1)}, bf16[2,4,96,256]{2,1,0,3:T(4,128)(2,1)S(1)}, u32[]{:S(2)}, u32[]{:S(2)}) %collective-permute-start) | collective-permute-done | bytes 393248 | tf_op jit(solution)/shard_map/while/body/eval_jaxpr/ppermute | solution.py:21
  725.7 4.7 convolution_bitcast_fusion.3
  733.3 20.0 %collective-permute-done = bf16[2,4,96,256]{2,1,0,3:T(4,128)(2,1)S(1)} collective-permute-done((bf16[2,4,96,256]{2,1,0,3:T(4,128)(2,1)S(1)}, bf16[2,4,96,256]{2,1,0,3:T(4,128)(2,1)S(1)}, u32[]{:S(2)}, u32[]{:S(2)}) %collective-permute-start) | collective-permute-done | bytes 393248 | tf_op jit(solution)/shard_map/while/body/eval_jaxpr/ppermute | solution.py:21
  753.3 4.7 convolution_bitcast_fusion.3
  760.9 21.1 %collective-permute-done = bf16[2,4,96,256]{2,1,0,3:T(4,128)(2,1)S(1)} collective-permute-done((bf16[2,4,96,256]{2,1,0,3:T(4,128)(2,1)S(1)}, bf16[2,4,96,256]{2,1,0,3:T(4,128)(2,1)S(1)}, u32[]{:S(2)}, u32[]{:S(2)}) %collective-permute-start) | collective-permute-done | bytes 393248 | tf_op jit(solution)/shard_map/while/body/eval_jaxpr/ppermute | solution.py:21
  782.0 4.7 convolution_bitcast_fusion.3
  789.6 22.2 %collective-permute-done = bf16[2,4,96,256]{2,1,0,3:T(4,128)(2,1)S(1)} collective-permute-done((bf16[2,4,96,256]{2,1,0,3:T(4,128)(2,1)S(1)}, bf16[2,4,96,256]{2,1,0,3:T(4,128)(2,1)S(1)}, u32[]{:S(2)}, u32[]{:S(2)}) %collective-permute-start) | collective-permute-done | bytes 393248 | tf_op jit(solution)/shard_map/while/body/eval_jaxpr/ppermute | solution.py:21
  819.4 23.3 %collective-permute-done = bf16[2,4,96,256]{2,1,0,3:T(4,128)(2,1)S(1)} collective-permute-done((bf16[2,4,96,256]{2,1,0,3:T(4,128)(2,1)S(1)}, bf16[2,4,96,256]{2,1,0,3:T(4,128)(2,1)S(1)}, u32[]{:S(2)}, u32[]{:S(2)}) %collective-permute-start) | collective-permute-done | bytes 393248 | tf_op jit(solution)/shard_map/while/body/eval_jaxpr/ppermute | solution.py:21
  850.3 22.6 %collective-permute-done = bf16[2,4,96,256]{2,1,0,3:T(4,128)(2,1)S(1)} collective-permute-done((bf16[2,4,96,256]{2,1,0,3:T(4,128)(2,1)S(1)}, bf16[2,4,96,256]{2,1,0,3:T(4,128)(2,1)S(1)}, u32[]{:S(2)}, u32[]{:S(2)}) %collective-permute-start) | collective-permute-done | bytes 393248 | tf_op jit(solution)/shard_map/while/body/eval_jaxpr/ppermute | solution.py:21
  880.5 21.8 %collective-permute-done = bf16[2,4,96,256]{2,1,0,3:T(4,128)(2,1)S(1)} collective-permute-done((bf16[2,4,96,256]{2,1,0,3:T(4,128)(2,1)S(1)}, bf16[2,4,96,256]{2,1,0,3:T(4,128)(2,1)S(1)}, u32[]{:S(2)}, u32[]{:S(2)}) %collective-permute-start) | collective-permute-done | bytes 393248 | tf_op jit(solution)/shard_map/while/body/eval_jaxpr/ppermute | solution.py:21
  909.9 20.8 %collective-permute-done = bf16[2,4,96,256]{2,1,0,3:T(4,128)(2,1)S(1)} collective-permute-done((bf16[2,4,96,256]{2,1,0,3:T(4,128)(2,1)S(1)}, bf16[2,4,96,256]{2,1,0,3:T(4,128)(2,1)S(1)}, u32[]{:S(2)}, u32[]{:S(2)}) %collective-permute-start) | collective-permute-done | bytes 393248 | tf_op jit(solution)/shard_map/while/body/eval_jaxpr/ppermute | solution.py:21
  938.3 19.9 %collective-permute-done = bf16[2,4,96,256]{2,1,0,3:T(4,128)(2,1)S(1)} collective-permute-done((bf16[2,4,96,256]{2,1,0,3:T(4,128)(2,1)S(1)}, bf16[2,4,96,256]{2,1,0,3:T(4,128)(2,1)S(1)}, u32[]{:S(2)}, u32[]{:S(2)}) %collective-permute-start) | collective-permute-done | bytes 393248 | tf_op jit(solution)/shard_map/while/body/eval_jaxpr/ppermute | solution.py:21
  965.8 19.0 %collective-permute-done = bf16[2,4,96,256]{2,1,0,3:T(4,128)(2,1)S(1)} collective-permute-done((bf16[2,4,96,256]{2,1,0,3:T(4,128)(2,1)S(1)}, bf16[2,4,96,256]{2,1,0,3:T(4,128)(2,1)S(1)}, u32[]{:S(2)}, u32[]{:S(2)}) %collective-permute-start) | collective-permute-done | bytes 393248 | tf_op jit(solution)/shard_map/while/body/eval_jaxpr/ppermute | solution.py:21
  992.4 17.8 %collective-permute-done = bf16[2,4,96,256]{2,1,0,3:T(4,128)(2,1)S(1)} collective-permute-done((bf16[2,4,96,256]{2,1,0,3:T(4,128)(2,1)S(1)}, bf16[2,4,96,256]{2,1,0,3:T(4,128)(2,1)S(1)}, u32[]{:S(2)}, u32[]{:S(2)}) %collective-permute-start) | collective-permute-done | bytes 393248 | tf_op jit(solution)/shard_map/while/body/eval_jaxpr/ppermute | solution.py:21
  (233 shorter events, 160.8 us)
Async XLA Ops:
  0.0 23.5 %collective-permute-start.1 = (bf16[2,4,24576]{2,1,0:T(4,128)(2,1)}, bf16[2,4,24576]{2,1,0:T(4,128)(2,1)S(1)}, u32[]{:S(2)}, u32[]{:S(2)}) collective-permute-start(bf16[2,4,24576]{2,1,0:T(4,128)(2,1)} %param.3), channel_id=1, source_target_pairs={{0,3},{1,4},{2,5},{3,6},{4,7},{5,8},{6,9},{7,10},{8,11},{9,12},{10... | collective-permute-start | bytes 1179656 | tf_op jit(solution)/shard_map/ppermute | solution.py:16
  2.9 23.0 %collective-permute-start.2 = (bf16[2,4,24576]{2,1,0:T(4,128)(2,1)}, bf16[2,4,24576]{2,1,0:T(4,128)(2,1)S(1)}, u32[]{:S(2)}, u32[]{:S(2)}) collective-permute-start(bf16[2,4,24576]{2,1,0:T(4,128)(2,1)} %param.3), channel_id=1, source_target_pairs={{0,2},{1,3},{2,4},{3,5},{4,6},{5,7},{6,8},{7,9},{8,10},{9,11},{10,... | collective-permute-start | bytes 1179656 | tf_op jit(solution)/shard_map/ppermute | solution.py:16
  6.0 21.8 %collective-permute-start.3 = (bf16[2,4,24576]{2,1,0:T(4,128)(2,1)}, bf16[2,4,24576]{2,1,0:T(4,128)(2,1)S(1)}, u32[]{:S(2)}, u32[]{:S(2)}) collective-permute-start(bf16[2,4,24576]{2,1,0:T(4,128)(2,1)} %param.3), channel_id=1, source_target_pairs={{0,1},{1,2},{2,3},{3,4},{4,5},{5,6},{6,7},{7,8},{8,9},{9,10},{10,1... | collective-permute-start | bytes 1179656 | tf_op jit(solution)/shard_map/ppermute | solution.py:16
  72.3 40.2 %all-to-all-start = ((bf16[16,2,6144]{2,1,0:T(2,128)(2,1)}), bf16[16,2,6144]{2,1,0:T(2,128)(2,1)S(1)}, u32[]{:S(2)}, u32[]{:S(2)}) async-start(bf16[16,2,6144]{2,1,0:T(2,128)(2,1)} %reshape.178), calls=%async_computation | async-start | bytes 786432 | tf_op jit(solution)/shard_map/all_to_all | solution.py:84
  149.0 25.3 %collective-permute-start = (bf16[2,4,96,256]{2,1,0,3:T(4,128)(2,1)S(1)}, bf16[2,4,96,256]{2,1,0,3:T(4,128)(2,1)S(1)}, u32[]{:S(2)}, u32[]{:S(2)}) collective-permute-start(bf16[2,4,96,256]{2,1,0,3:T(4,128)(2,1)S(1)} %get-tuple-element.242), channel_id=1, source_target_pairs={{0,16},{16,32},{32,48},{48,64},{64,80},{80,96},{96,112},{112,128},... | collective-permute-start | bytes 1179656 | tf_op jit(solution)/shard_map/while/body/eval_jaxpr/ppermute | solution.py:21
  180.0 24.2 %collective-permute-start = (bf16[2,4,96,256]{2,1,0,3:T(4,128)(2,1)S(1)}, bf16[2,4,96,256]{2,1,0,3:T(4,128)(2,1)S(1)}, u32[]{:S(2)}, u32[]{:S(2)}) collective-permute-start(bf16[2,4,96,256]{2,1,0,3:T(4,128)(2,1)S(1)} %get-tuple-element.242), channel_id=1, source_target_pairs={{0,16},{16,32},{32,48},{48,64},{64,80},{80,96},{96,112},{112,128},... | collective-permute-start | bytes 1179656 | tf_op jit(solution)/shard_map/while/body/eval_jaxpr/ppermute | solution.py:21
  209.9 23.4 %collective-permute-start = (bf16[2,4,96,256]{2,1,0,3:T(4,128)(2,1)S(1)}, bf16[2,4,96,256]{2,1,0,3:T(4,128)(2,1)S(1)}, u32[]{:S(2)}, u32[]{:S(2)}) collective-permute-start(bf16[2,4,96,256]{2,1,0,3:T(4,128)(2,1)S(1)} %get-tuple-element.242), channel_id=1, source_target_pairs={{0,16},{16,32},{32,48},{48,64},{64,80},{80,96},{96,112},{112,128},... | collective-permute-start | bytes 1179656 | tf_op jit(solution)/shard_map/while/body/eval_jaxpr/ppermute | solution.py:21
  238.9 45.9 %collective-permute-start = (bf16[2,4,96,256]{2,1,0,3:T(4,128)(2,1)S(1)}, bf16[2,4,96,256]{2,1,0,3:T(4,128)(2,1)S(1)}, u32[]{:S(2)}, u32[]{:S(2)}) collective-permute-start(bf16[2,4,96,256]{2,1,0,3:T(4,128)(2,1)S(1)} %get-tuple-element.242), channel_id=1, source_target_pairs={{0,16},{16,32},{32,48},{48,64},{64,80},{80,96},{96,112},{112,128},... | collective-permute-start | bytes 1179656 | tf_op jit(solution)/shard_map/while/body/eval_jaxpr/ppermute | solution.py:21
  290.4 23.0 %collective-permute-start = (bf16[2,4,96,256]{2,1,0,3:T(4,128)(2,1)S(1)}, bf16[2,4,96,256]{2,1,0,3:T(4,128)(2,1)S(1)}, u32[]{:S(2)}, u32[]{:S(2)}) collective-permute-start(bf16[2,4,96,256]{2,1,0,3:T(4,128)(2,1)S(1)} %get-tuple-element.242), channel_id=1, source_target_pairs={{0,16},{16,32},{32,48},{48,64},{64,80},{80,96},{96,112},{112,128},... | collective-permute-start | bytes 1179656 | tf_op jit(solution)/shard_map/while/body/eval_jaxpr/ppermute | solution.py:21
  319.1 22.1 %collective-permute-start = (bf16[2,4,96,256]{2,1,0,3:T(4,128)(2,1)S(1)}, bf16[2,4,96,256]{2,1,0,3:T(4,128)(2,1)S(1)}, u32[]{:S(2)}, u32[]{:S(2)}) collective-permute-start(bf16[2,4,96,256]{2,1,0,3:T(4,128)(2,1)S(1)} %get-tuple-element.242), channel_id=1, source_target_pairs={{0,16},{16,32},{32,48},{48,64},{64,80},{80,96},{96,112},{112,128},... | collective-permute-start | bytes 1179656 | tf_op jit(solution)/shard_map/while/body/eval_jaxpr/ppermute | solution.py:21
  346.8 21.2 %collective-permute-start = (bf16[2,4,96,256]{2,1,0,3:T(4,128)(2,1)S(1)}, bf16[2,4,96,256]{2,1,0,3:T(4,128)(2,1)S(1)}, u32[]{:S(2)}, u32[]{:S(2)}) collective-permute-start(bf16[2,4,96,256]{2,1,0,3:T(4,128)(2,1)S(1)} %get-tuple-element.242), channel_id=1, source_target_pairs={{0,16},{16,32},{32,48},{48,64},{64,80},{80,96},{96,112},{112,128},... | collective-permute-start | bytes 1179656 | tf_op jit(solution)/shard_map/while/body/eval_jaxpr/ppermute | solution.py:21
  373.6 20.2 %collective-permute-start = (bf16[2,4,96,256]{2,1,0,3:T(4,128)(2,1)S(1)}, bf16[2,4,96,256]{2,1,0,3:T(4,128)(2,1)S(1)}, u32[]{:S(2)}, u32[]{:S(2)}) collective-permute-start(bf16[2,4,96,256]{2,1,0,3:T(4,128)(2,1)S(1)} %get-tuple-element.242), channel_id=1, source_target_pairs={{0,16},{16,32},{32,48},{48,64},{64,80},{80,96},{96,112},{112,128},... | collective-permute-start | bytes 1179656 | tf_op jit(solution)/shard_map/while/body/eval_jaxpr/ppermute | solution.py:21
  399.5 19.8 %collective-permute-start = (bf16[2,4,96,256]{2,1,0,3:T(4,128)(2,1)S(1)}, bf16[2,4,96,256]{2,1,0,3:T(4,128)(2,1)S(1)}, u32[]{:S(2)}, u32[]{:S(2)}) collective-permute-start(bf16[2,4,96,256]{2,1,0,3:T(4,128)(2,1)S(1)} %get-tuple-element.242), channel_id=1, source_target_pairs={{0,16},{16,32},{32,48},{48,64},{64,80},{80,96},{96,112},{112,128},... | collective-permute-start | bytes 1179656 | tf_op jit(solution)/shard_map/while/body/eval_jaxpr/ppermute | solution.py:21
  425.0 19.8 %collective-permute-start = (bf16[2,4,96,256]{2,1,0,3:T(4,128)(2,1)S(1)}, bf16[2,4,96,256]{2,1,0,3:T(4,128)(2,1)S(1)}, u32[]{:S(2)}, u32[]{:S(2)}) collective-permute-start(bf16[2,4,96,256]{2,1,0,3:T(4,128)(2,1)S(1)} %get-tuple-element.242), channel_id=1, source_target_pairs={{0,16},{16,32},{32,48},{48,64},{64,80},{80,96},{96,112},{112,128},... | collective-permute-start | bytes 1179656 | tf_op jit(solution)/shard_map/while/body/eval_jaxpr/ppermute | solution.py:21
  450.4 19.8 %collective-permute-start = (bf16[2,4,96,256]{2,1,0,3:T(4,128)(2,1)S(1)}, bf16[2,4,96,256]{2,1,0,3:T(4,128)(2,1)S(1)}, u32[]{:S(2)}, u32[]{:S(2)}) collective-permute-start(bf16[2,4,96,256]{2,1,0,3:T(4,128)(2,1)S(1)} %get-tuple-element.242), channel_id=1, source_target_pairs={{0,16},{16,32},{32,48},{48,64},{64,80},{80,96},{96,112},{112,128},... | collective-permute-start | bytes 1179656 | tf_op jit(solution)/shard_map/while/body/eval_jaxpr/ppermute | solution.py:21
  475.8 19.8 %collective-permute-start = (bf16[2,4,96,256]{2,1,0,3:T(4,128)(2,1)S(1)}, bf16[2,4,96,256]{2,1,0,3:T(4,128)(2,1)S(1)}, u32[]{:S(2)}, u32[]{:S(2)}) collective-permute-start(bf16[2,4,96,256]{2,1,0,3:T(4,128)(2,1)S(1)} %get-tuple-element.242), channel_id=1, source_target_pairs={{0,16},{16,32},{32,48},{48,64},{64,80},{80,96},{96,112},{112,128},... | collective-permute-start | bytes 1179656 | tf_op jit(solution)/shard_map/while/body/eval_jaxpr/ppermute | solution.py:21
  501.3 19.8 %collective-permute-start = (bf16[2,4,96,256]{2,1,0,3:T(4,128)(2,1)S(1)}, bf16[2,4,96,256]{2,1,0,3:T(4,128)(2,1)S(1)}, u32[]{:S(2)}, u32[]{:S(2)}) collective-permute-start(bf16[2,4,96,256]{2,1,0,3:T(4,128)(2,1)S(1)} %get-tuple-element.242), channel_id=1, source_target_pairs={{0,16},{16,32},{32,48},{48,64},{64,80},{80,96},{96,112},{112,128},... | collective-permute-start | bytes 1179656 | tf_op jit(solution)/shard_map/while/body/eval_jaxpr/ppermute | solution.py:21
  526.7 19.8 %collective-permute-start = (bf16[2,4,96,256]{2,1,0,3:T(4,128)(2,1)S(1)}, bf16[2,4,96,256]{2,1,0,3:T(4,128)(2,1)S(1)}, u32[]{:S(2)}, u32[]{:S(2)}) collective-permute-start(bf16[2,4,96,256]{2,1,0,3:T(4,128)(2,1)S(1)} %get-tuple-element.242), channel_id=1, source_target_pairs={{0,16},{16,32},{32,48},{48,64},{64,80},{80,96},{96,112},{112,128},... | collective-permute-start | bytes 1179656 | tf_op jit(solution)/shard_map/while/body/eval_jaxpr/ppermute | solution.py:21
  552.2 19.8 %collective-permute-start = (bf16[2,4,96,256]{2,1,0,3:T(4,128)(2,1)S(1)}, bf16[2,4,96,256]{2,1,0,3:T(4,128)(2,1)S(1)}, u32[]{:S(2)}, u32[]{:S(2)}) collective-permute-start(bf16[2,4,96,256]{2,1,0,3:T(4,128)(2,1)S(1)} %get-tuple-element.242), channel_id=1, source_target_pairs={{0,16},{16,32},{32,48},{48,64},{64,80},{80,96},{96,112},{112,128},... | collective-permute-start | bytes 1179656 | tf_op jit(solution)/shard_map/while/body/eval_jaxpr/ppermute | solution.py:21
  577.6 19.8 %collective-permute-start = (bf16[2,4,96,256]{2,1,0,3:T(4,128)(2,1)S(1)}, bf16[2,4,96,256]{2,1,0,3:T(4,128)(2,1)S(1)}, u32[]{:S(2)}, u32[]{:S(2)}) collective-permute-start(bf16[2,4,96,256]{2,1,0,3:T(4,128)(2,1)S(1)} %get-tuple-element.242), channel_id=1, source_target_pairs={{0,16},{16,32},{32,48},{48,64},{64,80},{80,96},{96,112},{112,128},... | collective-permute-start | bytes 1179656 | tf_op jit(solution)/shard_map/while/body/eval_jaxpr/ppermute | solution.py:21
  603.0 19.8 %collective-permute-start = (bf16[2,4,96,256]{2,1,0,3:T(4,128)(2,1)S(1)}, bf16[2,4,96,256]{2,1,0,3:T(4,128)(2,1)S(1)}, u32[]{:S(2)}, u32[]{:S(2)}) collective-permute-start(bf16[2,4,96,256]{2,1,0,3:T(4,128)(2,1)S(1)} %get-tuple-element.242), channel_id=1, source_target_pairs={{0,16},{16,32},{32,48},{48,64},{64,80},{80,96},{96,112},{112,128},... | collective-permute-start | bytes 1179656 | tf_op jit(solution)/shard_map/while/body/eval_jaxpr/ppermute | solution.py:21
  628.5 19.8 %collective-permute-start = (bf16[2,4,96,256]{2,1,0,3:T(4,128)(2,1)S(1)}, bf16[2,4,96,256]{2,1,0,3:T(4,128)(2,1)S(1)}, u32[]{:S(2)}, u32[]{:S(2)}) collective-permute-start(bf16[2,4,96,256]{2,1,0,3:T(4,128)(2,1)S(1)} %get-tuple-element.242), channel_id=1, source_target_pairs={{0,16},{16,32},{32,48},{48,64},{64,80},{80,96},{96,112},{112,128},... | collective-permute-start | bytes 1179656 | tf_op jit(solution)/shard_map/while/body/eval_jaxpr/ppermute | solution.py:21
  653.9 19.8 %collective-permute-start = (bf16[2,4,96,256]{2,1,0,3:T(4,128)(2,1)S(1)}, bf16[2,4,96,256]{2,1,0,3:T(4,128)(2,1)S(1)}, u32[]{:S(2)}, u32[]{:S(2)}) collective-permute-start(bf16[2,4,96,256]{2,1,0,3:T(4,128)(2,1)S(1)} %get-tuple-element.242), channel_id=1, source_target_pairs={{0,16},{16,32},{32,48},{48,64},{64,80},{80,96},{96,112},{112,128},... | collective-permute-start | bytes 1179656 | tf_op jit(solution)/shard_map/while/body/eval_jaxpr/ppermute | solution.py:21
  679.4 19.8 %collective-permute-start = (bf16[2,4,96,256]{2,1,0,3:T(4,128)(2,1)S(1)}, bf16[2,4,96,256]{2,1,0,3:T(4,128)(2,1)S(1)}, u32[]{:S(2)}, u32[]{:S(2)}) collective-permute-start(bf16[2,4,96,256]{2,1,0,3:T(4,128)(2,1)S(1)} %get-tuple-element.242), channel_id=1, source_target_pairs={{0,16},{16,32},{32,48},{48,64},{64,80},{80,96},{96,112},{112,128},... | collective-permute-start | bytes 1179656 | tf_op jit(solution)/shard_map/while/body/eval_jaxpr/ppermute | solution.py:21
  704.8 20.9 %collective-permute-start = (bf16[2,4,96,256]{2,1,0,3:T(4,128)(2,1)S(1)}, bf16[2,4,96,256]{2,1,0,3:T(4,128)(2,1)S(1)}, u32[]{:S(2)}, u32[]{:S(2)}) collective-permute-start(bf16[2,4,96,256]{2,1,0,3:T(4,128)(2,1)S(1)} %get-tuple-element.242), channel_id=1, source_target_pairs={{0,16},{16,32},{32,48},{48,64},{64,80},{80,96},{96,112},{112,128},... | collective-permute-start | bytes 1179656 | tf_op jit(solution)/shard_map/while/body/eval_jaxpr/ppermute | solution.py:21
  731.3 21.9 %collective-permute-start = (bf16[2,4,96,256]{2,1,0,3:T(4,128)(2,1)S(1)}, bf16[2,4,96,256]{2,1,0,3:T(4,128)(2,1)S(1)}, u32[]{:S(2)}, u32[]{:S(2)}) collective-permute-start(bf16[2,4,96,256]{2,1,0,3:T(4,128)(2,1)S(1)} %get-tuple-element.242), channel_id=1, source_target_pairs={{0,16},{16,32},{32,48},{48,64},{64,80},{80,96},{96,112},{112,128},... | collective-permute-start | bytes 1179656 | tf_op jit(solution)/shard_map/while/body/eval_jaxpr/ppermute | solution.py:21
  758.9 23.0 %collective-permute-start = (bf16[2,4,96,256]{2,1,0,3:T(4,128)(2,1)S(1)}, bf16[2,4,96,256]{2,1,0,3:T(4,128)(2,1)S(1)}, u32[]{:S(2)}, u32[]{:S(2)}) collective-permute-start(bf16[2,4,96,256]{2,1,0,3:T(4,128)(2,1)S(1)} %get-tuple-element.242), channel_id=1, source_target_pairs={{0,16},{16,32},{32,48},{48,64},{64,80},{80,96},{96,112},{112,128},... | collective-permute-start | bytes 1179656 | tf_op jit(solution)/shard_map/while/body/eval_jaxpr/ppermute | solution.py:21
  787.6 24.1 %collective-permute-start = (bf16[2,4,96,256]{2,1,0,3:T(4,128)(2,1)S(1)}, bf16[2,4,96,256]{2,1,0,3:T(4,128)(2,1)S(1)}, u32[]{:S(2)}, u32[]{:S(2)}) collective-permute-start(bf16[2,4,96,256]{2,1,0,3:T(4,128)(2,1)S(1)} %get-tuple-element.242), channel_id=1, source_target_pairs={{0,16},{16,32},{32,48},{48,64},{64,80},{80,96},{96,112},{112,128},... | collective-permute-start | bytes 1179656 | tf_op jit(solution)/shard_map/while/body/eval_jaxpr/ppermute | solution.py:21
  817.4 25.3 %collective-permute-start = (bf16[2,4,96,256]{2,1,0,3:T(4,128)(2,1)S(1)}, bf16[2,4,96,256]{2,1,0,3:T(4,128)(2,1)S(1)}, u32[]{:S(2)}, u32[]{:S(2)}) collective-permute-start(bf16[2,4,96,256]{2,1,0,3:T(4,128)(2,1)S(1)} %get-tuple-element.242), channel_id=1, source_target_pairs={{0,16},{16,32},{32,48},{48,64},{64,80},{80,96},{96,112},{112,128},... | collective-permute-start | bytes 1179656 | tf_op jit(solution)/shard_map/while/body/eval_jaxpr/ppermute | solution.py:21
  848.3 24.6 %collective-permute-start = (bf16[2,4,96,256]{2,1,0,3:T(4,128)(2,1)S(1)}, bf16[2,4,96,256]{2,1,0,3:T(4,128)(2,1)S(1)}, u32[]{:S(2)}, u32[]{:S(2)}) collective-permute-start(bf16[2,4,96,256]{2,1,0,3:T(4,128)(2,1)S(1)} %get-tuple-element.242), channel_id=1, source_target_pairs={{0,16},{16,32},{32,48},{48,64},{64,80},{80,96},{96,112},{112,128},... | collective-permute-start | bytes 1179656 | tf_op jit(solution)/shard_map/while/body/eval_jaxpr/ppermute | solution.py:21
  878.6 23.7 %collective-permute-start = (bf16[2,4,96,256]{2,1,0,3:T(4,128)(2,1)S(1)}, bf16[2,4,96,256]{2,1,0,3:T(4,128)(2,1)S(1)}, u32[]{:S(2)}, u32[]{:S(2)}) collective-permute-start(bf16[2,4,96,256]{2,1,0,3:T(4,128)(2,1)S(1)} %get-tuple-element.242), channel_id=1, source_target_pairs={{0,16},{16,32},{32,48},{48,64},{64,80},{80,96},{96,112},{112,128},... | collective-permute-start | bytes 1179656 | tf_op jit(solution)/shard_map/while/body/eval_jaxpr/ppermute | solution.py:21
  907.9 22.8 %collective-permute-start = (bf16[2,4,96,256]{2,1,0,3:T(4,128)(2,1)S(1)}, bf16[2,4,96,256]{2,1,0,3:T(4,128)(2,1)S(1)}, u32[]{:S(2)}, u32[]{:S(2)}) collective-permute-start(bf16[2,4,96,256]{2,1,0,3:T(4,128)(2,1)S(1)} %get-tuple-element.242), channel_id=1, source_target_pairs={{0,16},{16,32},{32,48},{48,64},{64,80},{80,96},{96,112},{112,128},... | collective-permute-start | bytes 1179656 | tf_op jit(solution)/shard_map/while/body/eval_jaxpr/ppermute | solution.py:21
  936.4 21.9 %collective-permute-start = (bf16[2,4,96,256]{2,1,0,3:T(4,128)(2,1)S(1)}, bf16[2,4,96,256]{2,1,0,3:T(4,128)(2,1)S(1)}, u32[]{:S(2)}, u32[]{:S(2)}) collective-permute-start(bf16[2,4,96,256]{2,1,0,3:T(4,128)(2,1)S(1)} %get-tuple-element.242), channel_id=1, source_target_pairs={{0,16},{16,32},{32,48},{48,64},{64,80},{80,96},{96,112},{112,128},... | collective-permute-start | bytes 1179656 | tf_op jit(solution)/shard_map/while/body/eval_jaxpr/ppermute | solution.py:21
  963.9 21.0 %collective-permute-start = (bf16[2,4,96,256]{2,1,0,3:T(4,128)(2,1)S(1)}, bf16[2,4,96,256]{2,1,0,3:T(4,128)(2,1)S(1)}, u32[]{:S(2)}, u32[]{:S(2)}) collective-permute-start(bf16[2,4,96,256]{2,1,0,3:T(4,128)(2,1)S(1)} %get-tuple-element.242), channel_id=1, source_target_pairs={{0,16},{16,32},{32,48},{48,64},{64,80},{80,96},{96,112},{112,128},... | collective-permute-start | bytes 1179656 | tf_op jit(solution)/shard_map/while/body/eval_jaxpr/ppermute | solution.py:21
  990.5 19.8 %collective-permute-start = (bf16[2,4,96,256]{2,1,0,3:T(4,128)(2,1)S(1)}, bf16[2,4,96,256]{2,1,0,3:T(4,128)(2,1)S(1)}, u32[]{:S(2)}, u32[]{:S(2)}) collective-permute-start(bf16[2,4,96,256]{2,1,0,3:T(4,128)(2,1)S(1)} %get-tuple-element.242), channel_id=1, source_target_pairs={{0,16},{16,32},{32,48},{48,64},{64,80},{80,96},{96,112},{112,128},... | collective-permute-start | bytes 1179656 | tf_op jit(solution)/shard_map/while/body/eval_jaxpr/ppermute | solution.py:21
  1015.9 1.0 copy-start
where the time goes:
time: 1020 us
  waiting for transfers between devices  610 us (60%)
  matrix products  152 us (15%)
  starting transfers between devices  146 us (14%)
  local copies, waits for them, and re-layouts  88 us (9%)
  other arithmetic  18.4 us (2%)
    ppermute x31, waiting for transfers between devices, from_behind(): return lax.ppermute(x, axis, [(i, (i + by) % count) for i in range(count)])  591 us
    dot_general x32, matrix products, correlate(): jnp.einsum('aifc,bjfc->abijc', turned, other, preferred_element_type=jnp....  150 us
    ppermute x31, starting transfers between devices, from_behind(): return lax.ppermute(x, axis, [(i, (i + by) % count) for i in range(count)])  100 us
    unnamed x5, local copies, waits for them, and re-layouts  35.5 us
    all_to_all x1, starting transfers between devices, shards(): lax.all_to_all(spectra, 'tm', split_axis=3, concat_axis=2, tiled=True)  25.2 us
    ppermute x3, starting transfers between devices, passed_along(): lax.ppermute(value, axis, [(source, source + steps) for source in range(l...  20.8 us
  transfers between devices with their start and end apart: 35, of which 34 were waited for; matrix products, arithmetic and copies ran while one was open for 0% of the time, Pallas kernels for 0%

commit v1 on v0

v1 whole, which is shorter than its diff:
```python
import math

import jax
import jax.numpy as jnp
import ml_dtypes
import numpy as np
from jax import lax
from jax.experimental import pallas as pl
from jax.experimental.pallas import tpu as pltpu
from jax.sharding import Mesh
from jax.sharding import PartitionSpec as P

TAPS = 16
NCH = 4096
N1, N2 = 32, 128
STN, ZH, Q = 32, 2, 8
FRAMES = 96
BLOCK = 24
HIST = TAPS - 1
SENT = 6
PER = 4
PARAMS = pltpu.CompilerParams(vmem_limit_bytes=48 * 1024 * 1024)
F32, BF16 = jnp.float32, jnp.bfloat16
NT = (((1,), (1,)), ((), ()))


def prototype():
    index = np.arange(TAPS * NCH, dtype=np.float64)
    window = 0.5 - 0.5 * np.cos(2.0 * math.pi * (index + 0.5) / (TAPS * NCH))
    taps = np.sinc((index + 0.5 - TAPS * NCH / 2) / NCH) * window
    return taps.astype(np.float32).reshape(TAPS, N1, N2)


def halves(table):
    high = table.astype(ml_dtypes.bfloat16)
    low = (table - high.astype(np.float64)).astype(ml_dtypes.bfloat16)
    return high, low


def complex_block(angle):
    c, s = np.cos(angle), np.sin(angle)
    return np.block([[c, s], [-s, c]])


def tables():
    k1, k2 = np.arange(N1), np.arange(N2)
    first = complex_block(2 * math.pi * (np.outer(k1, k1) % N1) / N1)
    second = complex_block(2 * math.pi * (np.outer(k2, k2) % N2) / N2) / 64.0
    second = second.reshape(2, ZH, Q, 8, 2 * N2).transpose(2, 1, 0, 3, 4).reshape(2 * N2, 2 * N2)
    turn = 2 * math.pi * np.outer(k1, k2) / NCH
    first = np.concatenate(halves(first), 0)
    second = np.concatenate(halves(second), 0)
    twiddle = np.stack([np.cos(turn), np.sin(turn)]).astype(np.float32)
    return first, second, twiddle


def channelise_body(core, main, hist, taps, first, second, twiddle, out, frames, stage, turned_re, turned_im):
    @pl.when(core[0] == 0)
    def _():
        for r in range(2):
            frames[r, :HIST] = hist[r].astype(F32)
            for s in range(4):
                frames[r, HIST + SENT * s : HIST + SENT * (s + 1)] = main[s, r].astype(F32)

    @pl.when(core[0] != 0)
    def _():
        for r in range(2):
            frames[r, :3] = main[1, r, 3:].astype(F32)
            for s in range(2, 8):
                frames[r, 3 + SENT * (s - 2) : 3 + SENT * (s - 1)] = main[s, r].astype(F32)

    def pair(step, carry):
        for half in range(2):
            f = 2 * step + half
            for r in range(2):
                acc = taps[0] * frames[r, f]
                for k in range(1, TAPS):
                    acc = acc + taps[k] * frames[r, f + k]
                stage[N1 * r : N1 * (r + 1), N2 * half : N2 * (half + 1)] = acc.astype(BF16)
        both = jnp.dot(first[...], stage[...], preferred_element_type=F32)
        both = both[: 2 * N1] + both[2 * N1 :]
        for half in range(2):
            re = both[:N1, N2 * half : N2 * (half + 1)]
            im = both[N1:, N2 * half : N2 * (half + 1)]
            f = 2 * step + half
            turned_re[pl.ds(f, N1, stride=BLOCK), :] = re * twiddle[0] + im * twiddle[1]
            turned_im[pl.ds(f, N1, stride=BLOCK), :] = im * twiddle[0] - re * twiddle[1]
        return carry

    lax.fori_loop(0, BLOCK // 2, pair, 0)
    for t in range(3):
        rows = slice(256 * t, 256 * (t + 1))
        value = jnp.concatenate([turned_re[rows], turned_im[rows]], 1)
        high = value.astype(BF16)
        low = (value - high.astype(F32)).astype(BF16)
        both = lax.dot_general(second[...], high, NT, preferred_element_type=F32)
        rest = lax.dot_general(second[: 2 * N2], low, NT, preferred_element_type=F32)
        out[:, rows] = (both[: 2 * N2] + (both[2 * N2 :] + rest)).astype(BF16)


def channelise(core, main, hist, interpret=False):
    first, second, twiddle = tables()
    args = (core, main, hist, prototype(), first, second, twiddle)
    vmem = pl.BlockSpec(memory_space=pltpu.VMEM)
    return pl.pallas_call(
        channelise_body,
        out_shape=jax.ShapeDtypeStruct((2 * N2, N1 * BLOCK), BF16),
        in_specs=[pl.BlockSpec(memory_space=pltpu.SMEM)] + [vmem] * 6,
        out_specs=vmem,
        scratch_shapes=[
            pltpu.VMEM((2, BLOCK + HIST, N1, N2), F32),
            pltpu.VMEM((2 * N1, 2 * N2), BF16),
            pltpu.VMEM((N1 * BLOCK, N2), F32),
            pltpu.VMEM((N1 * BLOCK, N2), F32),
        ],
        compiler_params=PARAMS,
        interpret=interpret,
        name="channelise",
    )(*[jnp.asarray(a) for a in args])


def regroup_body(x, out):
    for z in range(ZH):
        pieces = []
        for c in range(2):
            for r in range(2):
                for i in range(PER):
                    pair = x[2 * i + c, 16 * z : 16 * z + 16, :].astype(F32)
                    pieces.append(pair[8 * r : 8 * r + 8])
        for t in range(N1 * BLOCK // 128):
            piece = jnp.concatenate([p[:, 128 * t : 128 * (t + 1)] for p in pieces], 0).T
            for part in range(16):
                row = 128 * t + 8 * part
                out[row // BLOCK, z, row % BLOCK : row % BLOCK + 8, :] = piece[8 * part : 8 * part + 8].astype(BF16)


def regroup(x, interpret=False):
    vmem = pl.BlockSpec(memory_space=pltpu.VMEM)
    return pl.pallas_call(
        regroup_body,
        out_shape=jax.ShapeDtypeStruct((STN, ZH, BLOCK, 128), BF16),
        in_specs=[vmem],
        out_specs=vmem,
        compiler_params=PARAMS,
        interpret=interpret,
        name="regroup",
    )(x)


def correlate_body(x, out, series, plain):
    most = jnp.zeros((8, 128), F32)
    zero = jnp.zeros((128 - FRAMES, 128), F32)
    for s in range(STN):
        both = jnp.concatenate([x[s, 0].astype(F32), x[s, 1].astype(F32)], 0)
        cols = jnp.concatenate([both, pltpu.roll(both, 64, 1), zero], 0)
        series[64 * s : 64 * (s + 1), :] = cols.T[:64]
    sign = jnp.where(lax.broadcasted_iota(jnp.int32, (STN, 8, 128), 1) < PER, 1.0, -1.0)
    for j in range(8):
        near = series[pl.ds(j, 8 * STN, stride=8), :].reshape(STN, 8, 128)
        far = (pltpu.roll(near, PER, 1) * sign).reshape(8 * STN, 128)
        left = jnp.concatenate([near.reshape(8 * STN, 128), far], 1).astype(BF16)
        right = []
        for r in range(2):
            rows = [series[pl.ds(32 * r + 8 * i + j, STN, stride=64), :] for i in range(PER)]
            right.append(jnp.concatenate(rows, 0))
        right = jnp.concatenate(right, 1).astype(BF16)
        tile = lax.dot_general(left, right, NT, preferred_element_type=F32) / FRAMES
        tile = tile.reshape(STN, 8, 128)
        plain[:, 8 * j : 8 * j + 8, :] = tile
        most = jnp.maximum(most, jnp.max(jnp.abs(tile), 0))
    top = jnp.max(jnp.max(most, 1, keepdims=True), 0, keepdims=True)
    power = jnp.maximum(jnp.floor(jnp.log2(jnp.maximum(top, 1e-37))) - 14.0, -126.0)
    out[:, :64, :] = plain[...] * jnp.exp2(-power).reshape(1, 1, 1)
    out[:, 64:, :] = jnp.broadcast_to(power.reshape(1, 1, 1), (STN, 8, 128))


def correlate(x, interpret=False):
    vmem = pl.BlockSpec(memory_space=pltpu.VMEM)
    return pl.pallas_call(
        correlate_body,
        out_shape=jax.ShapeDtypeStruct((STN, 72, 128), F32),
        in_specs=[vmem],
        out_specs=vmem,
        scratch_shapes=[pltpu.VMEM((64 * STN, 128), F32), pltpu.VMEM((STN, 64, 128), F32)],
        compiler_params=PARAMS,
        interpret=interpret,
        name="correlate",
    )(x)


def deliver_body(x, out, wide, order):
    for k in range(N1):
        wide[64 * k : 64 * (k + 1), :] = x[k, :64, :] * jnp.exp2(x[k, 64:65, :])
    for row in range(8):
        for half in range(2):
            cols = jnp.concatenate(
                [wide[pl.ds(8 * j + row, N1, stride=64), :] for j in range(4 * half, 4 * half + 4)], 0
            ).T
            base = 128 * (2 * row + half)
            for i in range(PER):
                order[pl.ds(base + i, STN, stride=PER), :] = cols[STN * i : STN * (i + 1)]
            out[row // PER, row % PER, :, 128 * half : 128 * (half + 1)] = order[base : base + 128, :]


def deliver(x, interpret=False):
    vmem = pl.BlockSpec(memory_space=pltpu.VMEM)
    return pl.pallas_call(
        deliver_body,
        out_shape=jax.ShapeDtypeStruct((2, PER, 128, 256), F32),
        in_specs=[vmem],
        out_specs=vmem,
        scratch_shapes=[pltpu.VMEM((64 * N1, 128), F32), pltpu.VMEM((16 * 128, 128), F32)],
        compiler_params=PARAMS,
        interpret=interpret,
        name="deliver",
    )(x)


def shards(voltages):
    frames = voltages.reshape(2, PER, SENT, N1, N2).transpose(1, 0, 2, 3, 4)
    frames = jnp.repeat(frames, 2, 0)
    half = lax.all_to_all(frames, "q", 0, 0, tiled=True)
    last = jnp.concatenate([half[5, :, 3:], half[6], half[7]], 1)
    pairs = [((0 * Q + 2 * x), (1 * Q + 2 * x)) for x in range(Q // 2)]
    hist = lax.ppermute(last, ("zh", "q"), pairs)
    core = (lax.axis_index("q") % 2).astype(jnp.int32).reshape(1)
    spectra = channelise(core, half, hist)
    spectra = lax.all_to_all(spectra.reshape(Q, 2 * N2 // Q, N1 * BLOCK), "q", 0, 0, tiled=True)
    spectra = regroup(spectra).reshape(STN * ZH, BLOCK, 128)
    spectra = lax.all_to_all(spectra, ("stn", "zh"), 0, 0, tiled=True)
    products = correlate(spectra.reshape(STN, ZH, BLOCK, 128))
    products = lax.all_to_all(products.astype(jnp.float16), "stn", 0, 0, tiled=True)
    return deliver(products.astype(F32))


def solution(mesh):
    split = Mesh(mesh.devices.reshape(STN, ZH, Q), ("stn", "zh", "q"))
    in_specs = (P(None, "stn", ("zh", "q")),)
    out_specs = P(None, "stn", None, ("zh", "q"))
    return jax.shard_map(shards, mesh=split, in_specs=in_specs, out_specs=out_specs, check_vma=False)
```

time: 1020 us -> 143 us (0.14)
  waiting for transfers between devices: 610 us -> 3.67 us
  matrix products: 152 us -> 0 us
  starting transfers between devices: 146 us -> 12 us
  blocking collectives: 0 us -> 119 us
  local copies, waits for them, and re-layouts: 88 us -> 1.62 us
  other arithmetic: 18.4 us -> 0.19 us
    ppermute x34 -> x1, waiting for transfers between devices: 595 us -> 3.67 us  [shards(): hist = lax.ppermute(last, ('zh', 'q'), pairs)]
    dot_general x34 -> x0, matrix products: 152 us -> none  [the longest x32 150 us: correlate(): jnp.einsum('aifc,bjfc->abijc', turned, other, preferred_element_type=jnp....]
    all_to_all x0 -> x4, blocking collectives: none -> 119 us  [the longest x1 50.8 us: shards(): spectra = lax.all_to_all(spectra, ('stn', 'zh'), 0, 0, tiled=True)]
    ppermute x34 -> x1, starting transfers between devices: 121 us -> 12 us  [shards(): hist = lax.ppermute(last, ('zh', 'q'), pairs)]
    unnamed x5 -> x8, local copies, waits for them, and re-layouts: 35.5 us -> 0.03 us
    all_to_all x1 -> x0, starting transfers between devices: 25.2 us -> none  [shards(): lax.all_to_all(spectra, 'tm', split_axis=3, concat_axis=2, tiled=True)]
    convert_element_type x3 -> x0, local copies, waits for them, and re-layouts: 17.7 us -> none  [the longest x1 14.1 us: transform(): return (second / radix).astype(jnp.bfloat16)]
    all_to_all x1 -> x0, waiting for transfers between devices: 15 us -> none  [shards(): lax.all_to_all(spectra, 'tm', split_axis=3, concat_axis=2, tiled=True)]
  transfers between devices with their start and end apart: 35 -> 1, of which waited for: 34 -> 1; matrix products, arithmetic and copies ran while one was open for 0% -> 0% of each run, Pallas kernels for 0% -> 0%
where the time goes in v1:
time: 143 us
  blocking collectives  119 us (83%)
  starting transfers between devices  12 us (8%)
  Pallas kernels  7.04 us (5%)
  waiting for transfers between devices  3.67 us (3%)
  local copies, waits for them, and re-layouts  1.62 us (1%)
    all_to_all x1, blocking collectives, shards(): spectra = lax.all_to_all(spectra, ('stn', 'zh'), 0, 0, tiled=True)  50.8 us
    all_to_all x1, blocking collectives, shards(): lax.all_to_all(products.astype(jnp.float16), 'stn', 0, 0, tiled=True)  36.2 us
    all_to_all x1, blocking collectives, shards(): half = lax.all_to_all(frames, 'q', 0, 0, tiled=True)  20.2 us
    ppermute x1, starting transfers between devices, shards(): hist = lax.ppermute(last, ('zh', 'q'), pairs)  12 us
    all_to_all x1, blocking collectives, shards(): lax.all_to_all(spectra.reshape(Q, 2 * N2 // Q, N1 * BLOCK), 'q', 0, 0, ti...  11.3 us
    ppermute x1, waiting for transfers between devices, shards(): hist = lax.ppermute(last, ('zh', 'q'), pairs)  3.67 us
    pallas_call x1, Pallas kernels, channelise(): pl.pallas_call(channelise_body, out_shape=jax.ShapeDtypeStruct((2 * N2, N...  3.46 us
  transfers between devices with their start and end apart: 1, of which 1 were waited for; matrix products, arithmetic and copies ran while one was open for 0% of the time, Pallas kernels for 0%

profile of v1, /device:TPU:2, one launch (start us, length us, event | category | flops | bytes accessed | tf_op | source)
XLA Modules:
  0.0 143.2 jit_solution(7955063294735838083)
XLA Ops:
  0.0 1.4 reshape.19
  1.4 0.1 broadcast_in_dim.3
  1.6 0.0 copy-start
  1.6 0.0 copy-start.1
  1.6 0.0 copy-start.2
  1.6 0.0 copy-start.3
  1.6 20.2 %all_to_all.20.main = bf16[8,2,6,32,128]{4,3,2,1,0:T(8,128)(2,1)S(1)} all-to-all(bf16[8,2,6,32,128]{4,3,2,1,0:T(8,128)(2,1)S(1)} %bitcast.15), channel_id=1, replica_groups=mesh['stn'=32,'zh'=2,'q'=8] {'q'}, dimensions={0} | all-to-all | bytes 1572864 | tf_op jit(solution)/shard_map/all_to_all | solution.py:222
  22.0 12.0 %collective-permute-start = (bf16[2,15,32,128]{3,2,1,0:T(8,128)(2,1)S(1)}, bf16[2,15,32,128]{3,2,1,0:T(8,128)(2,1)S(1)}, u32[]{:S(2)}, u32[]{:S(2)}) collective-permute-start(bf16[2,15,32,128]{3,2,1,0:T(8,128)(2,1)S(1)} %pad_maximum_fusion), channel_id=1, source_target_pairs={{0,8},{2,10},{4,12},{6,14},{16,24},{18,26},{20,28},{22,30},{32,40}... | collective-permute-start | bytes 737288 | tf_op jit(solution)/shard_map/ppermute | solution.py:225
  34.0 3.7 %collective-permute-done.hist = bf16[2,15,32,128]{3,2,1,0:T(8,128)(2,1)S(1)} collective-permute-done((bf16[2,15,32,128]{3,2,1,0:T(8,128)(2,1)S(1)}, bf16[2,15,32,128]{3,2,1,0:T(8,128)(2,1)S(1)}, u32[]{:S(2)}, u32[]{:S(2)}) %collective-permute-start) | collective-permute-done | bytes 245792 | tf_op jit(solution)/shard_map/ppermute | solution.py:225
  37.7 0.0 copy-done
  37.7 0.0 copy-done.1
  37.7 0.0 copy-done.2
  37.7 0.0 copy-done.3
  37.7 3.5 %channelise.1 = bf16[256,768]{1,0:T(8,128)(2,1)S(1)} custom-call(s32[1]{0:T(128)} %bitcast.core, bf16[8,2,6,32,128]{4,3,2,1,0:T(8,128)(2,1)S(1)} %all_to_all.20.main, bf16[2,15,32,128]{3,2,1,0:T(8,128)(2,1)S(1)} %collective-permute-done.hist, f32[16,32,128]{2,1,0:T(8,128)S(1)} %copy-done.1, bf16[128,64]{1,0:T(8,128)(2,1)S(1)} %copy-done.3, ...), custom_call_target="tpu_custom_call" | custom-call | tf_op jit(solution)/shard_map/channelise/pallas_call | solution.py:105
  41.2 11.3 %all_to_all.21.x = bf16[8,32,768]{2,1,0:T(8,128)(2,1)S(1)} all-to-all(bf16[8,32,768]{2,1,0:T(8,128)(2,1)S(1)} %bitcast.13), channel_id=1, replica_groups=mesh['stn'=32,'zh'=2,'q'=8] {'q'}, dimensions={0} | all-to-all | bytes 786432 | tf_op jit(solution)/shard_map/all_to_all | solution.py:228
  52.5 0.2 regroup.1
  52.7 50.8 %all_to_all.22 = bf16[64,24,128]{2,1,0:T(8,128)(2,1)S(1)} all-to-all(bf16[64,24,128]{2,1,0:T(8,128)(2,1)S(1)} %bitcast.12), channel_id=1, replica_groups=mesh['stn'=32,'zh'=2,'q'=8] {'stn','zh'}, dimensions={0} | all-to-all | bytes 786432 | tf_op jit(solution)/shard_map/all_to_all | solution.py:230
  103.5 1.6 %correlate.1 = f32[32,72,128]{2,1,0:T(8,128)S(1)} custom-call(bf16[32,2,24,128]{3,2,1,0:T(8,128)(2,1)S(1)} %bitcast.14), custom_call_target="tpu_custom_call" | custom-call | tf_op jit(solution)/shard_map/correlate/pallas_call | solution.py:179
  105.0 0.1 convert_element_type.6
  105.1 36.2 %all_to_all.23 = f16[32,72,128]{2,1,0:T(8,128)(2,1)S(1)} all-to-all(f16[32,72,128]{2,1,0:T(8,128)(2,1)S(1)} %convert_element_type.6), channel_id=1, replica_groups=mesh['stn'=32,'zh'=2,'q'=8] {'stn'}, dimensions={0} | all-to-all | bytes 1179648 | tf_op jit(solution)/shard_map/all_to_all | solution.py:232
  141.3 0.1 convert_element_type.7.x
  141.4 1.8 %deliver.1 = f32[2,4,128,256]{3,2,1,0:T(8,128)} custom-call(f32[32,72,128]{2,1,0:T(8,128)S(1)} %convert_element_type.7.x), custom_call_target="tpu_custom_call" | custom-call | tf_op jit(solution)/shard_map/deliver/pallas_call | solution.py:207
  (4 shorter events, 0.1 us)
Async XLA Ops:
  1.6 36.1 %copy-start = (bf16[512,256]{1,0:T(8,128)(2,1)S(1)}, bf16[512,256]{1,0:T(8,128)(2,1)}, u32[]{:S(2)}) copy-start(bf16[512,256]{1,0:T(8,128)(2,1)} %constant.27.clone.second) | copy-start | bytes 786436
  1.6 36.1 %copy-start.1 = (f32[16,32,128]{2,1,0:T(8,128)S(1)}, f32[16,32,128]{2,1,0:T(8,128)}, u32[]{:S(2)}) copy-start(f32[16,32,128]{2,1,0:T(8,128)} %constant.25.clone.taps) | copy-start | bytes 786436
  1.6 36.1 %copy-start.2 = (f32[2,32,128]{2,1,0:T(8,128)S(1)}, f32[2,32,128]{2,1,0:T(8,128)}, u32[]{:S(2)}) copy-start(f32[2,32,128]{2,1,0:T(8,128)} %constant.28.clone.twiddle) | copy-start | bytes 98308
  1.6 36.1 %copy-start.3 = (bf16[128,64]{1,0:T(8,128)(2,1)S(1)}, bf16[128,64]{1,0:T(8,128)(2,1)}, u32[]{:S(2)}) copy-start(bf16[128,64]{1,0:T(8,128)(2,1)} %constant.26.clone.first) | copy-start | bytes 49156
  22.0 15.7 %collective-permute-start = (bf16[2,15,32,128]{3,2,1,0:T(8,128)(2,1)S(1)}, bf16[2,15,32,128]{3,2,1,0:T(8,128)(2,1)S(1)}, u32[]{:S(2)}, u32[]{:S(2)}) collective-permute-start(bf16[2,15,32,128]{3,2,1,0:T(8,128)(2,1)S(1)} %pad_maximum_fusion), channel_id=1, source_target_pairs={{0,8},{2,10},{4,12},{6,14},{16,24},{18,26},{20,28},{22,30},{32,40}... | collective-permute-start | bytes 737288 | tf_op jit(solution)/shard_map/ppermute | solution.py:225

commit v2 on v1

--- a/solution.py
+++ b/solution.py
@@ -13,7 +13,7 @@
 TAPS = 16
 NCH = 4096
 N1, N2 = 32, 128
-STN, ZH, Q = 32, 2, 8
+STN, ZH, X, Q = 32, 2, 4, 8
 FRAMES = 96
 BLOCK = 24
 HIST = TAPS - 1
@@ -54,20 +54,25 @@
     return first, second, twiddle
 
 
-def channelise_body(core, main, hist, taps, first, second, twiddle, out, frames, stage, turned_re, turned_im):
+def channelise_body(core, own, other, hist, taps, first, second, twiddle, out, frames, stage, turned_re, turned_im):
+    def place(start, piece):
+        for r in range(2):
+            frames[r, start : start + piece.shape[1]] = piece[r].astype(F32)
+
     @pl.when(core[0] == 0)
     def _():
-        for r in range(2):
-            frames[r, :HIST] = hist[r].astype(F32)
-            for s in range(4):
-                frames[r, HIST + SENT * s : HIST + SENT * (s + 1)] = main[s, r].astype(F32)
+        place(0, hist)
+        for s in range(2):
+            place(HIST + 2 * SENT * s, own.at[s])
+            place(HIST + 2 * SENT * s + SENT, other.at[s])
 
     @pl.when(core[0] != 0)
     def _():
         for r in range(2):
-            frames[r, :3] = main[1, r, 3:].astype(F32)
-            for s in range(2, 8):
-                frames[r, 3 + SENT * (s - 2) : 3 + SENT * (s - 1)] = main[s, r].astype(F32)
+            frames[r, :3] = own[0, r, 3:].astype(F32)
+        for s in range(3):
+            place(3 + 2 * SENT * s, other.at[s])
+            place(3 + 2 * SENT * s + SENT, own.at[s + 1])
 
     def pair(step, carry):
         for half in range(2):
@@ -98,14 +103,14 @@
         out[:, rows] = (both[: 2 * N2] + (both[2 * N2 :] + rest)).astype(BF16)
 
 
-def channelise(core, main, hist, interpret=False):
+def channelise(core, own, other, hist, interpret=False):
     first, second, twiddle = tables()
-    args = (core, main, hist, prototype(), first, second, twiddle)
+    args = (core, own, other, hist, prototype(), first, second, twiddle)
     vmem = pl.BlockSpec(memory_space=pltpu.VMEM)
     return pl.pallas_call(
         channelise_body,
         out_shape=jax.ShapeDtypeStruct((2 * N2, N1 * BLOCK), BF16),
-        in_specs=[pl.BlockSpec(memory_space=pltpu.SMEM)] + [vmem] * 6,
+        in_specs=[pl.BlockSpec(memory_space=pltpu.SMEM)] + [vmem] * 7,
         out_specs=vmem,
         scratch_shapes=[
             pltpu.VMEM((2, BLOCK + HIST, N1, N2), F32),
@@ -216,16 +221,29 @@
     )(x)
 
 
+def last_frames(frames):
+    q = Q // X * lax.axis_index("x") + lax.axis_index("c")
+    rounds = []
+    for r in range(X):
+        piece = lax.dynamic_index_in_dim(frames, (q + r) % X, 1, False)
+        pairs = [(s, Q // X * ((s + r) % X)) for s in range(Q - 3, Q)]
+        rounds.append(lax.ppermute(piece, ("zh", "x", "c"), pairs))
+    rounds = jnp.stack(rounds)
+    parts = [
+        lax.dynamic_index_in_dim(rounds, (lax.axis_index("x") - s) % X, 0, False) for s in range(Q - 3, Q)
+    ]
+    last = jnp.concatenate([parts[0][:, 3:], parts[1], parts[2]], 1)
+    return lax.ppermute(last, ("zh", "x", "c"), [(Q // X * x, Q + Q // X * x) for x in range(X)])
+
+
 def shards(voltages):
-    frames = voltages.reshape(2, PER, SENT, N1, N2).transpose(1, 0, 2, 3, 4)
-    frames = jnp.repeat(frames, 2, 0)
-    half = lax.all_to_all(frames, "q", 0, 0, tiled=True)
-    last = jnp.concatenate([half[5, :, 3:], half[6], half[7]], 1)
-    pairs = [((0 * Q + 2 * x), (1 * Q + 2 * x)) for x in range(Q // 2)]
-    hist = lax.ppermute(last, ("zh", "q"), pairs)
-    core = (lax.axis_index("q") % 2).astype(jnp.int32).reshape(1)
-    spectra = channelise(core, half, hist)
-    spectra = lax.all_to_all(spectra.reshape(Q, 2 * N2 // Q, N1 * BLOCK), "q", 0, 0, tiled=True)
+    frames = voltages.reshape(2, PER, SENT, N1, N2)
+    hist = last_frames(frames)
+    core = lax.axis_index("c")
+    own = lax.all_to_all(frames.transpose(1, 0, 2, 3, 4), "x", 0, 0, tiled=True)
+    other = lax.ppermute(lax.dynamic_slice_in_dim(own, 1 - core, 3, 0), "c", [(0, 1), (1, 0)])
+    spectra = channelise(core.astype(jnp.int32).reshape(1), own, other, hist)
+    spectra = lax.all_to_all(spectra.reshape(Q, 2 * N2 // Q, N1 * BLOCK), ("x", "c"), 0, 0, tiled=True)
     spectra = regroup(spectra).reshape(STN * ZH, BLOCK, 128)
     spectra = lax.all_to_all(spectra, ("stn", "zh"), 0, 0, tiled=True)
     products = correlate(spectra.reshape(STN, ZH, BLOCK, 128))
@@ -234,7 +252,7 @@
 
 
 def solution(mesh):
-    split = Mesh(mesh.devices.reshape(STN, ZH, Q), ("stn", "zh", "q"))
-    in_specs = (P(None, "stn", ("zh", "q")),)
-    out_specs = P(None, "stn", None, ("zh", "q"))
+    split = Mesh(mesh.devices.reshape(STN, ZH, X, Q // X), ("stn", "zh", "x", "c"))
+    in_specs = (P(None, "stn", ("zh", "x", "c")),)
+    out_specs = P(None, "stn", None, ("zh", "x", "c"))
     return jax.shard_map(shards, mesh=split, in_specs=in_specs, out_specs=out_specs, check_vma=False)

time: 143 us -> 145 us (1.014)
  blocking collectives: 119 us -> 98.3 us
  starting transfers between devices: 12 us -> 24 us
  waiting for transfers between devices: 3.67 us -> 11.4 us
  local copies, waits for them, and re-layouts: 1.62 us -> 3.31 us
    all_to_all x2 -> x1, blocking collectives: 31.6 us -> 11.3 us  [shards(): lax.all_to_all(spectra.reshape(Q, 2 * N2 // Q, N1 * BLOCK), ('x', 'c'), 0...]
    all_to_all x0 -> x1, starting transfers between devices: none -> 10.4 us  [shards(): own = lax.all_to_all(frames.transpose(1, 0, 2, 3, 4), 'x', 0, 0, tiled=True)]
    all_to_all x0 -> x1, waiting for transfers between devices: none -> 6.57 us  [shards(): own = lax.all_to_all(frames.transpose(1, 0, 2, 3, 4), 'x', 0, 0, tiled=True)]
    ppermute x1 -> x6, starting transfers between devices: 12 us -> 13.5 us  [the longest x1 7.08 us: last_frames(): lax.ppermute(last, ('zh', 'x', 'c'), [(Q // X * x, Q + Q // X * x) for x...]
    ppermute x1 -> x6, waiting for transfers between devices: 3.67 us -> 4.8 us  [the longest x1 3.68 us: last_frames(): lax.ppermute(last, ('zh', 'x', 'c'), [(Q // X * x, Q + Q // X * x) for x...]
  transfers between devices with their start and end apart: 1 -> 7, of which waited for: 1 -> 3; matrix products, arithmetic and copies ran while one was open for 0% -> 0% of each run, Pallas kernels for 0% -> 0%
where the time goes in v2:
time: 145 us; the launch traced here: 144 us
  blocking collectives  98.3 us (68%)
  starting transfers between devices  24 us (17%)
  waiting for transfers between devices  11.4 us (8%)
  Pallas kernels  7.03 us (5%)
  local copies, waits for them, and re-layouts  3.31 us (2%)
    all_to_all x1, blocking collectives, shards(): spectra = lax.all_to_all(spectra, ('stn', 'zh'), 0, 0, tiled=True)  50.8 us
    all_to_all x1, blocking collectives, shards(): lax.all_to_all(products.astype(jnp.float16), 'stn', 0, 0, tiled=True)  36.2 us
    all_to_all x1, blocking collectives, shards(): lax.all_to_all(spectra.reshape(Q, 2 * N2 // Q, N1 * BLOCK), ('x', 'c'), 0...  11.3 us
    all_to_all x1, starting transfers between devices, shards(): own = lax.all_to_all(frames.transpose(1, 0, 2, 3, 4), 'x', 0, 0, tiled=True)  10.4 us
    ppermute x1, starting transfers between devices, last_frames(): lax.ppermute(last, ('zh', 'x', 'c'), [(Q // X * x, Q + Q // X * x) for x...  7.08 us
    all_to_all x1, waiting for transfers between devices, shards(): own = lax.all_to_all(frames.transpose(1, 0, 2, 3, 4), 'x', 0, 0, tiled=True)  6.57 us
    ppermute x4, starting transfers between devices, last_frames(): rounds.append(lax.ppermute(piece, ('zh', 'x', 'c'), pairs))  4.54 us
    ppermute x1, waiting for transfers between devices, last_frames(): lax.ppermute(last, ('zh', 'x', 'c'), [(Q // X * x, Q + Q // X * x) for x...  3.68 us
  transfers between devices with their start and end apart: 7, of which 3 were waited for; matrix products, arithmetic and copies ran while one was open for 0% of the time, Pallas kernels for 0%

profile of v2, /device:TPU:2, one launch (start us, length us, event | category | flops | bytes accessed | tf_op | source)
XLA Modules:
  0.0 144.3 jit_solution(4924624472128428599)
XLA Ops:
  0.0 1.4 reshape.20
  1.4 0.8 copy.10
  2.2 1.1 dynamic-slice_bitcast_fusion.6
  3.3 1.3 collective-permute-start.1
  4.6 1.3 collective-permute-start.3
  5.9 0.7 collective-permute-start.2
  6.5 1.3 collective-permute-start.4
  7.8 10.4 %all-to-all-start = ((bf16[4,2,6,32,128]{4,3,2,1,0:T(8,128)(2,1)}), bf16[4,2,6,32,128]{4,3,2,1,0:T(8,128)(2,1)S(1)}, u32[]{:S(2)}, u32[]{:S(2)}) async-start(bf16[4,2,6,32,128]{4,3,2,1,0:T(8,128)(2,1)} %bitcast.23.clone.2), calls=%async_computation | async-start | bytes 786432 | tf_op jit(solution)/shard_map/all_to_all | solution.py:243
  18.2 0.0 collective-permute-done.1
  18.2 0.0 collective-permute-done.3
  18.3 0.0 collective-permute-done.2
  18.3 1.1 collective-permute-done.4
  19.4 0.0 copy-start
  19.4 0.0 copy-start.1
  19.4 0.0 copy-start.2
  19.4 0.0 copy-start.3
  19.4 0.1 pad_maximum_fusion
  19.5 6.6 %all-to-all-done.own = bf16[4,2,6,32,128]{4,3,2,1,0:T(8,128)(2,1)S(1)} async-done(((bf16[4,2,6,32,128]{4,3,2,1,0:T(8,128)(2,1)}), bf16[4,2,6,32,128]{4,3,2,1,0:T(8,128)(2,1)S(1)}, u32[]{:S(2)}, u32[]{:S(2)}) %all-to-all-start) | async-done | bytes 393248 | tf_op jit(solution)/shard_map/all_to_all | solution.py:243
  26.1 1.9 %collective-permute-start = (bf16[3,2,6,32,128]{4,3,2,1,0:T(8,128)(2,1)S(1)}, bf16[3,2,6,32,128]{4,3,2,1,0:T(8,128)(2,1)S(1)}, u32[]{:S(2)}, u32[]{:S(2)}) collective-permute-start(bf16[3,2,6,32,128]{4,3,2,1,0:T(8,128)(2,1)S(1)} %constant_dynamic-slice_fusion), channel_id=1, source_target_pairs={{0,1},{1,0},{2,3},{3,2},{4,5},{5,4},{6,7},{7,6},{8,9},{9,8},{10,11... | collective-permute-start | bytes 884744 | tf_op jit(solution)/shard_map/ppermute | solution.py:244
  28.0 7.1 %collective-permute-start.5 = (bf16[2,15,32,128]{3,2,1,0:T(8,128)(2,1)S(1)}, bf16[2,15,32,128]{3,2,1,0:T(8,128)(2,1)S(1)}, u32[]{:S(2)}, u32[]{:S(2)}) collective-permute-start(bf16[2,15,32,128]{3,2,1,0:T(8,128)(2,1)S(1)} %pad_maximum_fusion.1), channel_id=1, source_target_pairs={{0,8},{2,10},{4,12},{6,14},{16,24},{18,26},{20,28},{22,30},{32,40}... | collective-permute-start | bytes 737288 | tf_op jit(solution)/shard_map/ppermute | solution.py:236
  35.1 3.7 %collective-permute-done.5.hist = bf16[2,15,32,128]{3,2,1,0:T(8,128)(2,1)S(1)} collective-permute-done((bf16[2,15,32,128]{3,2,1,0:T(8,128)(2,1)S(1)}, bf16[2,15,32,128]{3,2,1,0:T(8,128)(2,1)S(1)}, u32[]{:S(2)}, u32[]{:S(2)}) %collective-permute-start.5) | collective-permute-done | bytes 245792 | tf_op jit(solution)/shard_map/ppermute | solution.py:236
  38.8 0.0 collective-permute-done.other
  38.8 0.0 copy-done
  38.8 0.0 copy-done.1
  38.8 0.0 copy-done.2
  38.8 0.0 copy-done.3
  38.8 3.5 %channelise.1 = bf16[256,768]{1,0:T(8,128)(2,1)S(1)} custom-call(s32[1]{0:T(128)} %bitcast.core, bf16[4,2,6,32,128]{4,3,2,1,0:T(8,128)(2,1)S(1)} %all-to-all-done.own, bf16[3,2,6,32,128]{4,3,2,1,0:T(8,128)(2,1)S(1)} %collective-permute-done.other, bf16[2,15,32,128]{3,2,1,0:T(8,128)(2,1)S(1)} %collective-permute-done.5.hist, f32[16,32,128]{2,1,0:T(8,128)S(1)} %copy-done.1, ...), custom_call_target="tpu_custom_call" | custom-call | tf_op jit(solution)/shard_map/channelise/pallas_call | solution.py:110
  42.3 11.3 %all_to_all.20.x = bf16[8,32,768]{2,1,0:T(8,128)(2,1)S(1)} all-to-all(bf16[8,32,768]{2,1,0:T(8,128)(2,1)S(1)} %bitcast.25), channel_id=1, replica_groups=mesh['stn'=32,'zh'=2,'x'=4,'c'=2] {'x','c'}, dimensions={0} | all-to-all | bytes 786432 | tf_op jit(solution)/shard_map/all_to_all | solution.py:246
  53.6 0.2 regroup.1
  53.8 50.8 %all_to_all.21 = bf16[64,24,128]{2,1,0:T(8,128)(2,1)S(1)} all-to-all(bf16[64,24,128]{2,1,0:T(8,128)(2,1)S(1)} %bitcast.24), channel_id=1, replica_groups=mesh['stn'=32,'zh'=2,'x'=4,'c'=2] {'stn','zh'}, dimensions={0} | all-to-all | bytes 786432 | tf_op jit(solution)/shard_map/all_to_all | solution.py:248
  104.6 1.6 %correlate.1 = f32[32,72,128]{2,1,0:T(8,128)S(1)} custom-call(bf16[32,2,24,128]{3,2,1,0:T(8,128)(2,1)S(1)} %bitcast.26), custom_call_target="tpu_custom_call" | custom-call | tf_op jit(solution)/shard_map/correlate/pallas_call | solution.py:184
  106.2 0.1 convert_element_type.6
  106.3 36.2 %all_to_all.22 = f16[32,72,128]{2,1,0:T(8,128)(2,1)S(1)} all-to-all(f16[32,72,128]{2,1,0:T(8,128)(2,1)S(1)} %convert_element_type.6), channel_id=1, replica_groups=mesh['stn'=32,'zh'=2,'x'=4,'c'=2] {'stn'}, dimensions={0} | all-to-all | bytes 1179648 | tf_op jit(solution)/shard_map/all_to_all | solution.py:250
  142.4 0.1 convert_element_type.7.x
  142.5 1.8 %deliver.1 = f32[2,4,128,256]{3,2,1,0:T(8,128)} custom-call(f32[32,72,128]{2,1,0:T(8,128)S(1)} %convert_element_type.7.x), custom_call_target="tpu_custom_call" | custom-call | tf_op jit(solution)/shard_map/deliver/pallas_call | solution.py:212
  (4 shorter events, 0.1 us)
Async XLA Ops:
  3.3 15.0 %collective-permute-start.1 = (bf16[2,6,32,128]{3,2,1,0:T(8,128)(2,1)S(1)}, bf16[2,6,32,128]{3,2,1,0:T(8,128)(2,1)S(1)}, u32[]{:S(2)}, u32[]{:S(2)}) collective-permute-start(bf16[2,6,32,128]{3,2,1,0:T(8,128)(2,1)S(1)} %get-tuple-element.8), channel_id=1, source_target_pairs={{5,2},{6,4},{7,6},{21,18},{22,20},{23,22},{37,34},{38,36},{39,38},... | collective-permute-start | bytes 294920 | tf_op jit(solution)/shard_map/ppermute | solution.py:230
  4.6 13.7 %collective-permute-start.3 = (bf16[2,6,32,128]{3,2,1,0:T(8,128)(2,1)S(1)}, bf16[2,6,32,128]{3,2,1,0:T(8,128)(2,1)S(1)}, u32[]{:S(2)}, u32[]{:S(2)}) collective-permute-start(bf16[2,6,32,128]{3,2,1,0:T(8,128)(2,1)S(1)} %get-tuple-element.9), channel_id=1, source_target_pairs={{5,6},{6,0},{7,2},{21,22},{22,16},{23,18},{37,38},{38,32},{39,34},... | collective-permute-start | bytes 294920 | tf_op jit(solution)/shard_map/ppermute | solution.py:230
  5.9 12.4 %collective-permute-start.2 = (bf16[2,6,32,128]{3,2,1,0:T(8,128)(2,1)S(1)}, bf16[2,6,32,128]{3,2,1,0:T(8,128)(2,1)S(1)}, u32[]{:S(2)}, u32[]{:S(2)}) collective-permute-start(bf16[2,6,32,128]{3,2,1,0:T(8,128)(2,1)S(1)} %get-tuple-element.10), channel_id=1, source_target_pairs={{5,4},{6,6},{7,0},{21,20},{22,22},{23,16},{37,36},{38,38},{39,32},... | collective-permute-start | bytes 294920 | tf_op jit(solution)/shard_map/ppermute | solution.py:230
  6.5 12.8 %collective-permute-start.4 = (bf16[2,6,32,128]{3,2,1,0:T(8,128)(2,1)S(1)}, bf16[2,6,32,128]{3,2,1,0:T(8,128)(2,1)S(1)}, u32[]{:S(2)}, u32[]{:S(2)}) collective-permute-start(bf16[2,6,32,128]{3,2,1,0:T(8,128)(2,1)S(1)} %get-tuple-element.11), channel_id=1, source_target_pairs={{5,0},{6,2},{7,4},{21,16},{22,18},{23,20},{37,32},{38,34},{39,36},... | collective-permute-start | bytes 294920 | tf_op jit(solution)/shard_map/ppermute | solution.py:230
  7.8 18.2 %all-to-all-start = ((bf16[4,2,6,32,128]{4,3,2,1,0:T(8,128)(2,1)}), bf16[4,2,6,32,128]{4,3,2,1,0:T(8,128)(2,1)S(1)}, u32[]{:S(2)}, u32[]{:S(2)}) async-start(bf16[4,2,6,32,128]{4,3,2,1,0:T(8,128)(2,1)} %bitcast.23.clone.2), calls=%async_computation | async-start | bytes 786432 | tf_op jit(solution)/shard_map/all_to_all | solution.py:243
  19.4 19.5 %copy-start = (bf16[512,256]{1,0:T(8,128)(2,1)S(1)}, bf16[512,256]{1,0:T(8,128)(2,1)}, u32[]{:S(2)}) copy-start(bf16[512,256]{1,0:T(8,128)(2,1)} %constant.90.clone.second) | copy-start | bytes 786436
  19.4 19.5 %copy-start.1 = (f32[16,32,128]{2,1,0:T(8,128)S(1)}, f32[16,32,128]{2,1,0:T(8,128)}, u32[]{:S(2)}) copy-start(f32[16,32,128]{2,1,0:T(8,128)} %constant.88.clone.taps) | copy-start | bytes 786436
  19.4 19.5 %copy-start.2 = (f32[2,32,128]{2,1,0:T(8,128)S(1)}, f32[2,32,128]{2,1,0:T(8,128)}, u32[]{:S(2)}) copy-start(f32[2,32,128]{2,1,0:T(8,128)} %constant.91.clone.twiddle) | copy-start | bytes 98308
  19.4 19.5 %copy-start.3 = (bf16[128,64]{1,0:T(8,128)(2,1)S(1)}, bf16[128,64]{1,0:T(8,128)(2,1)}, u32[]{:S(2)}) copy-start(bf16[128,64]{1,0:T(8,128)(2,1)} %constant.89.clone.first) | copy-start | bytes 49156
  26.1 12.7 %collective-permute-start = (bf16[3,2,6,32,128]{4,3,2,1,0:T(8,128)(2,1)S(1)}, bf16[3,2,6,32,128]{4,3,2,1,0:T(8,128)(2,1)S(1)}, u32[]{:S(2)}, u32[]{:S(2)}) collective-permute-start(bf16[3,2,6,32,128]{4,3,2,1,0:T(8,128)(2,1)S(1)} %constant_dynamic-slice_fusion), channel_id=1, source_target_pairs={{0,1},{1,0},{2,3},{3,2},{4,5},{5,4},{6,7},{7,6},{8,9},{9,8},{10,11... | collective-permute-start | bytes 884744 | tf_op jit(solution)/shard_map/ppermute | solution.py:244
  28.0 10.8 %collective-permute-start.5 = (bf16[2,15,32,128]{3,2,1,0:T(8,128)(2,1)S(1)}, bf16[2,15,32,128]{3,2,1,0:T(8,128)(2,1)S(1)}, u32[]{:S(2)}, u32[]{:S(2)}) collective-permute-start(bf16[2,15,32,128]{3,2,1,0:T(8,128)(2,1)S(1)} %pad_maximum_fusion.1), channel_id=1, source_target_pairs={{0,8},{2,10},{4,12},{6,14},{16,24},{18,26},{20,28},{22,30},{32,40}... | collective-permute-start | bytes 737288 | tf_op jit(solution)/shard_map/ppermute | solution.py:236

commit v3 on v2

--- a/solution.py
+++ b/solution.py
@@ -54,25 +54,20 @@
     return first, second, twiddle
 
 
-def channelise_body(core, own, other, hist, taps, first, second, twiddle, out, frames, stage, turned_re, turned_im):
-    def place(start, piece):
-        for r in range(2):
-            frames[r, start : start + piece.shape[1]] = piece[r].astype(F32)
-
+def channelise_body(core, main, hist, taps, first, second, twiddle, out, frames, stage, turned_re, turned_im):
     @pl.when(core[0] == 0)
     def _():
-        place(0, hist)
-        for s in range(2):
-            place(HIST + 2 * SENT * s, own.at[s])
-            place(HIST + 2 * SENT * s + SENT, other.at[s])
+        for r in range(2):
+            frames[r, :HIST] = hist[r].astype(F32)
+            for s in range(4):
+                frames[r, HIST + SENT * s : HIST + SENT * (s + 1)] = main[s, r].astype(F32)
 
     @pl.when(core[0] != 0)
     def _():
         for r in range(2):
-            frames[r, :3] = own[0, r, 3:].astype(F32)
-        for s in range(3):
-            place(3 + 2 * SENT * s, other.at[s])
-            place(3 + 2 * SENT * s + SENT, own.at[s + 1])
+            frames[r, :3] = main[1, r, 3:].astype(F32)
+            for s in range(2, 8):
+                frames[r, 3 + SENT * (s - 2) : 3 + SENT * (s - 1)] = main[s, r].astype(F32)
 
     def pair(step, carry):
         for half in range(2):
@@ -103,14 +98,14 @@
         out[:, rows] = (both[: 2 * N2] + (both[2 * N2 :] + rest)).astype(BF16)
 
 
-def channelise(core, own, other, hist, interpret=False):
+def channelise(core, main, hist, interpret=False):
     first, second, twiddle = tables()
-    args = (core, own, other, hist, prototype(), first, second, twiddle)
+    args = (core, main, hist, prototype(), first, second, twiddle)
     vmem = pl.BlockSpec(memory_space=pltpu.VMEM)
     return pl.pallas_call(
         channelise_body,
         out_shape=jax.ShapeDtypeStruct((2 * N2, N1 * BLOCK), BF16),
-        in_specs=[pl.BlockSpec(memory_space=pltpu.SMEM)] + [vmem] * 7,
+        in_specs=[pl.BlockSpec(memory_space=pltpu.SMEM)] + [vmem] * 6,
         out_specs=vmem,
         scratch_shapes=[
             pltpu.VMEM((2, BLOCK + HIST, N1, N2), F32),
@@ -239,10 +234,10 @@
 def shards(voltages):
     frames = voltages.reshape(2, PER, SENT, N1, N2)
     hist = last_frames(frames)
-    core = lax.axis_index("c")
-    own = lax.all_to_all(frames.transpose(1, 0, 2, 3, 4), "x", 0, 0, tiled=True)
-    other = lax.ppermute(lax.dynamic_slice_in_dim(own, 1 - core, 3, 0), "c", [(0, 1), (1, 0)])
-    spectra = channelise(core.astype(jnp.int32).reshape(1), own, other, hist)
+    doubled = jnp.repeat(frames.transpose(1, 0, 2, 3, 4), Q // X, 0)
+    half = lax.all_to_all(doubled, ("x", "c"), 0, 0, tiled=True)
+    core = lax.axis_index("c").astype(jnp.int32).reshape(1)
+    spectra = channelise(core, half, hist)
     spectra = lax.all_to_all(spectra.reshape(Q, 2 * N2 // Q, N1 * BLOCK), ("x", "c"), 0, 0, tiled=True)
     spectra = regroup(spectra).reshape(STN * ZH, BLOCK, 128)
     spectra = lax.all_to_all(spectra, ("stn", "zh"), 0, 0, tiled=True)

time: 145 us -> 136 us (0.938)
  waiting for transfers between devices: 11.4 us -> 3.81 us
    all_to_all x1, waiting for transfers between devices: 6.57 us -> 0.11 us  [shards(): half = lax.all_to_all(doubled, ('x', 'c'), 0, 0, tiled=True)]
    ppermute x1 -> x0, starting transfers between devices: 1.92 us -> none  [shards(): lax.ppermute(lax.dynamic_slice_in_dim(own, 1 - core, 3, 0), 'c', [(0, 1),...]
  transfers between devices with their start and end apart: 7 -> 6, of which waited for: 3 -> 2; matrix products, arithmetic and copies ran while one was open for 0% -> 1% of each run, Pallas kernels for 0% -> 0%
where the time goes in v3:
time: 136 us
  blocking collectives  98.9 us (73%)
  starting transfers between devices  23.2 us (17%)
  Pallas kernels  7.04 us (5%)
  waiting for transfers between devices  3.81 us (3%)
  local copies, waits for them, and re-layouts  2.55 us (2%)
    all_to_all x1, blocking collectives, shards(): spectra = lax.all_to_all(spectra, ('stn', 'zh'), 0, 0, tiled=True)  50.8 us
    all_to_all x1, blocking collectives, shards(): lax.all_to_all(products.astype(jnp.float16), 'stn', 0, 0, tiled=True)  36.2 us
    all_to_all x1, blocking collectives, shards(): lax.all_to_all(spectra.reshape(Q, 2 * N2 // Q, N1 * BLOCK), ('x', 'c'), 0...  12 us
    all_to_all x1, starting transfers between devices, shards(): half = lax.all_to_all(doubled, ('x', 'c'), 0, 0, tiled=True)  11.1 us
    ppermute x1, starting transfers between devices, last_frames(): lax.ppermute(last, ('zh', 'x', 'c'), [(Q // X * x, Q + Q // X * x) for x...  7.63 us
    ppermute x4, starting transfers between devices, last_frames(): rounds.append(lax.ppermute(piece, ('zh', 'x', 'c'), pairs))  4.54 us
    ppermute x1, waiting for transfers between devices, last_frames(): lax.ppermute(last, ('zh', 'x', 'c'), [(Q // X * x, Q + Q // X * x) for x...  3.68 us
    pallas_call x1, Pallas kernels, channelise(): pl.pallas_call(channelise_body, out_shape=jax.ShapeDtypeStruct((2 * N2, N...  3.46 us
  transfers between devices with their start and end apart: 6, of which 2 were waited for; matrix products, arithmetic and copies ran while one was open for 1% of the time, Pallas kernels for 0%

profile of v3, /device:TPU:2, one launch (start us, length us, event | category | flops | bytes accessed | tf_op | source)
XLA Modules:
  0.0 136.1 jit_solution(1710746167200302013)
XLA Ops:
  0.0 1.4 %reshape.19 = bf16[2,4,6,32,128]{4,3,2,1,0:T(8,128)(2,1)S(1)} reshape(bf16[2,4,24576]{2,1,0:T(4,128)(2,1)} %param.5) | data formatting | bytes 786432 | tf_op jit(solution)/shard_map/reshape | solution.py:235
  1.5 1.3 collective-permute-start
  2.8 1.3 collective-permute-start.3
  4.1 1.3 collective-permute-start.2
  5.4 0.7 collective-permute-start.1
  6.1 1.0 broadcast_in_dim.3
  7.1 11.1 %all-to-all-start = ((bf16[8,2,6,32,128]{4,3,2,1,0:T(8,128)(2,1)}), bf16[8,2,6,32,128]{4,3,2,1,0:T(8,128)(2,1)S(1)}, u32[]{:S(2)}, u32[]{:S(2)}) async-start(bf16[8,2,6,32,128]{4,3,2,1,0:T(8,128)(2,1)} %bitcast.2), calls=%async_computation | async-start | bytes 1572864 | tf_op jit(solution)/shard_map/all_to_all | solution.py:238
  18.2 0.0 copy-start
  18.2 0.0 copy-start.1
  18.2 0.0 copy-start.2
  18.2 0.0 copy-start.3
  18.2 0.0 collective-permute-done
  18.3 0.0 collective-permute-done.3
  18.3 0.0 collective-permute-done.2
  18.3 0.0 collective-permute-done.1
  18.3 0.1 pad_maximum_fusion
  18.4 7.6 %collective-permute-start.4 = (bf16[2,15,32,128]{3,2,1,0:T(8,128)(2,1)S(1)}, bf16[2,15,32,128]{3,2,1,0:T(8,128)(2,1)S(1)}, u32[]{:S(2)}, u32[]{:S(2)}) collective-permute-start(bf16[2,15,32,128]{3,2,1,0:T(8,128)(2,1)S(1)} %pad_maximum_fusion.1), channel_id=1, source_target_pairs={{0,8},{2,10},{4,12},{6,14},{16,24},{18,26},{20,28},{22,30},{32,40}... | collective-permute-start | bytes 737288 | tf_op jit(solution)/shard_map/ppermute | solution.py:231
  26.1 3.7 %collective-permute-done.4.hist = bf16[2,15,32,128]{3,2,1,0:T(8,128)(2,1)S(1)} collective-permute-done((bf16[2,15,32,128]{3,2,1,0:T(8,128)(2,1)S(1)}, bf16[2,15,32,128]{3,2,1,0:T(8,128)(2,1)S(1)}, u32[]{:S(2)}, u32[]{:S(2)}) %collective-permute-start.4) | collective-permute-done | bytes 245792 | tf_op jit(solution)/shard_map/ppermute | solution.py:231
  29.8 0.1 all-to-all-done.main
  29.9 0.0 copy-done
  29.9 0.0 copy-done.1
  29.9 0.0 copy-done.2
  29.9 0.0 copy-done.3
  29.9 3.5 %channelise.1 = bf16[256,768]{1,0:T(8,128)(2,1)S(1)} custom-call(s32[1]{0:T(128)} %bitcast.core, bf16[8,2,6,32,128]{4,3,2,1,0:T(8,128)(2,1)S(1)} %all-to-all-done.main, bf16[2,15,32,128]{3,2,1,0:T(8,128)(2,1)S(1)} %collective-permute-done.4.hist, f32[16,32,128]{2,1,0:T(8,128)S(1)} %copy-done.1, bf16[128,64]{1,0:T(8,128)(2,1)S(1)} %copy-done.3, ...), custom_call_target="tpu_custom_call" | custom-call | tf_op jit(solution)/shard_map/channelise/pallas_call | solution.py:105
  33.4 12.0 %all_to_all.20.x = bf16[8,32,768]{2,1,0:T(8,128)(2,1)S(1)} all-to-all(bf16[8,32,768]{2,1,0:T(8,128)(2,1)S(1)} %bitcast.25), channel_id=1, replica_groups=mesh['stn'=32,'zh'=2,'x'=4,'c'=2] {'x','c'}, dimensions={0} | all-to-all | bytes 786432 | tf_op jit(solution)/shard_map/all_to_all | solution.py:241
  45.3 0.2 regroup.1
  45.5 50.8 %all_to_all.21 = bf16[64,24,128]{2,1,0:T(8,128)(2,1)S(1)} all-to-all(bf16[64,24,128]{2,1,0:T(8,128)(2,1)S(1)} %bitcast.24), channel_id=1, replica_groups=mesh['stn'=32,'zh'=2,'x'=4,'c'=2] {'stn','zh'}, dimensions={0} | all-to-all | bytes 786432 | tf_op jit(solution)/shard_map/all_to_all | solution.py:243
  96.3 1.6 %correlate.1 = f32[32,72,128]{2,1,0:T(8,128)S(1)} custom-call(bf16[32,2,24,128]{3,2,1,0:T(8,128)(2,1)S(1)} %bitcast.26), custom_call_target="tpu_custom_call" | custom-call | tf_op jit(solution)/shard_map/correlate/pallas_call | solution.py:179
  97.9 0.1 convert_element_type.6
  98.0 36.2 %all_to_all.22 = f16[32,72,128]{2,1,0:T(8,128)(2,1)S(1)} all-to-all(f16[32,72,128]{2,1,0:T(8,128)(2,1)S(1)} %convert_element_type.6), channel_id=1, replica_groups=mesh['stn'=32,'zh'=2,'x'=4,'c'=2] {'stn'}, dimensions={0} | all-to-all | bytes 1179648 | tf_op jit(solution)/shard_map/all_to_all | solution.py:245
  134.1 0.1 convert_element_type.7.x
  134.2 1.8 %deliver.1 = f32[2,4,128,256]{3,2,1,0:T(8,128)} custom-call(f32[32,72,128]{2,1,0:T(8,128)S(1)} %convert_element_type.7.x), custom_call_target="tpu_custom_call" | custom-call | tf_op jit(solution)/shard_map/deliver/pallas_call | solution.py:207
  (5 shorter events, 0.1 us)
Async XLA Ops:
  1.5 16.8 %collective-permute-start = (bf16[2,6,32,128]{3,2,1,0:T(8,128)(2,1)S(1)}, bf16[2,6,32,128]{3,2,1,0:T(8,128)(2,1)S(1)}, u32[]{:S(2)}, u32[]{:S(2)}) collective-permute-start(bf16[2,6,32,128]{3,2,1,0:T(8,128)(2,1)S(1)} %get-tuple-element.8), channel_id=1, source_target_pairs={{5,2},{6,4},{7,6},{21,18},{22,20},{23,22},{37,34},{38,36},{39,38},... | collective-permute-start | bytes 294920 | tf_op jit(solution)/shard_map/ppermute | solution.py:225
  2.8 15.5 %collective-permute-start.3 = (bf16[2,6,32,128]{3,2,1,0:T(8,128)(2,1)S(1)}, bf16[2,6,32,128]{3,2,1,0:T(8,128)(2,1)S(1)}, u32[]{:S(2)}, u32[]{:S(2)}) collective-permute-start(bf16[2,6,32,128]{3,2,1,0:T(8,128)(2,1)S(1)} %get-tuple-element.9), channel_id=1, source_target_pairs={{5,0},{6,2},{7,4},{21,16},{22,18},{23,20},{37,32},{38,34},{39,36},... | collective-permute-start | bytes 294920 | tf_op jit(solution)/shard_map/ppermute | solution.py:225
  4.1 14.2 %collective-permute-start.2 = (bf16[2,6,32,128]{3,2,1,0:T(8,128)(2,1)S(1)}, bf16[2,6,32,128]{3,2,1,0:T(8,128)(2,1)S(1)}, u32[]{:S(2)}, u32[]{:S(2)}) collective-permute-start(bf16[2,6,32,128]{3,2,1,0:T(8,128)(2,1)S(1)} %get-tuple-element.10), channel_id=1, source_target_pairs={{5,6},{6,0},{7,2},{21,22},{22,16},{23,18},{37,38},{38,32},{39,34},... | collective-permute-start | bytes 294920 | tf_op jit(solution)/shard_map/ppermute | solution.py:225
  5.4 12.9 %collective-permute-start.1 = (bf16[2,6,32,128]{3,2,1,0:T(8,128)(2,1)S(1)}, bf16[2,6,32,128]{3,2,1,0:T(8,128)(2,1)S(1)}, u32[]{:S(2)}, u32[]{:S(2)}) collective-permute-start(bf16[2,6,32,128]{3,2,1,0:T(8,128)(2,1)S(1)} %get-tuple-element.11), channel_id=1, source_target_pairs={{5,4},{6,6},{7,0},{21,20},{22,22},{23,16},{37,36},{38,38},{39,32},... | collective-permute-start | bytes 294920 | tf_op jit(solution)/shard_map/ppermute | solution.py:225
  7.1 22.8 %all-to-all-start = ((bf16[8,2,6,32,128]{4,3,2,1,0:T(8,128)(2,1)}), bf16[8,2,6,32,128]{4,3,2,1,0:T(8,128)(2,1)S(1)}, u32[]{:S(2)}, u32[]{:S(2)}) async-start(bf16[8,2,6,32,128]{4,3,2,1,0:T(8,128)(2,1)} %bitcast.2), calls=%async_computation | async-start | bytes 1572864 | tf_op jit(solution)/shard_map/all_to_all | solution.py:238
  18.2 11.7 %copy-start = (bf16[512,256]{1,0:T(8,128)(2,1)S(1)}, bf16[512,256]{1,0:T(8,128)(2,1)}, u32[]{:S(2)}) copy-start(bf16[512,256]{1,0:T(8,128)(2,1)} %constant.87.clone.second) | copy-start | bytes 786436
  18.2 11.7 %copy-start.1 = (f32[16,32,128]{2,1,0:T(8,128)S(1)}, f32[16,32,128]{2,1,0:T(8,128)}, u32[]{:S(2)}) copy-start(f32[16,32,128]{2,1,0:T(8,128)} %constant.85.clone.taps) | copy-start | bytes 786436
  18.2 11.7 %copy-start.2 = (f32[2,32,128]{2,1,0:T(8,128)S(1)}, f32[2,32,128]{2,1,0:T(8,128)}, u32[]{:S(2)}) copy-start(f32[2,32,128]{2,1,0:T(8,128)} %constant.88.clone.twiddle) | copy-start | bytes 98308
  18.2 11.7 %copy-start.3 = (bf16[128,64]{1,0:T(8,128)(2,1)S(1)}, bf16[128,64]{1,0:T(8,128)(2,1)}, u32[]{:S(2)}) copy-start(bf16[128,64]{1,0:T(8,128)(2,1)} %constant.86.clone.first) | copy-start | bytes 49156
  18.4 11.3 %collective-permute-start.4 = (bf16[2,15,32,128]{3,2,1,0:T(8,128)(2,1)S(1)}, bf16[2,15,32,128]{3,2,1,0:T(8,128)(2,1)S(1)}, u32[]{:S(2)}, u32[]{:S(2)}) collective-permute-start(bf16[2,15,32,128]{3,2,1,0:T(8,128)(2,1)S(1)} %pad_maximum_fusion.1), channel_id=1, source_target_pairs={{0,8},{2,10},{4,12},{6,14},{16,24},{18,26},{20,28},{22,30},{32,40}... | collective-permute-start | bytes 737288 | tf_op jit(solution)/shard_map/ppermute | solution.py:231

commit v4 on v3

--- a/solution.py
+++ b/solution.py
@@ -54,15 +54,15 @@
     return first, second, twiddle
 
 
-def channelise_body(core, main, hist, taps, first, second, twiddle, out, frames, stage, turned_re, turned_im):
-    @pl.when(core[0] == 0)
+def channelise_body(place, main, hist, taps, first, second, twiddle, out, frames, stage, turned_re, turned_im):
+    @pl.when(place[0] == 0)
     def _():
         for r in range(2):
             frames[r, :HIST] = hist[r].astype(F32)
             for s in range(4):
                 frames[r, HIST + SENT * s : HIST + SENT * (s + 1)] = main[s, r].astype(F32)
 
-    @pl.when(core[0] != 0)
+    @pl.when(place[0] != 0)
     def _():
         for r in range(2):
             frames[r, :3] = main[1, r, 3:].astype(F32)
@@ -70,13 +70,19 @@
                 frames[r, 3 + SENT * (s - 2) : 3 + SENT * (s - 1)] = main[s, r].astype(F32)
 
     def pair(step, carry):
-        for half in range(2):
-            f = 2 * step + half
+        for t in range(0, N1, 16):
+            rows = slice(t, t + 16)
             for r in range(2):
-                acc = taps[0] * frames[r, f]
-                for k in range(1, TAPS):
-                    acc = acc + taps[k] * frames[r, f + k]
-                stage[N1 * r : N1 * (r + 1), N2 * half : N2 * (half + 1)] = acc.astype(BF16)
+                early = frames[r, 2 * step, rows]
+                sums = None
+                for k in range(TAPS):
+                    late = frames[r, 2 * step + k + 1, rows]
+                    tap = taps[k, rows]
+                    terms = (tap * early, tap * late)
+                    sums = terms if sums is None else (sums[0] + terms[0], sums[1] + terms[1])
+                    early = late
+                for half in range(2):
+                    stage[N1 * r + t : N1 * r + t + 16, N2 * half : N2 * (half + 1)] = sums[half].astype(BF16)
         both = jnp.dot(first[...], stage[...], preferred_element_type=F32)
         both = both[: 2 * N1] + both[2 * N1 :]
         for half in range(2):
@@ -98,9 +104,9 @@
         out[:, rows] = (both[: 2 * N2] + (both[2 * N2 :] + rest)).astype(BF16)
 
 
-def channelise(core, main, hist, interpret=False):
+def channelise(place, main, hist, interpret=False):
     first, second, twiddle = tables()
-    args = (core, main, hist, prototype(), first, second, twiddle)
+    args = (place, main, hist, prototype(), first, second, twiddle)
     vmem = pl.BlockSpec(memory_space=pltpu.VMEM)
     return pl.pallas_call(
         channelise_body,
@@ -170,15 +176,17 @@
         most = jnp.maximum(most, jnp.max(jnp.abs(tile), 0))
     top = jnp.max(jnp.max(most, 1, keepdims=True), 0, keepdims=True)
     power = jnp.maximum(jnp.floor(jnp.log2(jnp.maximum(top, 1e-37))) - 14.0, -126.0)
-    out[:, :64, :] = plain[...] * jnp.exp2(-power).reshape(1, 1, 1)
-    out[:, 64:, :] = jnp.broadcast_to(power.reshape(1, 1, 1), (STN, 8, 128))
+    factor, power = jnp.exp2(-power).reshape(1, 1, 1), power.reshape(1, 1, 1)
+    station, row, lane = (lax.broadcasted_iota(jnp.int32, (STN, 8, 128), d) for d in range(3))
+    out[:, :8, :] = jnp.where((row == 1) & (lane == station), power, plain[:, :8, :] * factor)
+    out[:, 8:, :] = plain[:, 8:, :] * factor
 
 
 def correlate(x, interpret=False):
     vmem = pl.BlockSpec(memory_space=pltpu.VMEM)
     return pl.pallas_call(
         correlate_body,
-        out_shape=jax.ShapeDtypeStruct((STN, 72, 128), F32),
+        out_shape=jax.ShapeDtypeStruct((STN, 64, 128), F32),
         in_specs=[vmem],
         out_specs=vmem,
         scratch_shapes=[pltpu.VMEM((64 * STN, 128), F32), pltpu.VMEM((STN, 64, 128), F32)],
@@ -188,32 +196,44 @@
     )(x)
 
 
-def deliver_body(x, out, wide, order):
-    for k in range(N1):
-        wide[64 * k : 64 * (k + 1), :] = x[k, :64, :] * jnp.exp2(x[k, 64:65, :])
-    for row in range(8):
-        for half in range(2):
-            cols = jnp.concatenate(
-                [wide[pl.ds(8 * j + row, N1, stride=64), :] for j in range(4 * half, 4 * half + 4)], 0
-            ).T
-            base = 128 * (2 * row + half)
-            for i in range(PER):
-                order[pl.ds(base + i, STN, stride=PER), :] = cols[STN * i : STN * (i + 1)]
-            out[row // PER, row % PER, :, 128 * half : 128 * (half + 1)] = order[base : base + 128, :]
-
-
-def deliver(x, interpret=False):
-    vmem = pl.BlockSpec(memory_space=pltpu.VMEM)
+def deliver_body(place, x, out, wide, order):
+    row = pl.program_id(0)
+
+    @pl.when(row == 0)
+    def _():
+        here = x[:, :8, :]
+        line, lane = (lax.broadcasted_iota(jnp.int32, (N1, 8, 128), d) for d in (1, 2))
+        holder = (line == 1) & (lane == place[1])
+        mirror = (line == 0) & (lane == place[1] + STN)
+
+        def pick(mask):
+            return jnp.sum(jnp.sum(jnp.where(mask, here, 0.0), 2, keepdims=True), 1, keepdims=True)
+
+        factor = jnp.exp2(pick(holder))
+        wide[:, :8, :] = jnp.where(holder, pick(mirror), here) * factor
+        wide[:, 8:, :] = x[:, 8:, :] * factor
+
+    flat = wide.reshape(64 * N1, 128)
+    for half in range(2):
+        rows = [flat[pl.ds(8 * j + row, N1, stride=64), :] for j in range(4 * half, 4 * half + 4)]
+        cols = jnp.concatenate(rows, 0).T
+        for i in range(PER):
+            order[pl.ds(128 * half + i, STN, stride=PER), :] = cols[STN * i : STN * (i + 1)]
+        out[0, 0, :, 128 * half : 128 * (half + 1)] = order[128 * half : 128 * (half + 1), :]
+
+
+def deliver(place, x, interpret=False):
     return pl.pallas_call(
         deliver_body,
+        grid=(8,),
         out_shape=jax.ShapeDtypeStruct((2, PER, 128, 256), F32),
-        in_specs=[vmem],
-        out_specs=vmem,
-        scratch_shapes=[pltpu.VMEM((64 * N1, 128), F32), pltpu.VMEM((16 * 128, 128), F32)],
+        in_specs=[pl.BlockSpec(memory_space=pltpu.SMEM), pl.BlockSpec(memory_space=pltpu.VMEM)],
+        out_specs=pl.BlockSpec((1, 1, 128, 256), lambda row: (row // PER, row % PER, 0, 0)),
+        scratch_shapes=[pltpu.VMEM((N1, 64, 128), F32), pltpu.VMEM((2 * 128, 128), F32)],
         compiler_params=PARAMS,
         interpret=interpret,
         name="deliver",
-    )(x)
+    )(place, x)
 
 
 def last_frames(frames):
@@ -236,14 +256,14 @@
     hist = last_frames(frames)
     doubled = jnp.repeat(frames.transpose(1, 0, 2, 3, 4), Q // X, 0)
     half = lax.all_to_all(doubled, ("x", "c"), 0, 0, tiled=True)
-    core = lax.axis_index("c").astype(jnp.int32).reshape(1)
-    spectra = channelise(core, half, hist)
+    place = jnp.stack([lax.axis_index("c"), lax.axis_index("stn")]).astype(jnp.int32)
+    spectra = channelise(place, half, hist)
     spectra = lax.all_to_all(spectra.reshape(Q, 2 * N2 // Q, N1 * BLOCK), ("x", "c"), 0, 0, tiled=True)
     spectra = regroup(spectra).reshape(STN * ZH, BLOCK, 128)
     spectra = lax.all_to_all(spectra, ("stn", "zh"), 0, 0, tiled=True)
     products = correlate(spectra.reshape(STN, ZH, BLOCK, 128))
     products = lax.all_to_all(products.astype(jnp.float16), "stn", 0, 0, tiled=True)
-    return deliver(products.astype(F32))
+    return deliver(place, products.astype(F32))
 
 
 def solution(mesh):

time: 136 us -> 136 us (level)
  blocking collectives: 98.9 us -> 95.9 us
  Pallas kernels: 7.04 us -> 9.94 us
    all_to_all x1, blocking collectives: 36.2 us -> 33.1 us  [shards(): lax.all_to_all(products.astype(jnp.float16), 'stn', 0, 0, tiled=True)]
    pallas_call x2, Pallas kernels: 3.4 us -> 5.87 us  [the longest x1 4.29 us: deliver(): pl.pallas_call(deliver_body, grid=(8,), out_shape=jax.ShapeDtypeStruct((2...]
  transfers between devices with their start and end apart: 6 -> 6, of which waited for: 2 -> 1; matrix products, arithmetic and copies ran while one was open for 1% -> 1% of each run, Pallas kernels for 0% -> 0%
where the time goes in v4:
time: 136 us
  blocking collectives  95.9 us (71%)
  starting transfers between devices  23.4 us (17%)
  Pallas kernels  9.94 us (7%)
  waiting for transfers between devices  3.63 us (3%)
  local copies, waits for them, and re-layouts  2.56 us (2%)
    all_to_all x1, blocking collectives, shards(): spectra = lax.all_to_all(spectra, ('stn', 'zh'), 0, 0, tiled=True)  50.8 us
    all_to_all x1, blocking collectives, shards(): lax.all_to_all(products.astype(jnp.float16), 'stn', 0, 0, tiled=True)  33.1 us
    all_to_all x1, blocking collectives, shards(): lax.all_to_all(spectra.reshape(Q, 2 * N2 // Q, N1 * BLOCK), ('x', 'c'), 0...  12.1 us
    all_to_all x1, starting transfers between devices, shards(): half = lax.all_to_all(doubled, ('x', 'c'), 0, 0, tiled=True)  11.1 us
    ppermute x1, starting transfers between devices, last_frames(): lax.ppermute(last, ('zh', 'x', 'c'), [(Q // X * x, Q + Q // X * x) for x...  7.77 us
    ppermute x4, starting transfers between devices, last_frames(): rounds.append(lax.ppermute(piece, ('zh', 'x', 'c'), pairs))  4.54 us
    pallas_call x1, Pallas kernels, deliver(): pl.pallas_call(deliver_body, grid=(8,), out_shape=jax.ShapeDtypeStruct((2...  4.29 us
    pallas_call x1, Pallas kernels, channelise(): pl.pallas_call(channelise_body, out_shape=jax.ShapeDtypeStruct((2 * N2, N...  3.9 us
  transfers between devices with their start and end apart: 6, of which 1 were waited for; matrix products, arithmetic and copies ran while one was open for 1% of the time, Pallas kernels for 0%

profile of v4, /device:TPU:2, one launch (start us, length us, event | category | flops | bytes accessed | tf_op | source)
XLA Modules:
  0.0 136.0 jit_solution(6466089356586657956)
XLA Ops:
  0.0 1.4 %reshape.15 = bf16[2,4,6,32,128]{4,3,2,1,0:T(8,128)(2,1)S(1)} reshape(bf16[2,4,24576]{2,1,0:T(4,128)(2,1)} %param.5) | data formatting | bytes 786432 | tf_op jit(solution)/shard_map/reshape | solution.py:255
  1.5 1.3 collective-permute-start
  2.8 1.3 collective-permute-start.3
  4.1 1.3 collective-permute-start.2
  5.4 0.7 collective-permute-start.1
  6.1 1.0 broadcast_in_dim.3
  7.1 11.1 %all-to-all-start = ((bf16[8,2,6,32,128]{4,3,2,1,0:T(8,128)(2,1)}), bf16[8,2,6,32,128]{4,3,2,1,0:T(8,128)(2,1)S(1)}, u32[]{:S(2)}, u32[]{:S(2)}) async-start(bf16[8,2,6,32,128]{4,3,2,1,0:T(8,128)(2,1)} %bitcast.3), calls=%async_computation | async-start | bytes 1572864 | tf_op jit(solution)/shard_map/all_to_all | solution.py:258
  18.2 0.0 collective-permute-done
  18.2 0.0 collective-permute-done.3
  18.2 0.0 collective-permute-done.2
  18.2 0.0 collective-permute-done.1
  18.2 0.1 pad_maximum_fusion
  18.3 0.0 copy-start.1
  18.3 0.0 copy-start
  18.3 0.0 copy-start.2
  18.4 0.0 copy-start.3
  18.4 7.8 %collective-permute-start.4 = (bf16[2,15,32,128]{3,2,1,0:T(8,128)(2,1)S(1)}, bf16[2,15,32,128]{3,2,1,0:T(8,128)(2,1)S(1)}, u32[]{:S(2)}, u32[]{:S(2)}) collective-permute-start(bf16[2,15,32,128]{3,2,1,0:T(8,128)(2,1)S(1)} %pad_maximum_fusion.1), channel_id=1, source_target_pairs={{0,8},{2,10},{4,12},{6,14},{16,24},{18,26},{20,28},{22,30},{32,40}... | collective-permute-start | bytes 737288 | tf_op jit(solution)/shard_map/ppermute | solution.py:251
  26.2 0.1 pad_add_fusion.place
  26.3 3.6 %collective-permute-done.4.hist = bf16[2,15,32,128]{3,2,1,0:T(8,128)(2,1)S(1)} collective-permute-done((bf16[2,15,32,128]{3,2,1,0:T(8,128)(2,1)S(1)}, bf16[2,15,32,128]{3,2,1,0:T(8,128)(2,1)S(1)}, u32[]{:S(2)}, u32[]{:S(2)}) %collective-permute-start.4) | collective-permute-done | bytes 245792 | tf_op jit(solution)/shard_map/ppermute | solution.py:251
  29.9 0.0 all-to-all-done.main
  29.9 0.0 copy-done.1
  29.9 0.0 copy-done
  29.9 0.0 copy-done.2
  29.9 0.0 copy-done.3
  29.9 3.9 %channelise.1 = bf16[256,768]{1,0:T(8,128)(2,1)S(1)} custom-call(s32[2]{0:T(128)S(1)} %pad_add_fusion.place, bf16[8,2,6,32,128]{4,3,2,1,0:T(8,128)(2,1)S(1)} %all-to-all-done.main, bf16[2,15,32,128]{3,2,1,0:T(8,128)(2,1)S(1)} %collective-permute-done.4.hist, f32[16,32,128]{2,1,0:T(8,128)S(1)} %copy-done.1, bf16[128,64]{1,0:T(8,128)(2,1)S(1)} %copy-done.3, ...), custom_call_target="tpu_custom_call" | custom-call | tf_op jit(solution)/shard_map/channelise/pallas_call | solution.py:111
  33.8 12.1 %all_to_all.20.x = bf16[8,32,768]{2,1,0:T(8,128)(2,1)S(1)} all-to-all(bf16[8,32,768]{2,1,0:T(8,128)(2,1)S(1)} %bitcast.26), channel_id=1, replica_groups=mesh['stn'=32,'zh'=2,'x'=4,'c'=2] {'x','c'}, dimensions={0} | all-to-all | bytes 786432 | tf_op jit(solution)/shard_map/all_to_all | solution.py:261
  45.9 0.2 regroup.1
  46.1 50.8 %all_to_all.21 = bf16[64,24,128]{2,1,0:T(8,128)(2,1)S(1)} all-to-all(bf16[64,24,128]{2,1,0:T(8,128)(2,1)S(1)} %bitcast.25), channel_id=1, replica_groups=mesh['stn'=32,'zh'=2,'x'=4,'c'=2] {'stn','zh'}, dimensions={0} | all-to-all | bytes 786432 | tf_op jit(solution)/shard_map/all_to_all | solution.py:263
  96.8 1.6 %correlate.1 = f32[32,64,128]{2,1,0:T(8,128)S(1)} custom-call(bf16[32,2,24,128]{3,2,1,0:T(8,128)(2,1)S(1)} %bitcast.27), custom_call_target="tpu_custom_call" | custom-call | tf_op jit(solution)/shard_map/correlate/pallas_call | solution.py:187
  98.4 0.1 convert_element_type.6
  98.6 33.1 %all_to_all.22 = f16[32,64,128]{2,1,0:T(8,128)(2,1)S(1)} all-to-all(f16[32,64,128]{2,1,0:T(8,128)(2,1)S(1)} %convert_element_type.6), channel_id=1, replica_groups=mesh['stn'=32,'zh'=2,'x'=4,'c'=2] {'stn'}, dimensions={0} | all-to-all | bytes 1048576 | tf_op jit(solution)/shard_map/all_to_all | solution.py:265
  131.6 0.1 convert_element_type.7.x
  131.7 4.3 %deliver.1 = f32[2,4,128,256]{3,2,1,0:T(8,128)} custom-call(s32[2]{0:T(128)S(1)} %pad_add_fusion.place, f32[32,64,128]{2,1,0:T(8,128)S(1)} %convert_element_type.7.x), custom_call_target="tpu_custom_call" | custom-call | tf_op jit(solution)/shard_map/deliver/pallas_call | solution.py:226
  (5 shorter events, 0.1 us)
Async XLA Ops:
  1.5 16.7 %collective-permute-start = (bf16[2,6,32,128]{3,2,1,0:T(8,128)(2,1)S(1)}, bf16[2,6,32,128]{3,2,1,0:T(8,128)(2,1)S(1)}, u32[]{:S(2)}, u32[]{:S(2)}) collective-permute-start(bf16[2,6,32,128]{3,2,1,0:T(8,128)(2,1)S(1)} %get-tuple-element.8), channel_id=1, source_target_pairs={{5,2},{6,4},{7,6},{21,18},{22,20},{23,22},{37,34},{38,36},{39,38},... | collective-permute-start | bytes 294920 | tf_op jit(solution)/shard_map/ppermute | solution.py:245
  2.8 15.4 %collective-permute-start.3 = (bf16[2,6,32,128]{3,2,1,0:T(8,128)(2,1)S(1)}, bf16[2,6,32,128]{3,2,1,0:T(8,128)(2,1)S(1)}, u32[]{:S(2)}, u32[]{:S(2)}) collective-permute-start(bf16[2,6,32,128]{3,2,1,0:T(8,128)(2,1)S(1)} %get-tuple-element.9), channel_id=1, source_target_pairs={{5,0},{6,2},{7,4},{21,16},{22,18},{23,20},{37,32},{38,34},{39,36},... | collective-permute-start | bytes 294920 | tf_op jit(solution)/shard_map/ppermute | solution.py:245
  4.1 14.1 %collective-permute-start.2 = (bf16[2,6,32,128]{3,2,1,0:T(8,128)(2,1)S(1)}, bf16[2,6,32,128]{3,2,1,0:T(8,128)(2,1)S(1)}, u32[]{:S(2)}, u32[]{:S(2)}) collective-permute-start(bf16[2,6,32,128]{3,2,1,0:T(8,128)(2,1)S(1)} %get-tuple-element.10), channel_id=1, source_target_pairs={{5,6},{6,0},{7,2},{21,22},{22,16},{23,18},{37,38},{38,32},{39,34},... | collective-permute-start | bytes 294920 | tf_op jit(solution)/shard_map/ppermute | solution.py:245
  5.4 12.8 %collective-permute-start.1 = (bf16[2,6,32,128]{3,2,1,0:T(8,128)(2,1)S(1)}, bf16[2,6,32,128]{3,2,1,0:T(8,128)(2,1)S(1)}, u32[]{:S(2)}, u32[]{:S(2)}) collective-permute-start(bf16[2,6,32,128]{3,2,1,0:T(8,128)(2,1)S(1)} %get-tuple-element.11), channel_id=1, source_target_pairs={{5,4},{6,6},{7,0},{21,20},{22,22},{23,16},{37,36},{38,38},{39,32},... | collective-permute-start | bytes 294920 | tf_op jit(solution)/shard_map/ppermute | solution.py:245
  7.1 22.8 %all-to-all-start = ((bf16[8,2,6,32,128]{4,3,2,1,0:T(8,128)(2,1)}), bf16[8,2,6,32,128]{4,3,2,1,0:T(8,128)(2,1)S(1)}, u32[]{:S(2)}, u32[]{:S(2)}) async-start(bf16[8,2,6,32,128]{4,3,2,1,0:T(8,128)(2,1)} %bitcast.3), calls=%async_computation | async-start | bytes 1572864 | tf_op jit(solution)/shard_map/all_to_all | solution.py:258
  18.3 11.6 %copy-start.1 = (f32[16,32,128]{2,1,0:T(8,128)S(1)}, f32[16,32,128]{2,1,0:T(8,128)}, u32[]{:S(2)}) copy-start(f32[16,32,128]{2,1,0:T(8,128)} %constant.91.clone.taps) | copy-start | bytes 786436
  18.3 11.6 %copy-start = (bf16[512,256]{1,0:T(8,128)(2,1)S(1)}, bf16[512,256]{1,0:T(8,128)(2,1)}, u32[]{:S(2)}) copy-start(bf16[512,256]{1,0:T(8,128)(2,1)} %constant.93.clone.second) | copy-start | bytes 786436
  18.3 11.5 %copy-start.2 = (f32[2,32,128]{2,1,0:T(8,128)S(1)}, f32[2,32,128]{2,1,0:T(8,128)}, u32[]{:S(2)}) copy-start(f32[2,32,128]{2,1,0:T(8,128)} %constant.94.clone.twiddle) | copy-start | bytes 98308
  18.4 11.5 %copy-start.3 = (bf16[128,64]{1,0:T(8,128)(2,1)S(1)}, bf16[128,64]{1,0:T(8,128)(2,1)}, u32[]{:S(2)}) copy-start(bf16[128,64]{1,0:T(8,128)(2,1)} %constant.92.clone.first) | copy-start | bytes 49156
  18.4 11.5 %collective-permute-start.4 = (bf16[2,15,32,128]{3,2,1,0:T(8,128)(2,1)S(1)}, bf16[2,15,32,128]{3,2,1,0:T(8,128)(2,1)S(1)}, u32[]{:S(2)}, u32[]{:S(2)}) collective-permute-start(bf16[2,15,32,128]{3,2,1,0:T(8,128)(2,1)S(1)} %pad_maximum_fusion.1), channel_id=1, source_target_pairs={{0,8},{2,10},{4,12},{6,14},{16,24},{18,26},{20,28},{22,30},{32,40}... | collective-permute-start | bytes 737288 | tf_op jit(solution)/shard_map/ppermute | solution.py:251

commit v5 on v3

--- a/solution.py
+++ b/solution.py
@@ -54,15 +54,15 @@
     return first, second, twiddle
 
 
-def channelise_body(core, main, hist, taps, first, second, twiddle, out, frames, stage, turned_re, turned_im):
-    @pl.when(core[0] == 0)
+def channelise_body(place, main, hist, taps, first, second, twiddle, out, frames, stage, turned_re, turned_im):
+    @pl.when(place[0] == 0)
     def _():
         for r in range(2):
             frames[r, :HIST] = hist[r].astype(F32)
             for s in range(4):
                 frames[r, HIST + SENT * s : HIST + SENT * (s + 1)] = main[s, r].astype(F32)
 
-    @pl.when(core[0] != 0)
+    @pl.when(place[0] != 0)
     def _():
         for r in range(2):
             frames[r, :3] = main[1, r, 3:].astype(F32)
@@ -98,9 +98,9 @@
         out[:, rows] = (both[: 2 * N2] + (both[2 * N2 :] + rest)).astype(BF16)
 
 
-def channelise(core, main, hist, interpret=False):
+def channelise(place, main, hist, interpret=False):
     first, second, twiddle = tables()
-    args = (core, main, hist, prototype(), first, second, twiddle)
+    args = (place, main, hist, prototype(), first, second, twiddle)
     vmem = pl.BlockSpec(memory_space=pltpu.VMEM)
     return pl.pallas_call(
         channelise_body,
@@ -170,15 +170,17 @@
         most = jnp.maximum(most, jnp.max(jnp.abs(tile), 0))
     top = jnp.max(jnp.max(most, 1, keepdims=True), 0, keepdims=True)
     power = jnp.maximum(jnp.floor(jnp.log2(jnp.maximum(top, 1e-37))) - 14.0, -126.0)
-    out[:, :64, :] = plain[...] * jnp.exp2(-power).reshape(1, 1, 1)
-    out[:, 64:, :] = jnp.broadcast_to(power.reshape(1, 1, 1), (STN, 8, 128))
+    factor, power = jnp.exp2(-power).reshape(1, 1, 1), power.reshape(1, 1, 1)
+    station, row, lane = (lax.broadcasted_iota(jnp.int32, (STN, 8, 128), d) for d in range(3))
+    out[:, :8, :] = jnp.where((row == 1) & (lane == station), power, plain[:, :8, :] * factor)
+    out[:, 8:, :] = plain[:, 8:, :] * factor
 
 
 def correlate(x, interpret=False):
     vmem = pl.BlockSpec(memory_space=pltpu.VMEM)
     return pl.pallas_call(
         correlate_body,
-        out_shape=jax.ShapeDtypeStruct((STN, 72, 128), F32),
+        out_shape=jax.ShapeDtypeStruct((STN, 64, 128), F32),
         in_specs=[vmem],
         out_specs=vmem,
         scratch_shapes=[pltpu.VMEM((64 * STN, 128), F32), pltpu.VMEM((STN, 64, 128), F32)],
@@ -188,32 +190,41 @@
     )(x)
 
 
-def deliver_body(x, out, wide, order):
-    for k in range(N1):
-        wide[64 * k : 64 * (k + 1), :] = x[k, :64, :] * jnp.exp2(x[k, 64:65, :])
+def deliver_body(place, x, out, wide, order):
+    here = x[:, :8, :]
+    line, lane = (lax.broadcasted_iota(jnp.int32, (N1, 8, 128), d) for d in (1, 2))
+    holder = (line == 1) & (lane == place[1])
+    mirror = (line == 0) & (lane == place[1] + STN)
+
+    def pick(mask):
+        return jnp.sum(jnp.sum(jnp.where(mask, here, 0.0), 1, keepdims=True), 2, keepdims=True)
+
+    factor = jnp.exp2(pick(holder))
+    wide[...] = x[...] * factor
+    wide[:, :8, :] = jnp.where(holder, pick(mirror), here) * factor
+    flat = wide.reshape(64 * N1, 128)
     for row in range(8):
         for half in range(2):
-            cols = jnp.concatenate(
-                [wide[pl.ds(8 * j + row, N1, stride=64), :] for j in range(4 * half, 4 * half + 4)], 0
-            ).T
+            rows = [flat[pl.ds(8 * j + row, N1, stride=64), :] for j in range(4 * half, 4 * half + 4)]
+            cols = jnp.concatenate(rows, 0).T
             base = 128 * (2 * row + half)
             for i in range(PER):
                 order[pl.ds(base + i, STN, stride=PER), :] = cols[STN * i : STN * (i + 1)]
             out[row // PER, row % PER, :, 128 * half : 128 * (half + 1)] = order[base : base + 128, :]
 
 
-def deliver(x, interpret=False):
+def deliver(place, x, interpret=False):
     vmem = pl.BlockSpec(memory_space=pltpu.VMEM)
     return pl.pallas_call(
         deliver_body,
         out_shape=jax.ShapeDtypeStruct((2, PER, 128, 256), F32),
-        in_specs=[vmem],
-        out_specs=vmem,
-        scratch_shapes=[pltpu.VMEM((64 * N1, 128), F32), pltpu.VMEM((16 * 128, 128), F32)],
+        in_specs=[pl.BlockSpec(memory_space=pltpu.SMEM), vmem],
+        out_specs=vmem,
+        scratch_shapes=[pltpu.VMEM((N1, 64, 128), F32), pltpu.VMEM((16 * 128, 128), F32)],
         compiler_params=PARAMS,
         interpret=interpret,
         name="deliver",
-    )(x)
+    )(place, x)
 
 
 def last_frames(frames):
@@ -236,14 +247,14 @@
     hist = last_frames(frames)
     doubled = jnp.repeat(frames.transpose(1, 0, 2, 3, 4), Q // X, 0)
     half = lax.all_to_all(doubled, ("x", "c"), 0, 0, tiled=True)
-    core = lax.axis_index("c").astype(jnp.int32).reshape(1)
-    spectra = channelise(core, half, hist)
+    place = jnp.stack([lax.axis_index("c"), lax.axis_index("stn")]).astype(jnp.int32)
+    spectra = channelise(place, half, hist)
     spectra = lax.all_to_all(spectra.reshape(Q, 2 * N2 // Q, N1 * BLOCK), ("x", "c"), 0, 0, tiled=True)
     spectra = regroup(spectra).reshape(STN * ZH, BLOCK, 128)
     spectra = lax.all_to_all(spectra, ("stn", "zh"), 0, 0, tiled=True)
     products = correlate(spectra.reshape(STN, ZH, BLOCK, 128))
     products = lax.all_to_all(products.astype(jnp.float16), "stn", 0, 0, tiled=True)
-    return deliver(products.astype(F32))
+    return deliver(place, products.astype(F32))
 
 
 def solution(mesh):

time: 136 us -> 135 us (level)
  blocking collectives: 98.9 us -> 95.9 us
    all_to_all x1, blocking collectives: 36.2 us -> 33.1 us  [shards(): lax.all_to_all(products.astype(jnp.float16), 'stn', 0, 0, tiled=True)]
  transfers between devices with their start and end apart: 6 -> 6, of which waited for: 2 -> 1; matrix products, arithmetic and copies ran while one was open for 1% -> 1% of each run, Pallas kernels for 0% -> 0%
where the time goes in v5:
time: 135 us; the launch traced here: 134 us
  blocking collectives  95.9 us (71%)
  starting transfers between devices  23.4 us (17%)
  Pallas kernels  8.18 us (6%)
  waiting for transfers between devices  3.63 us (3%)
  local copies, waits for them, and re-layouts  2.56 us (2%)
    all_to_all x1, blocking collectives, shards(): spectra = lax.all_to_all(spectra, ('stn', 'zh'), 0, 0, tiled=True)  50.8 us
    all_to_all x1, blocking collectives, shards(): lax.all_to_all(products.astype(jnp.float16), 'stn', 0, 0, tiled=True)  33.1 us
    all_to_all x1, blocking collectives, shards(): lax.all_to_all(spectra.reshape(Q, 2 * N2 // Q, N1 * BLOCK), ('x', 'c'), 0...  12.1 us
    all_to_all x1, starting transfers between devices, shards(): half = lax.all_to_all(doubled, ('x', 'c'), 0, 0, tiled=True)  11.1 us
    ppermute x1, starting transfers between devices, last_frames(): lax.ppermute(last, ('zh', 'x', 'c'), [(Q // X * x, Q + Q // X * x) for x...  7.77 us
    ppermute x4, starting transfers between devices, last_frames(): rounds.append(lax.ppermute(piece, ('zh', 'x', 'c'), pairs))  4.54 us
    pallas_call x1, Pallas kernels, channelise(): pl.pallas_call(channelise_body, out_shape=jax.ShapeDtypeStruct((2 * N2, N...  4 us
    ppermute x1, waiting for transfers between devices, last_frames(): lax.ppermute(last, ('zh', 'x', 'c'), [(Q // X * x, Q + Q // X * x) for x...  3.6 us
  transfers between devices with their start and end apart: 6, of which 1 were waited for; matrix products, arithmetic and copies ran while one was open for 1% of the time, Pallas kernels for 0%

profile of v5, /device:TPU:2, one launch (start us, length us, event | category | flops | bytes accessed | tf_op | source)
XLA Modules:
  0.0 134.2 jit_solution(5453403339598816086)
XLA Ops:
  0.0 1.4 %reshape.15 = bf16[2,4,6,32,128]{4,3,2,1,0:T(8,128)(2,1)S(1)} reshape(bf16[2,4,24576]{2,1,0:T(4,128)(2,1)} %param.5) | data formatting | bytes 786432 | tf_op jit(solution)/shard_map/reshape | solution.py:246
  1.5 1.3 collective-permute-start
  2.8 1.3 collective-permute-start.3
  4.1 1.3 collective-permute-start.2
  5.4 0.7 collective-permute-start.1
  6.1 1.0 broadcast_in_dim.3
  7.1 11.1 %all-to-all-start = ((bf16[8,2,6,32,128]{4,3,2,1,0:T(8,128)(2,1)}), bf16[8,2,6,32,128]{4,3,2,1,0:T(8,128)(2,1)S(1)}, u32[]{:S(2)}, u32[]{:S(2)}) async-start(bf16[8,2,6,32,128]{4,3,2,1,0:T(8,128)(2,1)} %bitcast.3), calls=%async_computation | async-start | bytes 1572864 | tf_op jit(solution)/shard_map/all_to_all | solution.py:249
  18.2 0.0 collective-permute-done
  18.2 0.0 collective-permute-done.3
  18.2 0.0 collective-permute-done.2
  18.2 0.0 collective-permute-done.1
  18.2 0.1 pad_maximum_fusion
  18.3 0.0 copy-start.1
  18.3 0.0 copy-start
  18.3 0.0 copy-start.2
  18.4 0.0 copy-start.3
  18.4 7.8 %collective-permute-start.4 = (bf16[2,15,32,128]{3,2,1,0:T(8,128)(2,1)S(1)}, bf16[2,15,32,128]{3,2,1,0:T(8,128)(2,1)S(1)}, u32[]{:S(2)}, u32[]{:S(2)}) collective-permute-start(bf16[2,15,32,128]{3,2,1,0:T(8,128)(2,1)S(1)} %pad_maximum_fusion.1), channel_id=1, source_target_pairs={{0,8},{2,10},{4,12},{6,14},{16,24},{18,26},{20,28},{22,30},{32,40}... | collective-permute-start | bytes 737288 | tf_op jit(solution)/shard_map/ppermute | solution.py:242
  26.2 0.1 pad_add_fusion.place
  26.3 3.6 %collective-permute-done.4.hist = bf16[2,15,32,128]{3,2,1,0:T(8,128)(2,1)S(1)} collective-permute-done((bf16[2,15,32,128]{3,2,1,0:T(8,128)(2,1)S(1)}, bf16[2,15,32,128]{3,2,1,0:T(8,128)(2,1)S(1)}, u32[]{:S(2)}, u32[]{:S(2)}) %collective-permute-start.4) | collective-permute-done | bytes 245792 | tf_op jit(solution)/shard_map/ppermute | solution.py:242
  29.9 0.0 all-to-all-done.main
  29.9 0.0 copy-done.1
  29.9 0.0 copy-done
  29.9 0.0 copy-done.2
  29.9 0.0 copy-done.3
  29.9 4.0 %channelise.1 = bf16[256,768]{1,0:T(8,128)(2,1)S(1)} custom-call(s32[2]{0:T(128)S(1)} %pad_add_fusion.place, bf16[8,2,6,32,128]{4,3,2,1,0:T(8,128)(2,1)S(1)} %all-to-all-done.main, bf16[2,15,32,128]{3,2,1,0:T(8,128)(2,1)S(1)} %collective-permute-done.4.hist, f32[16,32,128]{2,1,0:T(8,128)S(1)} %copy-done.1, bf16[128,64]{1,0:T(8,128)(2,1)S(1)} %copy-done.3, ...), custom_call_target="tpu_custom_call" | custom-call | tf_op jit(solution)/shard_map/channelise/pallas_call | solution.py:105
  33.9 12.1 %all_to_all.20.x = bf16[8,32,768]{2,1,0:T(8,128)(2,1)S(1)} all-to-all(bf16[8,32,768]{2,1,0:T(8,128)(2,1)S(1)} %bitcast.26), channel_id=1, replica_groups=mesh['stn'=32,'zh'=2,'x'=4,'c'=2] {'x','c'}, dimensions={0} | all-to-all | bytes 786432 | tf_op jit(solution)/shard_map/all_to_all | solution.py:252
  46.0 0.2 regroup.1
  46.2 50.8 %all_to_all.21 = bf16[64,24,128]{2,1,0:T(8,128)(2,1)S(1)} all-to-all(bf16[64,24,128]{2,1,0:T(8,128)(2,1)S(1)} %bitcast.25), channel_id=1, replica_groups=mesh['stn'=32,'zh'=2,'x'=4,'c'=2] {'stn','zh'}, dimensions={0} | all-to-all | bytes 786432 | tf_op jit(solution)/shard_map/all_to_all | solution.py:254
  96.9 1.6 %correlate.1 = f32[32,64,128]{2,1,0:T(8,128)S(1)} custom-call(bf16[32,2,24,128]{3,2,1,0:T(8,128)(2,1)S(1)} %bitcast.27), custom_call_target="tpu_custom_call" | custom-call | tf_op jit(solution)/shard_map/correlate/pallas_call | solution.py:181
  98.5 0.1 convert_element_type.6
  98.7 33.1 %all_to_all.22 = f16[32,64,128]{2,1,0:T(8,128)(2,1)S(1)} all-to-all(f16[32,64,128]{2,1,0:T(8,128)(2,1)S(1)} %convert_element_type.6), channel_id=1, replica_groups=mesh['stn'=32,'zh'=2,'x'=4,'c'=2] {'stn'}, dimensions={0} | all-to-all | bytes 1048576 | tf_op jit(solution)/shard_map/all_to_all | solution.py:256
  131.7 0.1 convert_element_type.7.x
  131.8 2.4 %deliver.1 = f32[2,4,128,256]{3,2,1,0:T(8,128)} custom-call(s32[2]{0:T(128)S(1)} %pad_add_fusion.place, f32[32,64,128]{2,1,0:T(8,128)S(1)} %convert_element_type.7.x), custom_call_target="tpu_custom_call" | custom-call | tf_op jit(solution)/shard_map/deliver/pallas_call | solution.py:218
  (5 shorter events, 0.1 us)
Async XLA Ops:
  1.5 16.7 %collective-permute-start = (bf16[2,6,32,128]{3,2,1,0:T(8,128)(2,1)S(1)}, bf16[2,6,32,128]{3,2,1,0:T(8,128)(2,1)S(1)}, u32[]{:S(2)}, u32[]{:S(2)}) collective-permute-start(bf16[2,6,32,128]{3,2,1,0:T(8,128)(2,1)S(1)} %get-tuple-element.8), channel_id=1, source_target_pairs={{5,2},{6,4},{7,6},{21,18},{22,20},{23,22},{37,34},{38,36},{39,38},... | collective-permute-start | bytes 294920 | tf_op jit(solution)/shard_map/ppermute | solution.py:236
  2.8 15.4 %collective-permute-start.3 = (bf16[2,6,32,128]{3,2,1,0:T(8,128)(2,1)S(1)}, bf16[2,6,32,128]{3,2,1,0:T(8,128)(2,1)S(1)}, u32[]{:S(2)}, u32[]{:S(2)}) collective-permute-start(bf16[2,6,32,128]{3,2,1,0:T(8,128)(2,1)S(1)} %get-tuple-element.9), channel_id=1, source_target_pairs={{5,0},{6,2},{7,4},{21,16},{22,18},{23,20},{37,32},{38,34},{39,36},... | collective-permute-start | bytes 294920 | tf_op jit(solution)/shard_map/ppermute | solution.py:236
  4.1 14.1 %collective-permute-start.2 = (bf16[2,6,32,128]{3,2,1,0:T(8,128)(2,1)S(1)}, bf16[2,6,32,128]{3,2,1,0:T(8,128)(2,1)S(1)}, u32[]{:S(2)}, u32[]{:S(2)}) collective-permute-start(bf16[2,6,32,128]{3,2,1,0:T(8,128)(2,1)S(1)} %get-tuple-element.10), channel_id=1, source_target_pairs={{5,6},{6,0},{7,2},{21,22},{22,16},{23,18},{37,38},{38,32},{39,34},... | collective-permute-start | bytes 294920 | tf_op jit(solution)/shard_map/ppermute | solution.py:236
  5.4 12.8 %collective-permute-start.1 = (bf16[2,6,32,128]{3,2,1,0:T(8,128)(2,1)S(1)}, bf16[2,6,32,128]{3,2,1,0:T(8,128)(2,1)S(1)}, u32[]{:S(2)}, u32[]{:S(2)}) collective-permute-start(bf16[2,6,32,128]{3,2,1,0:T(8,128)(2,1)S(1)} %get-tuple-element.11), channel_id=1, source_target_pairs={{5,4},{6,6},{7,0},{21,20},{22,22},{23,16},{37,36},{38,38},{39,32},... | collective-permute-start | bytes 294920 | tf_op jit(solution)/shard_map/ppermute | solution.py:236
  7.1 22.8 %all-to-all-start = ((bf16[8,2,6,32,128]{4,3,2,1,0:T(8,128)(2,1)}), bf16[8,2,6,32,128]{4,3,2,1,0:T(8,128)(2,1)S(1)}, u32[]{:S(2)}, u32[]{:S(2)}) async-start(bf16[8,2,6,32,128]{4,3,2,1,0:T(8,128)(2,1)} %bitcast.3), calls=%async_computation | async-start | bytes 1572864 | tf_op jit(solution)/shard_map/all_to_all | solution.py:249
  18.3 11.6 %copy-start.1 = (f32[16,32,128]{2,1,0:T(8,128)S(1)}, f32[16,32,128]{2,1,0:T(8,128)}, u32[]{:S(2)}) copy-start(f32[16,32,128]{2,1,0:T(8,128)} %constant.91.clone.taps) | copy-start | bytes 786436
  18.3 11.6 %copy-start = (bf16[512,256]{1,0:T(8,128)(2,1)S(1)}, bf16[512,256]{1,0:T(8,128)(2,1)}, u32[]{:S(2)}) copy-start(bf16[512,256]{1,0:T(8,128)(2,1)} %constant.93.clone.second) | copy-start | bytes 786436
  18.3 11.5 %copy-start.2 = (f32[2,32,128]{2,1,0:T(8,128)S(1)}, f32[2,32,128]{2,1,0:T(8,128)}, u32[]{:S(2)}) copy-start(f32[2,32,128]{2,1,0:T(8,128)} %constant.94.clone.twiddle) | copy-start | bytes 98308
  18.4 11.5 %copy-start.3 = (bf16[128,64]{1,0:T(8,128)(2,1)S(1)}, bf16[128,64]{1,0:T(8,128)(2,1)}, u32[]{:S(2)}) copy-start(bf16[128,64]{1,0:T(8,128)(2,1)} %constant.92.clone.first) | copy-start | bytes 49156
  18.4 11.5 %collective-permute-start.4 = (bf16[2,15,32,128]{3,2,1,0:T(8,128)(2,1)S(1)}, bf16[2,15,32,128]{3,2,1,0:T(8,128)(2,1)S(1)}, u32[]{:S(2)}, u32[]{:S(2)}) collective-permute-start(bf16[2,15,32,128]{3,2,1,0:T(8,128)(2,1)S(1)} %pad_maximum_fusion.1), channel_id=1, source_target_pairs={{0,8},{2,10},{4,12},{6,14},{16,24},{18,26},{20,28},{22,30},{32,40}... | collective-permute-start | bytes 737288 | tf_op jit(solution)/shard_map/ppermute | solution.py:242

commit v6 on v5

--- a/solution.py
+++ b/solution.py
@@ -17,6 +17,8 @@
 FRAMES = 96
 BLOCK = 24
 HIST = TAPS - 1
+LATE = 8
+FEW = BLOCK - LATE
 SENT = 6
 PER = 4
 PARAMS = pltpu.CompilerParams(vmem_limit_bytes=48 * 1024 * 1024)
@@ -54,41 +56,23 @@
     return first, second, twiddle
 
 
-def channelise_body(place, main, hist, taps, first, second, twiddle, out, frames, stage, turned_re, turned_im):
-    @pl.when(place[0] == 0)
-    def _():
-        for r in range(2):
-            frames[r, :HIST] = hist[r].astype(F32)
-            for s in range(4):
-                frames[r, HIST + SENT * s : HIST + SENT * (s + 1)] = main[s, r].astype(F32)
-
-    @pl.when(place[0] != 0)
-    def _():
-        for r in range(2):
-            frames[r, :3] = main[1, r, 3:].astype(F32)
-            for s in range(2, 8):
-                frames[r, 3 + SENT * (s - 2) : 3 + SENT * (s - 1)] = main[s, r].astype(F32)
-
+def spectrum(filtered, count, first, second, twiddle, stage, turned_re, turned_im, out):
     def pair(step, carry):
         for half in range(2):
-            f = 2 * step + half
             for r in range(2):
-                acc = taps[0] * frames[r, f]
-                for k in range(1, TAPS):
-                    acc = acc + taps[k] * frames[r, f + k]
-                stage[N1 * r : N1 * (r + 1), N2 * half : N2 * (half + 1)] = acc.astype(BF16)
+                stage[N1 * r : N1 * (r + 1), N2 * half : N2 * (half + 1)] = filtered(r, 2 * step + half).astype(BF16)
         both = jnp.dot(first[...], stage[...], preferred_element_type=F32)
         both = both[: 2 * N1] + both[2 * N1 :]
         for half in range(2):
             re = both[:N1, N2 * half : N2 * (half + 1)]
             im = both[N1:, N2 * half : N2 * (half + 1)]
-            f = 2 * step + half
-            turned_re[pl.ds(f, N1, stride=BLOCK), :] = re * twiddle[0] + im * twiddle[1]
-            turned_im[pl.ds(f, N1, stride=BLOCK), :] = im * twiddle[0] - re * twiddle[1]
+            rows = pl.ds(2 * step + half, N1, stride=count)
+            turned_re[rows, :] = re * twiddle[0] + im * twiddle[1]
+            turned_im[rows, :] = im * twiddle[0] - re * twiddle[1]
         return carry
 
-    lax.fori_loop(0, BLOCK // 2, pair, 0)
-    for t in range(3):
+    lax.fori_loop(0, count // 2, pair, 0)
+    for t in range(N1 * count // 256):
         rows = slice(256 * t, 256 * (t + 1))
         value = jnp.concatenate([turned_re[rows], turned_im[rows]], 1)
         high = value.astype(BF16)
@@ -98,25 +82,82 @@
         out[:, rows] = (both[: 2 * N2] + (both[2 * N2 :] + rest)).astype(BF16)
 
 
-def channelise(place, main, hist, interpret=False):
-    first, second, twiddle = tables()
-    args = (place, main, hist, prototype(), first, second, twiddle)
+def early_body(core, station, main, taps, first, second, twiddle, sums, out, frames, stage, turned_re, turned_im):
+    @pl.when(core[0] == 0)
+    def _():
+        for r in range(2):
+            frames[r, :HIST] = jnp.zeros((HIST, N1, N2), F32)
+            for s in range(4):
+                frames[r, HIST + SENT * s : HIST + SENT * (s + 1)] = main[s, r].astype(F32)
+
+    @pl.when(core[0] != 0)
+    def _():
+        for r in range(2):
+            frames[r, :3] = main[1, r, 3:].astype(F32)
+            for s in range(2, 8):
+                frames[r, 3 + SENT * (s - 2) : 3 + SENT * (s - 1)] = main[s, r].astype(F32)
+
+    def filtered(r, f):
+        acc = taps[0] * frames[r, f]
+        for k in range(1, TAPS):
+            acc = acc + taps[k] * frames[r, f + k]
+        return acc
+
+    def keep(f, carry):
+        for r in range(2):
+            sums[r, f] = filtered(r, f)
+        return carry
+
+    lax.fori_loop(0, FEW, keep, 0)
+    late = lambda r, f: filtered(r, FEW + f)
+    spectrum(late, LATE, first, second, twiddle, stage, turned_re, turned_im, out)
+
+
+def rest_body(core, station, sums, hist, done, taps, first, second, twiddle, out, total, past, stage, turned_re, turned_im):
+    out[:, N1 * FEW :] = done[...]
+    total[...] = sums[...]
+
+    @pl.when(core[0] == 0)
+    def _():
+        past[...] = hist[...].astype(F32)
+        for f in range(HIST):
+            for r in range(2):
+                acc = sums[r, f]
+                for k in range(HIST - f):
+                    acc = acc + taps[k] * past[r, f + k]
+                total[r, f] = acc
+
+    spectrum(lambda r, f: total[r, f], FEW, first, second, twiddle, stage, turned_re, turned_im, out)
+
+
+def kernel(body, scalars, args, out_shape, scratch, frames, name, interpret):
     vmem = pl.BlockSpec(memory_space=pltpu.VMEM)
+    scratch = scratch + [
+        pltpu.VMEM((2 * N1, 2 * N2), BF16),
+        pltpu.VMEM((N1 * frames, N2), F32),
+        pltpu.VMEM((N1 * frames, N2), F32),
+    ]
     return pl.pallas_call(
-        channelise_body,
-        out_shape=jax.ShapeDtypeStruct((2 * N2, N1 * BLOCK), BF16),
-        in_specs=[pl.BlockSpec(memory_space=pltpu.SMEM)] + [vmem] * 6,
-        out_specs=vmem,
-        scratch_shapes=[
-            pltpu.VMEM((2, BLOCK + HIST, N1, N2), F32),
-            pltpu.VMEM((2 * N1, 2 * N2), BF16),
-            pltpu.VMEM((N1 * BLOCK, N2), F32),
-            pltpu.VMEM((N1 * BLOCK, N2), F32),
-        ],
+        body,
+        out_shape=out_shape,
+        in_specs=[pl.BlockSpec(memory_space=pltpu.SMEM)] * len(scalars) + [vmem] * len(args),
+        out_specs=jax.tree.map(lambda _: vmem, out_shape),
+        scratch_shapes=scratch,
         compiler_params=PARAMS,
         interpret=interpret,
-        name="channelise",
-    )(*[jnp.asarray(a) for a in args])
+        name=name,
+    )(*scalars, *args)
+
+
+def channelise(scalars, main, hist, interpret=False):
+    fixed = [jnp.asarray(a) for a in (prototype(), *tables())]
+    shape = jax.ShapeDtypeStruct
+    outs = (shape((2, FEW, N1, N2), F32), shape((2 * N2, N1 * LATE), BF16))
+    scratch = [pltpu.VMEM((2, BLOCK + HIST, N1, N2), F32)]
+    sums, done = kernel(early_body, scalars, (main, *fixed), outs, scratch, LATE, "early", interpret)
+    outs = shape((2 * N2, N1 * BLOCK), BF16)
+    scratch = [pltpu.VMEM((2, FEW, N1, N2), F32), pltpu.VMEM((2, HIST, N1, N2), F32)]
+    return kernel(rest_body, scalars, (sums, hist, done, *fixed), outs, scratch, FEW, "rest", interpret)
 
 
 def regroup_body(x, out):
@@ -130,8 +171,10 @@
         for t in range(N1 * BLOCK // 128):
             piece = jnp.concatenate([p[:, 128 * t : 128 * (t + 1)] for p in pieces], 0).T
             for part in range(16):
-                row = 128 * t + 8 * part
-                out[row // BLOCK, z, row % BLOCK : row % BLOCK + 8, :] = piece[8 * part : 8 * part + 8].astype(BF16)
+                k, f = divmod(128 * t + 8 * part, FEW)
+                if k >= N1:
+                    k, f = 16 * t + part - N1 * FEW // 8, FEW
+                out[k, z, f : f + 8, :] = piece[8 * part : 8 * part + 8].astype(BF16)
 
 
 def regroup(x, interpret=False):
@@ -190,11 +233,11 @@
     )(x)
 
 
-def deliver_body(place, x, out, wide, order):
+def deliver_body(station, x, out, wide, order):
     here = x[:, :8, :]
     line, lane = (lax.broadcasted_iota(jnp.int32, (N1, 8, 128), d) for d in (1, 2))
-    holder = (line == 1) & (lane == place[1])
-    mirror = (line == 0) & (lane == place[1] + STN)
+    holder = (line == 1) & (lane == station[0])
+    mirror = (line == 0) & (lane == station[0] + STN)
 
     def pick(mask):
         return jnp.sum(jnp.sum(jnp.where(mask, here, 0.0), 1, keepdims=True), 2, keepdims=True)
@@ -213,7 +256,7 @@
             out[row // PER, row % PER, :, 128 * half : 128 * (half + 1)] = order[base : base + 128, :]
 
 
-def deliver(place, x, interpret=False):
+def deliver(station, x, interpret=False):
     vmem = pl.BlockSpec(memory_space=pltpu.VMEM)
     return pl.pallas_call(
         deliver_body,
@@ -224,7 +267,7 @@
         compiler_params=PARAMS,
         interpret=interpret,
         name="deliver",
-    )(place, x)
+    )(station, x)
 
 
 def last_frames(frames):
@@ -247,14 +290,15 @@
     hist = last_frames(frames)
     doubled = jnp.repeat(frames.transpose(1, 0, 2, 3, 4), Q // X, 0)
     half = lax.all_to_all(doubled, ("x", "c"), 0, 0, tiled=True)
-    place = jnp.stack([lax.axis_index("c"), lax.axis_index("stn")]).astype(jnp.int32)
-    spectra = channelise(place, half, hist)
+    core = lax.axis_index("c").astype(jnp.int32).reshape(1)
+    station = lax.axis_index("stn").astype(jnp.int32).reshape(1)
+    spectra = channelise((core, station), half, hist)
     spectra = lax.all_to_all(spectra.reshape(Q, 2 * N2 // Q, N1 * BLOCK), ("x", "c"), 0, 0, tiled=True)
     spectra = regroup(spectra).reshape(STN * ZH, BLOCK, 128)
     spectra = lax.all_to_all(spectra, ("stn", "zh"), 0, 0, tiled=True)
     products = correlate(spectra.reshape(STN, ZH, BLOCK, 128))
     products = lax.all_to_all(products.astype(jnp.float16), "stn", 0, 0, tiled=True)
-    return deliver(place, products.astype(F32))
+    return deliver(station, products.astype(F32))
 
 
 def solution(mesh):

time: 135 us -> 132 us (0.978)
  blocking collectives: 95.9 us -> 93.7 us
    all_to_all x1, waiting for transfers between devices: 0.01 us -> 3.69 us  [shards(): half = lax.all_to_all(doubled, ('x', 'c'), 0, 0, tiled=True)]
    ppermute x1, waiting for transfers between devices: 3.6 us -> 0.01 us  [last_frames(): lax.ppermute(last, ('zh', 'x', 'c'), [(Q // X * x, Q + Q // X * x) for x...]
    all_to_all x1, blocking collectives: 50.8 us -> 49.3 us  [shards(): spectra = lax.all_to_all(spectra, ('stn', 'zh'), 0, 0, tiled=True)]
    pallas_call x1 -> x2, Pallas kernels: 4 us -> 4.35 us  [kernel(): pl.pallas_call(body, out_shape=out_shape, in_specs=[pl.BlockSpec(memory_s...]
  transfers between devices with their start and end apart: 6 -> 6, of which waited for: 1 -> 1; matrix products, arithmetic and copies ran while one was open for 1% -> 1% of each run, Pallas kernels for 0% -> 2%
where the time goes in v6:
time: 132 us
  blocking collectives  93.7 us (71%)
  starting transfers between devices  23.4 us (18%)
  Pallas kernels  7.99 us (6%)
  waiting for transfers between devices  3.71 us (3%)
  local copies, waits for them, and re-layouts  2.56 us (2%)
    all_to_all x1, blocking collectives, shards(): spectra = lax.all_to_all(spectra, ('stn', 'zh'), 0, 0, tiled=True)  49.3 us
    all_to_all x1, blocking collectives, shards(): lax.all_to_all(products.astype(jnp.float16), 'stn', 0, 0, tiled=True)  33.1 us
    all_to_all x1, blocking collectives, shards(): lax.all_to_all(spectra.reshape(Q, 2 * N2 // Q, N1 * BLOCK), ('x', 'c'), 0...  11.3 us
    all_to_all x1, starting transfers between devices, shards(): half = lax.all_to_all(doubled, ('x', 'c'), 0, 0, tiled=True)  11.1 us
    ppermute x1, starting transfers between devices, last_frames(): lax.ppermute(last, ('zh', 'x', 'c'), [(Q // X * x, Q + Q // X * x) for x...  7.77 us
    ppermute x4, starting transfers between devices, last_frames(): rounds.append(lax.ppermute(piece, ('zh', 'x', 'c'), pairs))  4.54 us
    pallas_call x2, Pallas kernels, kernel(): pl.pallas_call(body, out_shape=out_shape, in_specs=[pl.BlockSpec(memory_s...  4.35 us
    all_to_all x1, waiting for transfers between devices, shards(): half = lax.all_to_all(doubled, ('x', 'c'), 0, 0, tiled=True)  3.69 us
  transfers between devices with their start and end apart: 6, of which 1 were waited for; matrix products, arithmetic and copies ran while one was open for 1% of the time, Pallas kernels for 2%

profile of v6, /device:TPU:2, one launch (start us, length us, event | category | flops | bytes accessed | tf_op | source)
XLA Modules:
  0.0 131.8 jit_solution(212381939234620673)
XLA Ops:
  0.0 1.4 %reshape.23 = bf16[2,4,6,32,128]{4,3,2,1,0:T(8,128)(2,1)S(1)} reshape(bf16[2,4,24576]{2,1,0:T(4,128)(2,1)} %param.5) | data formatting | bytes 786432 | tf_op jit(solution)/shard_map/reshape | solution.py:289
  1.5 1.3 collective-permute-start
  2.8 1.3 collective-permute-start.3
  4.1 1.3 collective-permute-start.2
  5.4 0.7 collective-permute-start.1
  6.1 1.0 broadcast_in_dim.3
  7.1 11.1 %all-to-all-start = ((bf16[8,2,6,32,128]{4,3,2,1,0:T(8,128)(2,1)}), bf16[8,2,6,32,128]{4,3,2,1,0:T(8,128)(2,1)S(1)}, u32[]{:S(2)}, u32[]{:S(2)}) async-start(bf16[8,2,6,32,128]{4,3,2,1,0:T(8,128)(2,1)} %bitcast.3), calls=%async_computation | async-start | bytes 1572864 | tf_op jit(solution)/shard_map/all_to_all | solution.py:292
  18.2 0.0 collective-permute-done
  18.2 0.0 collective-permute-done.3
  18.2 0.0 collective-permute-done.2
  18.2 0.0 collective-permute-done.1
  18.2 0.1 pad_maximum_fusion
  18.3 0.0 copy-start.1
  18.3 0.0 copy-start
  18.3 0.0 copy-start.2
  18.4 0.0 copy-start.3
  18.4 7.8 %collective-permute-start.4 = (bf16[2,15,32,128]{3,2,1,0:T(8,128)(2,1)S(1)}, bf16[2,15,32,128]{3,2,1,0:T(8,128)(2,1)S(1)}, u32[]{:S(2)}, u32[]{:S(2)}) collective-permute-start(bf16[2,15,32,128]{3,2,1,0:T(8,128)(2,1)S(1)} %pad_maximum_fusion.1), channel_id=1, source_target_pairs={{0,8},{2,10},{4,12},{6,14},{16,24},{18,26},{20,28},{22,30},{32,40}... | collective-permute-start | bytes 737288 | tf_op jit(solution)/shard_map/ppermute | solution.py:285
  26.2 3.7 %all-to-all-done.main = bf16[8,2,6,32,128]{4,3,2,1,0:T(8,128)(2,1)S(1)} async-done(((bf16[8,2,6,32,128]{4,3,2,1,0:T(8,128)(2,1)}), bf16[8,2,6,32,128]{4,3,2,1,0:T(8,128)(2,1)S(1)}, u32[]{:S(2)}, u32[]{:S(2)}) %all-to-all-start) | async-done | bytes 786464 | tf_op jit(solution)/shard_map/all_to_all | solution.py:292
  29.9 0.0 copy-done.1
  29.9 0.0 copy-done
  29.9 0.0 copy-done.2
  29.9 0.0 copy-done.3
  29.9 2.2 %early.1 = (f32[2,16,32,128]{3,2,1,0:T(8,128)S(1)}, bf16[256,256]{1,0:T(8,128)(2,1)S(1)}) custom-call(s32[1]{0:T(128)} %bitcast.1.core, s32[1]{0:T(128)} %bitcast.station, bf16[8,2,6,32,128]{4,3,2,1,0:T(8,128)(2,1)S(1)} %all-to-all-done.main, f32[16,32,128]{2,1,0:T(8,128)S(1)} %copy-done.1, bf16[128,64]{1,0:T(8,128)(2,1)S(1)} %copy-done.3, ...), custom_call_target="tpu_custom_call" | custom-call | tf_op jit(solution)/shard_map/early/pallas_call | solution.py:140
  32.1 0.0 collective-permute-done.4.hist
  32.1 2.2 %rest.1 = bf16[256,768]{1,0:T(8,128)(2,1)S(1)} custom-call(s32[1]{0:T(128)} %bitcast.1.core, s32[1]{0:T(128)} %bitcast.station, f32[2,16,32,128]{3,2,1,0:T(8,128)S(1)} %get-tuple-element.7.sums, bf16[2,15,32,128]{3,2,1,0:T(8,128)(2,1)S(1)} %collective-permute-done.4.hist, bf16[256,256]{1,0:T(8,128)(2,1)S(1)} %get-tuple-element.8.done, ...), custom_call_target="tpu_custom_call" | custom-call | tf_op jit(solution)/shard_map/rest/pallas_call | solution.py:140
  34.3 11.3 %all_to_all.20.x = bf16[8,32,768]{2,1,0:T(8,128)(2,1)S(1)} all-to-all(bf16[8,32,768]{2,1,0:T(8,128)(2,1)S(1)} %bitcast.26), channel_id=1, replica_groups=mesh['stn'=32,'zh'=2,'x'=4,'c'=2] {'x','c'}, dimensions={0} | all-to-all | bytes 786432 | tf_op jit(solution)/shard_map/all_to_all | solution.py:296
  45.6 0.2 regroup.1
  45.8 49.3 %all_to_all.21 = bf16[64,24,128]{2,1,0:T(8,128)(2,1)S(1)} all-to-all(bf16[64,24,128]{2,1,0:T(8,128)(2,1)S(1)} %bitcast.25), channel_id=1, replica_groups=mesh['stn'=32,'zh'=2,'x'=4,'c'=2] {'stn','zh'}, dimensions={0} | all-to-all | bytes 786432 | tf_op jit(solution)/shard_map/all_to_all | solution.py:298
  95.1 1.6 %correlate.1 = f32[32,64,128]{2,1,0:T(8,128)S(1)} custom-call(bf16[32,2,24,128]{3,2,1,0:T(8,128)(2,1)S(1)} %bitcast.27), custom_call_target="tpu_custom_call" | custom-call | tf_op jit(solution)/shard_map/correlate/pallas_call | solution.py:224
  96.7 0.1 convert_element_type.6
  96.8 33.1 %all_to_all.22 = f16[32,64,128]{2,1,0:T(8,128)(2,1)S(1)} all-to-all(f16[32,64,128]{2,1,0:T(8,128)(2,1)S(1)} %convert_element_type.6), channel_id=1, replica_groups=mesh['stn'=32,'zh'=2,'x'=4,'c'=2] {'stn'}, dimensions={0} | all-to-all | bytes 1048576 | tf_op jit(solution)/shard_map/all_to_all | solution.py:300
  129.8 0.1 convert_element_type.7.x
  129.9 1.9 %deliver.1 = f32[2,4,128,256]{3,2,1,0:T(8,128)} custom-call(s32[1]{0:T(128)} %bitcast.station, f32[32,64,128]{2,1,0:T(8,128)S(1)} %convert_element_type.7.x), custom_call_target="tpu_custom_call" | custom-call | tf_op jit(solution)/shard_map/deliver/pallas_call | solution.py:261
  (5 shorter events, 0.1 us)
Async XLA Ops:
  1.5 16.7 %collective-permute-start = (bf16[2,6,32,128]{3,2,1,0:T(8,128)(2,1)S(1)}, bf16[2,6,32,128]{3,2,1,0:T(8,128)(2,1)S(1)}, u32[]{:S(2)}, u32[]{:S(2)}) collective-permute-start(bf16[2,6,32,128]{3,2,1,0:T(8,128)(2,1)S(1)} %get-tuple-element.12), channel_id=1, source_target_pairs={{5,2},{6,4},{7,6},{21,18},{22,20},{23,22},{37,34},{38,36},{39,38},... | collective-permute-start | bytes 294920 | tf_op jit(solution)/shard_map/ppermute | solution.py:279
  2.8 15.4 %collective-permute-start.3 = (bf16[2,6,32,128]{3,2,1,0:T(8,128)(2,1)S(1)}, bf16[2,6,32,128]{3,2,1,0:T(8,128)(2,1)S(1)}, u32[]{:S(2)}, u32[]{:S(2)}) collective-permute-start(bf16[2,6,32,128]{3,2,1,0:T(8,128)(2,1)S(1)} %get-tuple-element.13), channel_id=1, source_target_pairs={{5,0},{6,2},{7,4},{21,16},{22,18},{23,20},{37,32},{38,34},{39,36},... | collective-permute-start | bytes 294920 | tf_op jit(solution)/shard_map/ppermute | solution.py:279
  4.1 14.1 %collective-permute-start.2 = (bf16[2,6,32,128]{3,2,1,0:T(8,128)(2,1)S(1)}, bf16[2,6,32,128]{3,2,1,0:T(8,128)(2,1)S(1)}, u32[]{:S(2)}, u32[]{:S(2)}) collective-permute-start(bf16[2,6,32,128]{3,2,1,0:T(8,128)(2,1)S(1)} %get-tuple-element.14), channel_id=1, source_target_pairs={{5,6},{6,0},{7,2},{21,22},{22,16},{23,18},{37,38},{38,32},{39,34},... | collective-permute-start | bytes 294920 | tf_op jit(solution)/shard_map/ppermute | solution.py:279
  5.4 12.8 %collective-permute-start.1 = (bf16[2,6,32,128]{3,2,1,0:T(8,128)(2,1)S(1)}, bf16[2,6,32,128]{3,2,1,0:T(8,128)(2,1)S(1)}, u32[]{:S(2)}, u32[]{:S(2)}) collective-permute-start(bf16[2,6,32,128]{3,2,1,0:T(8,128)(2,1)S(1)} %get-tuple-element.15), channel_id=1, source_target_pairs={{5,4},{6,6},{7,0},{21,20},{22,22},{23,16},{37,36},{38,38},{39,32},... | collective-permute-start | bytes 294920 | tf_op jit(solution)/shard_map/ppermute | solution.py:279
  7.1 22.8 %all-to-all-start = ((bf16[8,2,6,32,128]{4,3,2,1,0:T(8,128)(2,1)}), bf16[8,2,6,32,128]{4,3,2,1,0:T(8,128)(2,1)S(1)}, u32[]{:S(2)}, u32[]{:S(2)}) async-start(bf16[8,2,6,32,128]{4,3,2,1,0:T(8,128)(2,1)} %bitcast.3), calls=%async_computation | async-start | bytes 1572864 | tf_op jit(solution)/shard_map/all_to_all | solution.py:292
  18.3 11.6 %copy-start.1 = (f32[16,32,128]{2,1,0:T(8,128)S(1)}, f32[16,32,128]{2,1,0:T(8,128)}, u32[]{:S(2)}) copy-start(f32[16,32,128]{2,1,0:T(8,128)} %constant.91.clone.taps) | copy-start | bytes 786436
  18.3 11.6 %copy-start = (bf16[512,256]{1,0:T(8,128)(2,1)S(1)}, bf16[512,256]{1,0:T(8,128)(2,1)}, u32[]{:S(2)}) copy-start(bf16[512,256]{1,0:T(8,128)(2,1)} %constant.93.clone.second) | copy-start | bytes 786436
  18.3 11.5 %copy-start.2 = (f32[2,32,128]{2,1,0:T(8,128)S(1)}, f32[2,32,128]{2,1,0:T(8,128)}, u32[]{:S(2)}) copy-start(f32[2,32,128]{2,1,0:T(8,128)} %constant.94.clone.twiddle) | copy-start | bytes 98308
  18.4 11.5 %copy-start.3 = (bf16[128,64]{1,0:T(8,128)(2,1)S(1)}, bf16[128,64]{1,0:T(8,128)(2,1)}, u32[]{:S(2)}) copy-start(bf16[128,64]{1,0:T(8,128)(2,1)} %constant.92.clone.first) | copy-start | bytes 49156
  18.4 13.7 %collective-permute-start.4 = (bf16[2,15,32,128]{3,2,1,0:T(8,128)(2,1)S(1)}, bf16[2,15,32,128]{3,2,1,0:T(8,128)(2,1)S(1)}, u32[]{:S(2)}, u32[]{:S(2)}) collective-permute-start(bf16[2,15,32,128]{3,2,1,0:T(8,128)(2,1)S(1)} %pad_maximum_fusion.1), channel_id=1, source_target_pairs={{0,8},{2,10},{4,12},{6,14},{16,24},{18,26},{20,28},{22,30},{32,40}... | collective-permute-start | bytes 737288 | tf_op jit(solution)/shard_map/ppermute | solution.py:285

commit v7 on v6

--- a/solution.py
+++ b/solution.py
@@ -82,25 +82,20 @@
         out[:, rows] = (both[: 2 * N2] + (both[2 * N2 :] + rest)).astype(BF16)
 
 
-def early_body(core, station, main, taps, first, second, twiddle, sums, out, frames, stage, turned_re, turned_im):
-    @pl.when(core[0] == 0)
-    def _():
-        for r in range(2):
-            frames[r, :HIST] = jnp.zeros((HIST, N1, N2), F32)
-            for s in range(4):
-                frames[r, HIST + SENT * s : HIST + SENT * (s + 1)] = main[s, r].astype(F32)
-
-    @pl.when(core[0] != 0)
-    def _():
-        for r in range(2):
-            frames[r, :3] = main[1, r, 3:].astype(F32)
-            for s in range(2, 8):
-                frames[r, 3 + SENT * (s - 2) : 3 + SENT * (s - 1)] = main[s, r].astype(F32)
+def early_body(core, column, station, *refs):
+    pieces, refs = refs[:Q], refs[Q:]
+    taps, first, second, twiddle, sums, out, frames, stage, turned_re, turned_im = refs
+    start = BLOCK * core[0]
+    for r in range(2):
+        frames[r, :HIST] = jnp.zeros((HIST, N1, N2), F32)
+        for p in range(Q):
+            shard = Q // X * ((column[0] + X - p // 2) % X) + (core[0] + p) % 2
+            frames[r, pl.ds(HIST + SENT * shard, SENT)] = pieces[p][r].astype(F32)
 
     def filtered(r, f):
-        acc = taps[0] * frames[r, f]
+        acc = taps[0] * frames[r, start + f]
         for k in range(1, TAPS):
-            acc = acc + taps[k] * frames[r, f + k]
+            acc = acc + taps[k] * frames[r, start + f + k]
         return acc
 
     def keep(f, carry):
@@ -113,7 +108,7 @@
     spectrum(late, LATE, first, second, twiddle, stage, turned_re, turned_im, out)
 
 
-def rest_body(core, station, sums, hist, done, taps, first, second, twiddle, out, total, past, stage, turned_re, turned_im):
+def rest_body(core, column, station, sums, hist, done, taps, first, second, twiddle, out, total, past, stage, turned_re, turned_im):
     out[:, N1 * FEW :] = done[...]
     total[...] = sums[...]
 
@@ -149,12 +144,12 @@
     )(*scalars, *args)
 
 
-def channelise(scalars, main, hist, interpret=False):
+def channelise(scalars, pieces, hist, interpret=False):
     fixed = [jnp.asarray(a) for a in (prototype(), *tables())]
     shape = jax.ShapeDtypeStruct
     outs = (shape((2, FEW, N1, N2), F32), shape((2 * N2, N1 * LATE), BF16))
-    scratch = [pltpu.VMEM((2, BLOCK + HIST, N1, N2), F32)]
-    sums, done = kernel(early_body, scalars, (main, *fixed), outs, scratch, LATE, "early", interpret)
+    scratch = [pltpu.VMEM((2, HIST + Q * SENT, N1, N2), F32)]
+    sums, done = kernel(early_body, scalars, (*pieces, *fixed), outs, scratch, LATE, "early", interpret)
     outs = shape((2 * N2, N1 * BLOCK), BF16)
     scratch = [pltpu.VMEM((2, FEW, N1, N2), F32), pltpu.VMEM((2, HIST, N1, N2), F32)]
     return kernel(rest_body, scalars, (sums, hist, done, *fixed), outs, scratch, FEW, "rest", interpret)
@@ -285,20 +280,28 @@
     return lax.ppermute(last, ("zh", "x", "c"), [(Q // X * x, Q + Q // X * x) for x in range(X)])
 
 
+def half_of_input(frames):
+    pieces = []
+    for p in range(Q):
+        dx, dc = divmod(p, 2)
+        piece = lax.dynamic_index_in_dim(frames, (lax.axis_index("x") + dx) % X, 1, False)
+        pairs = [(2 * x + c, 2 * ((x + dx) % X) + (c + dc) % 2) for x in range(X) for c in range(2)]
+        pieces.append(lax.ppermute(piece, ("x", "c"), pairs) if p else piece)
+    return pieces
+
+
 def shards(voltages):
     frames = voltages.reshape(2, PER, SENT, N1, N2)
     hist = last_frames(frames)
-    doubled = jnp.repeat(frames.transpose(1, 0, 2, 3, 4), Q // X, 0)
-    half = lax.all_to_all(doubled, ("x", "c"), 0, 0, tiled=True)
-    core = lax.axis_index("c").astype(jnp.int32).reshape(1)
-    station = lax.axis_index("stn").astype(jnp.int32).reshape(1)
-    spectra = channelise((core, station), half, hist)
+    pieces = half_of_input(frames)
+    scalars = [lax.axis_index(name).astype(jnp.int32).reshape(1) for name in ("c", "x", "stn")]
+    spectra = channelise(scalars, pieces, hist)
     spectra = lax.all_to_all(spectra.reshape(Q, 2 * N2 // Q, N1 * BLOCK), ("x", "c"), 0, 0, tiled=True)
     spectra = regroup(spectra).reshape(STN * ZH, BLOCK, 128)
     spectra = lax.all_to_all(spectra, ("stn", "zh"), 0, 0, tiled=True)
     products = correlate(spectra.reshape(STN, ZH, BLOCK, 128))
     products = lax.all_to_all(products.astype(jnp.float16), "stn", 0, 0, tiled=True)
-    return deliver(station, products.astype(F32))
+    return deliver(scalars[2], products.astype(F32))
 
 
 def solution(mesh):

time: 132 us -> 138 us (1.045)
  waiting for transfers between devices: 3.71 us -> 14.5 us
  blocking collectives: 93.7 us -> 84.1 us
  starting transfers between devices: 23.4 us -> 28.7 us
    ppermute x0 -> x7, starting transfers between devices: none -> 21.7 us  [half_of_input(): pieces.append(lax.ppermute(piece, ('x', 'c'), pairs) if p else piece)]
    ppermute x4, waiting for transfers between devices: 0.01 us -> 11.6 us  [last_frames(): rounds.append(lax.ppermute(piece, ('zh', 'x', 'c'), pairs))]
    all_to_all x1 -> x0, starting transfers between devices: 11.1 us -> none  [shards(): half = lax.all_to_all(doubled, ('x', 'c'), 0, 0, tiled=True)]
    all_to_all x1, blocking collectives: 49.3 us -> 39 us  [shards(): spectra = lax.all_to_all(spectra, ('stn', 'zh'), 0, 0, tiled=True)]
    ppermute x1, starting transfers between devices: 7.77 us -> 2.44 us  [last_frames(): lax.ppermute(last, ('zh', 'x', 'c'), [(Q // X * x, Q + Q // X * x) for x...]
    all_to_all x1 -> x0, waiting for transfers between devices: 3.69 us -> none  [shards(): half = lax.all_to_all(doubled, ('x', 'c'), 0, 0, tiled=True)]
    ppermute x0 -> x7, waiting for transfers between devices: none -> 2.92 us  [half_of_input(): pieces.append(lax.ppermute(piece, ('x', 'c'), pairs) if p else piece)]
  transfers between devices with their start and end apart: 6 -> 12, of which waited for: 1 -> 4; matrix products, arithmetic and copies ran while one was open for 1% -> 0% of each run, Pallas kernels for 2% -> 2%
where the time goes in v7:
time: 138 us
  blocking collectives  84.1 us (61%)
  starting transfers between devices  28.7 us (21%)
  waiting for transfers between devices  14.5 us (11%)
  Pallas kernels  8.06 us (6%)
  local copies, waits for them, and re-layouts  1.54 us (1%)
    all_to_all x1, blocking collectives, shards(): spectra = lax.all_to_all(spectra, ('stn', 'zh'), 0, 0, tiled=True)  39 us
    all_to_all x1, blocking collectives, shards(): lax.all_to_all(products.astype(jnp.float16), 'stn', 0, 0, tiled=True)  33.1 us
    ppermute x7, starting transfers between devices, half_of_input(): pieces.append(lax.ppermute(piece, ('x', 'c'), pairs) if p else piece)  21.7 us
    all_to_all x1, blocking collectives, shards(): lax.all_to_all(spectra.reshape(Q, 2 * N2 // Q, N1 * BLOCK), ('x', 'c'), 0...  12 us
    ppermute x4, waiting for transfers between devices, last_frames(): rounds.append(lax.ppermute(piece, ('zh', 'x', 'c'), pairs))  11.6 us
    ppermute x4, starting transfers between devices, last_frames(): rounds.append(lax.ppermute(piece, ('zh', 'x', 'c'), pairs))  4.54 us
    pallas_call x2, Pallas kernels, kernel(): pl.pallas_call(body, out_shape=out_shape, in_specs=[pl.BlockSpec(memory_s...  4.42 us
    ppermute x7, waiting for transfers between devices, half_of_input(): pieces.append(lax.ppermute(piece, ('x', 'c'), pairs) if p else piece)  2.92 us
  transfers between devices with their start and end apart: 12, of which 4 were waited for; matrix products, arithmetic and copies ran while one was open for 0% of the time, Pallas kernels for 2%

profile of v7, /device:TPU:2, one launch (start us, length us, event | category | flops | bytes accessed | tf_op | source)
XLA Modules:
  0.0 137.6 jit_solution(4840511402930598571)
XLA Ops:
  0.0 1.4 %reshape.24 = bf16[2,4,6,32,128]{4,3,2,1,0:T(8,128)(2,1)S(1)} reshape(bf16[2,4,24576]{2,1,0:T(4,128)(2,1)} %param.5) | data formatting | bytes 786432 | tf_op jit(solution)/shard_map/reshape | solution.py:294
  1.5 0.1 dynamic-slice_bitcast_fusion.6
  1.5 1.3 collective-permute-start.7
  2.8 0.7 collective-permute-start.8
  3.5 1.3 collective-permute-start.9
  4.8 1.3 collective-permute-start.10
  6.2 1.3 collective-permute-done.7
  7.5 0.0 collective-permute-done.8
  7.5 7.9 %collective-permute-done.9 = bf16[2,6,32,128]{3,2,1,0:T(8,128)(2,1)S(1)} collective-permute-done((bf16[2,6,32,128]{3,2,1,0:T(8,128)(2,1)S(1)}, bf16[2,6,32,128]{3,2,1,0:T(8,128)(2,1)S(1)}, u32[]{:S(2)}, u32[]{:S(2)}) %collective-permute-start.9) | collective-permute-done | bytes 98336 | tf_op jit(solution)/shard_map/ppermute | solution.py:274
  15.4 2.4 %collective-permute-done.10 = bf16[2,6,32,128]{3,2,1,0:T(8,128)(2,1)S(1)} collective-permute-done((bf16[2,6,32,128]{3,2,1,0:T(8,128)(2,1)S(1)}, bf16[2,6,32,128]{3,2,1,0:T(8,128)(2,1)S(1)}, u32[]{:S(2)}, u32[]{:S(2)}) %collective-permute-start.10) | collective-permute-done | bytes 98336 | tf_op jit(solution)/shard_map/ppermute | solution.py:274
  17.8 0.1 pad_maximum_fusion
  17.8 0.0 copy-start.1
  17.9 0.0 copy-start
  17.9 0.0 copy-start.2
  17.9 0.0 copy-start.3
  17.9 2.4 %collective-permute-start.11 = (bf16[2,15,32,128]{3,2,1,0:T(8,128)(2,1)S(1)}, bf16[2,15,32,128]{3,2,1,0:T(8,128)(2,1)S(1)}, u32[]{:S(2)}, u32[]{:S(2)}) collective-permute-start(bf16[2,15,32,128]{3,2,1,0:T(8,128)(2,1)S(1)} %pad_maximum_fusion.1), channel_id=1, source_target_pairs={{0,8},{2,10},{4,12},{6,14},{16,24},{18,26},{20,28},{22,30},{32,40}... | collective-permute-start | bytes 737288 | tf_op jit(solution)/shard_map/ppermute | solution.py:280
  20.4 1.9 %collective-permute-start.4 = (bf16[2,6,32,128]{3,2,1,0:T(8,128)(2,1)S(1)}, bf16[2,6,32,128]{3,2,1,0:T(8,128)(2,1)S(1)}, u32[]{:S(2)}, u32[]{:S(2)}) collective-permute-start(bf16[2,6,32,128]{3,2,1,0:T(8,128)(2,1)S(1)} %get-tuple-element.13), channel_id=1, source_target_pairs={{0,5},{1,4},{2,7},{3,6},{4,1},{5,0},{6,3},{7,2},{8,13},{9,12},{10,... | collective-permute-start | bytes 294920 | tf_op jit(solution)/shard_map/ppermute | solution.py:289
  22.3 4.0 %collective-permute-start.3 = (bf16[2,6,32,128]{3,2,1,0:T(8,128)(2,1)S(1)}, bf16[2,6,32,128]{3,2,1,0:T(8,128)(2,1)S(1)}, u32[]{:S(2)}, u32[]{:S(2)}) collective-permute-start(bf16[2,6,32,128]{3,2,1,0:T(8,128)(2,1)S(1)} %get-tuple-element.13), channel_id=1, source_target_pairs={{0,4},{1,5},{2,6},{3,7},{4,0},{5,1},{6,2},{7,3},{8,12},{9,13},{10,... | collective-permute-start | bytes 294920 | tf_op jit(solution)/shard_map/ppermute | solution.py:289
  26.4 4.2 %collective-permute-start.2 = (bf16[2,6,32,128]{3,2,1,0:T(8,128)(2,1)S(1)}, bf16[2,6,32,128]{3,2,1,0:T(8,128)(2,1)S(1)}, u32[]{:S(2)}, u32[]{:S(2)}) collective-permute-start(bf16[2,6,32,128]{3,2,1,0:T(8,128)(2,1)S(1)} %get-tuple-element.14), channel_id=1, source_target_pairs={{0,3},{1,2},{2,5},{3,4},{4,7},{5,6},{6,1},{7,0},{8,11},{9,10},{10,... | collective-permute-start | bytes 294920 | tf_op jit(solution)/shard_map/ppermute | solution.py:289
  30.6 3.1 %collective-permute-start.1 = (bf16[2,6,32,128]{3,2,1,0:T(8,128)(2,1)S(1)}, bf16[2,6,32,128]{3,2,1,0:T(8,128)(2,1)S(1)}, u32[]{:S(2)}, u32[]{:S(2)}) collective-permute-start(bf16[2,6,32,128]{3,2,1,0:T(8,128)(2,1)S(1)} %get-tuple-element.14), channel_id=1, source_target_pairs={{0,2},{1,3},{2,4},{3,5},{4,6},{5,7},{6,0},{7,1},{8,10},{9,11},{10,... | collective-permute-start | bytes 294920 | tf_op jit(solution)/shard_map/ppermute | solution.py:289
  33.7 0.0 collective-permute-done.4.refs_5_
  33.7 1.9 %collective-permute-start = (bf16[2,6,32,128]{3,2,1,0:T(8,128)(2,1)S(1)}, bf16[2,6,32,128]{3,2,1,0:T(8,128)(2,1)S(1)}, u32[]{:S(2)}, u32[]{:S(2)}) collective-permute-start(bf16[2,6,32,128]{3,2,1,0:T(8,128)(2,1)S(1)} %get-tuple-element.15.refs_0_), channel_id=1, source_target_pairs={{0,1},{1,0},{2,3},{3,2},{4,5},{5,4},{6,7},{7,6},{8,9},{9,8},{10,11... | collective-permute-start | bytes 294920 | tf_op jit(solution)/shard_map/ppermute | solution.py:289
  35.7 0.0 collective-permute-done.3.refs_4_
  35.7 2.8 %collective-permute-start.6 = (bf16[2,6,32,128]{3,2,1,0:T(8,128)(2,1)S(1)}, bf16[2,6,32,128]{3,2,1,0:T(8,128)(2,1)S(1)}, u32[]{:S(2)}, u32[]{:S(2)}) collective-permute-start(bf16[2,6,32,128]{3,2,1,0:T(8,128)(2,1)S(1)} %get-tuple-element.19), channel_id=1, source_target_pairs={{0,7},{1,6},{2,1},{3,0},{4,3},{5,2},{6,5},{7,4},{8,15},{9,14},{10,... | collective-permute-start | bytes 294920 | tf_op jit(solution)/shard_map/ppermute | solution.py:289
  38.5 0.0 collective-permute-done.2.refs_3_
  38.5 3.7 %collective-permute-start.5 = (bf16[2,6,32,128]{3,2,1,0:T(8,128)(2,1)S(1)}, bf16[2,6,32,128]{3,2,1,0:T(8,128)(2,1)S(1)}, u32[]{:S(2)}, u32[]{:S(2)}) collective-permute-start(bf16[2,6,32,128]{3,2,1,0:T(8,128)(2,1)S(1)} %get-tuple-element.19), channel_id=1, source_target_pairs={{0,6},{1,7},{2,0},{3,1},{4,2},{5,3},{6,4},{7,5},{8,14},{9,15},{10,... | collective-permute-start | bytes 294920 | tf_op jit(solution)/shard_map/ppermute | solution.py:289
  42.2 0.0 collective-permute-done.1.refs_2_
  42.2 0.0 collective-permute-done.refs_1_
  42.2 0.0 collective-permute-done.6.refs_7_
  42.2 2.9 %collective-permute-done.5.refs_6_ = bf16[2,6,32,128]{3,2,1,0:T(8,128)(2,1)S(1)} collective-permute-done((bf16[2,6,32,128]{3,2,1,0:T(8,128)(2,1)S(1)}, bf16[2,6,32,128]{3,2,1,0:T(8,128)(2,1)S(1)}, u32[]{:S(2)}, u32[]{:S(2)}) %collective-permute-start.5) | collective-permute-done | bytes 98336 | tf_op jit(solution)/shard_map/ppermute | solution.py:289
  45.1 0.0 copy-done.1
  45.1 0.0 copy-done
  45.1 0.0 copy-done.2
  45.1 0.0 copy-done.3
  45.2 2.3 %early.1 = (f32[2,16,32,128]{3,2,1,0:T(8,128)S(1)}, bf16[256,256]{1,0:T(8,128)(2,1)S(1)}) custom-call(s32[1]{0:T(128)} %bitcast.1.core, s32[1]{0:T(128)} %bitcast.2.column, s32[1]{0:T(128)} %bitcast.station, bf16[2,6,32,128]{3,2,1,0:T(8,128)(2,1)S(1)} %get-tuple-element.15.refs_0_, bf16[2,6,32,128]{3,2,1,0:T(8,128)(2,1)S(1)} %collective-permute-done.refs_1_, ...), custom_call_target="tpu_custom_call" | custom-call | tf_op jit(solution)/shard_map/early/pallas_call | solution.py:135
  47.4 0.0 collective-permute-done.11.hist
  47.4 2.2 %rest.1 = bf16[256,768]{1,0:T(8,128)(2,1)S(1)} custom-call(s32[1]{0:T(128)} %bitcast.1.core, s32[1]{0:T(128)} %bitcast.2.column, s32[1]{0:T(128)} %bitcast.station, f32[2,16,32,128]{3,2,1,0:T(8,128)S(1)} %get-tuple-element.7.sums, bf16[2,15,32,128]{3,2,1,0:T(8,128)(2,1)S(1)} %collective-permute-done.11.hist, bf16[256,256]{1,0:T(8,128)(2,1)S(1)} %get-tuple-element.8.done, ...), custom_call_target="tpu_custom_call" | custom-call | tf_op jit(solution)/shard_map/rest/pallas_call | solution.py:135
  49.6 12.0 %all_to_all.15.x = bf16[8,32,768]{2,1,0:T(8,128)(2,1)S(1)} all-to-all(bf16[8,32,768]{2,1,0:T(8,128)(2,1)S(1)} %bitcast.42), channel_id=1, replica_groups=mesh['stn'=32,'zh'=2,'x'=4,'c'=2] {'x','c'}, dimensions={0} | all-to-all | bytes 786432 | tf_op jit(solution)/shard_map/all_to_all | solution.py:299
  61.6 0.2 regroup.1
  61.8 39.0 %all_to_all.16 = bf16[64,24,128]{2,1,0:T(8,128)(2,1)S(1)} all-to-all(bf16[64,24,128]{2,1,0:T(8,128)(2,1)S(1)} %bitcast.40), channel_id=1, replica_groups=mesh['stn'=32,'zh'=2,'x'=4,'c'=2] {'stn','zh'}, dimensions={0} | all-to-all | bytes 786432 | tf_op jit(solution)/shard_map/all_to_all | solution.py:301
  100.8 1.6 %correlate.1 = f32[32,64,128]{2,1,0:T(8,128)S(1)} custom-call(bf16[32,2,24,128]{3,2,1,0:T(8,128)(2,1)S(1)} %bitcast.41), custom_call_target="tpu_custom_call" | custom-call | tf_op jit(solution)/shard_map/correlate/pallas_call | solution.py:219
  102.4 0.1 convert_element_type.6
  102.5 33.1 %all_to_all.17 = f16[32,64,128]{2,1,0:T(8,128)(2,1)S(1)} all-to-all(f16[32,64,128]{2,1,0:T(8,128)(2,1)S(1)} %convert_element_type.6), channel_id=1, replica_groups=mesh['stn'=32,'zh'=2,'x'=4,'c'=2] {'stn'}, dimensions={0} | all-to-all | bytes 1048576 | tf_op jit(solution)/shard_map/all_to_all | solution.py:303
  135.6 0.1 convert_element_type.7.x
  135.7 1.9 %deliver.1 = f32[2,4,128,256]{3,2,1,0:T(8,128)} custom-call(s32[1]{0:T(128)} %bitcast.station, f32[32,64,128]{2,1,0:T(8,128)S(1)} %convert_element_type.7.x), custom_call_target="tpu_custom_call" | custom-call | tf_op jit(solution)/shard_map/deliver/pallas_call | solution.py:256
  (3 shorter events, 0.1 us)
Async XLA Ops:
  1.5 5.9 %collective-permute-start.7 = (bf16[2,6,32,128]{3,2,1,0:T(8,128)(2,1)S(1)}, bf16[2,6,32,128]{3,2,1,0:T(8,128)(2,1)S(1)}, u32[]{:S(2)}, u32[]{:S(2)}) collective-permute-start(bf16[2,6,32,128]{3,2,1,0:T(8,128)(2,1)S(1)} %get-tuple-element.12), channel_id=1, source_target_pairs={{5,2},{6,4},{7,6},{21,18},{22,20},{23,22},{37,34},{38,36},{39,38},... | collective-permute-start | bytes 294920 | tf_op jit(solution)/shard_map/ppermute | solution.py:274
  2.8 4.6 %collective-permute-start.8 = (bf16[2,6,32,128]{3,2,1,0:T(8,128)(2,1)S(1)}, bf16[2,6,32,128]{3,2,1,0:T(8,128)(2,1)S(1)}, u32[]{:S(2)}, u32[]{:S(2)}) collective-permute-start(bf16[2,6,32,128]{3,2,1,0:T(8,128)(2,1)S(1)} %get-tuple-element.16), channel_id=1, source_target_pairs={{5,4},{6,6},{7,0},{21,20},{22,22},{23,16},{37,36},{38,38},{39,32},... | collective-permute-start | bytes 294920 | tf_op jit(solution)/shard_map/ppermute | solution.py:274
  3.5 11.9 %collective-permute-start.9 = (bf16[2,6,32,128]{3,2,1,0:T(8,128)(2,1)S(1)}, bf16[2,6,32,128]{3,2,1,0:T(8,128)(2,1)S(1)}, u32[]{:S(2)}, u32[]{:S(2)}) collective-permute-start(bf16[2,6,32,128]{3,2,1,0:T(8,128)(2,1)S(1)} %get-tuple-element.17), channel_id=1, source_target_pairs={{5,6},{6,0},{7,2},{21,22},{22,16},{23,18},{37,38},{38,32},{39,34},... | collective-permute-start | bytes 294920 | tf_op jit(solution)/shard_map/ppermute | solution.py:274
  4.8 12.9 %collective-permute-start.10 = (bf16[2,6,32,128]{3,2,1,0:T(8,128)(2,1)S(1)}, bf16[2,6,32,128]{3,2,1,0:T(8,128)(2,1)S(1)}, u32[]{:S(2)}, u32[]{:S(2)}) collective-permute-start(bf16[2,6,32,128]{3,2,1,0:T(8,128)(2,1)S(1)} %get-tuple-element.18), channel_id=1, source_target_pairs={{5,0},{6,2},{7,4},{21,16},{22,18},{23,20},{37,32},{38,34},{39,36},... | collective-permute-start | bytes 294920 | tf_op jit(solution)/shard_map/ppermute | solution.py:274
  17.8 27.3 %copy-start.1 = (f32[16,32,128]{2,1,0:T(8,128)S(1)}, f32[16,32,128]{2,1,0:T(8,128)}, u32[]{:S(2)}) copy-start(f32[16,32,128]{2,1,0:T(8,128)} %constant.131.clone.refs_8_.taps) | copy-start | bytes 786436
  17.9 27.3 %copy-start = (bf16[512,256]{1,0:T(8,128)(2,1)S(1)}, bf16[512,256]{1,0:T(8,128)(2,1)}, u32[]{:S(2)}) copy-start(bf16[512,256]{1,0:T(8,128)(2,1)} %constant.133.clone.refs_10_.second) | copy-start | bytes 786436
  17.9 27.3 %copy-start.2 = (f32[2,32,128]{2,1,0:T(8,128)S(1)}, f32[2,32,128]{2,1,0:T(8,128)}, u32[]{:S(2)}) copy-start(f32[2,32,128]{2,1,0:T(8,128)} %constant.134.clone.refs_11_.twiddle) | copy-start | bytes 98308
  17.9 27.2 %copy-start.3 = (bf16[128,64]{1,0:T(8,128)(2,1)S(1)}, bf16[128,64]{1,0:T(8,128)(2,1)}, u32[]{:S(2)}) copy-start(bf16[128,64]{1,0:T(8,128)(2,1)} %constant.132.clone.refs_9_.first) | copy-start | bytes 49156
  17.9 29.5 %collective-permute-start.11 = (bf16[2,15,32,128]{3,2,1,0:T(8,128)(2,1)S(1)}, bf16[2,15,32,128]{3,2,1,0:T(8,128)(2,1)S(1)}, u32[]{:S(2)}, u32[]{:S(2)}) collective-permute-start(bf16[2,15,32,128]{3,2,1,0:T(8,128)(2,1)S(1)} %pad_maximum_fusion.1), channel_id=1, source_target_pairs={{0,8},{2,10},{4,12},{6,14},{16,24},{18,26},{20,28},{22,30},{32,40}... | collective-permute-start | bytes 737288 | tf_op jit(solution)/shard_map/ppermute | solution.py:280
  20.4 13.3 %collective-permute-start.4 = (bf16[2,6,32,128]{3,2,1,0:T(8,128)(2,1)S(1)}, bf16[2,6,32,128]{3,2,1,0:T(8,128)(2,1)S(1)}, u32[]{:S(2)}, u32[]{:S(2)}) collective-permute-start(bf16[2,6,32,128]{3,2,1,0:T(8,128)(2,1)S(1)} %get-tuple-element.13), channel_id=1, source_target_pairs={{0,5},{1,4},{2,7},{3,6},{4,1},{5,0},{6,3},{7,2},{8,13},{9,12},{10,... | collective-permute-start | bytes 294920 | tf_op jit(solution)/shard_map/ppermute | solution.py:289
  22.3 13.3 %collective-permute-start.3 = (bf16[2,6,32,128]{3,2,1,0:T(8,128)(2,1)S(1)}, bf16[2,6,32,128]{3,2,1,0:T(8,128)(2,1)S(1)}, u32[]{:S(2)}, u32[]{:S(2)}) collective-permute-start(bf16[2,6,32,128]{3,2,1,0:T(8,128)(2,1)S(1)} %get-tuple-element.13), channel_id=1, source_target_pairs={{0,4},{1,5},{2,6},{3,7},{4,0},{5,1},{6,2},{7,3},{8,12},{9,13},{10,... | collective-permute-start | bytes 294920 | tf_op jit(solution)/shard_map/ppermute | solution.py:289
  26.4 12.2 %collective-permute-start.2 = (bf16[2,6,32,128]{3,2,1,0:T(8,128)(2,1)S(1)}, bf16[2,6,32,128]{3,2,1,0:T(8,128)(2,1)S(1)}, u32[]{:S(2)}, u32[]{:S(2)}) collective-permute-start(bf16[2,6,32,128]{3,2,1,0:T(8,128)(2,1)S(1)} %get-tuple-element.14), channel_id=1, source_target_pairs={{0,3},{1,2},{2,5},{3,4},{4,7},{5,6},{6,1},{7,0},{8,11},{9,10},{10,... | collective-permute-start | bytes 294920 | tf_op jit(solution)/shard_map/ppermute | solution.py:289
  30.6 11.6 %collective-permute-start.1 = (bf16[2,6,32,128]{3,2,1,0:T(8,128)(2,1)S(1)}, bf16[2,6,32,128]{3,2,1,0:T(8,128)(2,1)S(1)}, u32[]{:S(2)}, u32[]{:S(2)}) collective-permute-start(bf16[2,6,32,128]{3,2,1,0:T(8,128)(2,1)S(1)} %get-tuple-element.14), channel_id=1, source_target_pairs={{0,2},{1,3},{2,4},{3,5},{4,6},{5,7},{6,0},{7,1},{8,10},{9,11},{10,... | collective-permute-start | bytes 294920 | tf_op jit(solution)/shard_map/ppermute | solution.py:289
  33.7 8.5 %collective-permute-start = (bf16[2,6,32,128]{3,2,1,0:T(8,128)(2,1)S(1)}, bf16[2,6,32,128]{3,2,1,0:T(8,128)(2,1)S(1)}, u32[]{:S(2)}, u32[]{:S(2)}) collective-permute-start(bf16[2,6,32,128]{3,2,1,0:T(8,128)(2,1)S(1)} %get-tuple-element.15.refs_0_), channel_id=1, source_target_pairs={{0,1},{1,0},{2,3},{3,2},{4,5},{5,4},{6,7},{7,6},{8,9},{9,8},{10,11... | collective-permute-start | bytes 294920 | tf_op jit(solution)/shard_map/ppermute | solution.py:289
  35.7 6.5 %collective-permute-start.6 = (bf16[2,6,32,128]{3,2,1,0:T(8,128)(2,1)S(1)}, bf16[2,6,32,128]{3,2,1,0:T(8,128)(2,1)S(1)}, u32[]{:S(2)}, u32[]{:S(2)}) collective-permute-start(bf16[2,6,32,128]{3,2,1,0:T(8,128)(2,1)S(1)} %get-tuple-element.19), channel_id=1, source_target_pairs={{0,7},{1,6},{2,1},{3,0},{4,3},{5,2},{6,5},{7,4},{8,15},{9,14},{10,... | collective-permute-start | bytes 294920 | tf_op jit(solution)/shard_map/ppermute | solution.py:289
  38.5 6.6 %collective-permute-start.5 = (bf16[2,6,32,128]{3,2,1,0:T(8,128)(2,1)S(1)}, bf16[2,6,32,128]{3,2,1,0:T(8,128)(2,1)S(1)}, u32[]{:S(2)}, u32[]{:S(2)}) collective-permute-start(bf16[2,6,32,128]{3,2,1,0:T(8,128)(2,1)S(1)} %get-tuple-element.19), channel_id=1, source_target_pairs={{0,6},{1,7},{2,0},{3,1},{4,2},{5,3},{6,4},{7,5},{8,14},{9,15},{10,... | collective-permute-start | bytes 294920 | tf_op jit(solution)/shard_map/ppermute | solution.py:289

commit v8 on v7

--- a/solution.py
+++ b/solution.py
@@ -82,20 +82,19 @@
         out[:, rows] = (both[: 2 * N2] + (both[2 * N2 :] + rest)).astype(BF16)
 
 
-def early_body(core, column, station, *refs):
-    pieces, refs = refs[:Q], refs[Q:]
+def early_body(place, station, *refs):
+    pieces, refs = refs[:PER], refs[PER:]
     taps, first, second, twiddle, sums, out, frames, stage, turned_re, turned_im = refs
-    start = BLOCK * core[0]
     for r in range(2):
         frames[r, :HIST] = jnp.zeros((HIST, N1, N2), F32)
-        for p in range(Q):
-            shard = Q // X * ((column[0] + X - p // 2) % X) + (core[0] + p) % 2
+        for p in range(PER):
+            shard = jnp.bitwise_xor(place[0] % PER, p)
             frames[r, pl.ds(HIST + SENT * shard, SENT)] = pieces[p][r].astype(F32)
 
     def filtered(r, f):
-        acc = taps[0] * frames[r, start + f]
+        acc = taps[0] * frames[r, f]
         for k in range(1, TAPS):
-            acc = acc + taps[k] * frames[r, start + f + k]
+            acc = acc + taps[k] * frames[r, f + k]
         return acc
 
     def keep(f, carry):
@@ -108,19 +107,24 @@
     spectrum(late, LATE, first, second, twiddle, stage, turned_re, turned_im, out)
 
 
-def rest_body(core, column, station, sums, hist, done, taps, first, second, twiddle, out, total, past, stage, turned_re, turned_im):
+def rest_body(place, station, sums, far, near, done, taps, first, second, twiddle, out, total, past, stage, turned_re, turned_im):
     out[:, N1 * FEW :] = done[...]
-    total[...] = sums[...]
-
-    @pl.when(core[0] == 0)
+
+    @pl.when(place[0] < PER)
     def _():
-        past[...] = hist[...].astype(F32)
+        past[...] = far[...].astype(F32)
+
+    @pl.when(place[0] >= PER)
+    def _():
+        past[...] = near[...].astype(F32)
+
+    for r in range(2):
         for f in range(HIST):
-            for r in range(2):
-                acc = sums[r, f]
-                for k in range(HIST - f):
-                    acc = acc + taps[k] * past[r, f + k]
-                total[r, f] = acc
+            acc = sums[r, f]
+            for k in range(HIST - f):
+                acc = acc + taps[k] * past[r, f + k]
+            total[r, f] = acc
+        total[r, HIST:] = sums[r, HIST:]
 
     spectrum(lambda r, f: total[r, f], FEW, first, second, twiddle, stage, turned_re, turned_im, out)
 
@@ -144,15 +148,15 @@
     )(*scalars, *args)
 
 
-def channelise(scalars, pieces, hist, interpret=False):
+def channelise(scalars, pieces, far, near, interpret=False):
     fixed = [jnp.asarray(a) for a in (prototype(), *tables())]
     shape = jax.ShapeDtypeStruct
     outs = (shape((2, FEW, N1, N2), F32), shape((2 * N2, N1 * LATE), BF16))
-    scratch = [pltpu.VMEM((2, HIST + Q * SENT, N1, N2), F32)]
+    scratch = [pltpu.VMEM((2, HIST + BLOCK, N1, N2), F32)]
     sums, done = kernel(early_body, scalars, (*pieces, *fixed), outs, scratch, LATE, "early", interpret)
     outs = shape((2 * N2, N1 * BLOCK), BF16)
     scratch = [pltpu.VMEM((2, FEW, N1, N2), F32), pltpu.VMEM((2, HIST, N1, N2), F32)]
-    return kernel(rest_body, scalars, (sums, hist, done, *fixed), outs, scratch, FEW, "rest", interpret)
+    return kernel(rest_body, scalars, (sums, far, near, done, *fixed), outs, scratch, FEW, "rest", interpret)
 
 
 def regroup_body(x, out):
@@ -161,7 +165,7 @@
         for c in range(2):
             for r in range(2):
                 for i in range(PER):
-                    pair = x[2 * i + c, 16 * z : 16 * z + 16, :].astype(F32)
+                    pair = x[PER * c + i, 16 * z : 16 * z + 16, :].astype(F32)
                     pieces.append(pair[8 * r : 8 * r + 8])
         for t in range(N1 * BLOCK // 128):
             piece = jnp.concatenate([p[:, 128 * t : 128 * (t + 1)] for p in pieces], 0).T
@@ -265,11 +269,10 @@
     )(station, x)
 
 
-def last_frames(frames):
-    q = Q // X * lax.axis_index("x") + lax.axis_index("c")
+def last_frames(frames, place):
     rounds = []
     for r in range(X):
-        piece = lax.dynamic_index_in_dim(frames, (q + r) % X, 1, False)
+        piece = lax.dynamic_index_in_dim(frames, (place + r) % X, 1, False)
         pairs = [(s, Q // X * ((s + r) % X)) for s in range(Q - 3, Q)]
         rounds.append(lax.ppermute(piece, ("zh", "x", "c"), pairs))
     rounds = jnp.stack(rounds)
@@ -277,31 +280,35 @@
         lax.dynamic_index_in_dim(rounds, (lax.axis_index("x") - s) % X, 0, False) for s in range(Q - 3, Q)
     ]
     last = jnp.concatenate([parts[0][:, 3:], parts[1], parts[2]], 1)
-    return lax.ppermute(last, ("zh", "x", "c"), [(Q // X * x, Q + Q // X * x) for x in range(X)])
-
-
-def half_of_input(frames):
+    last, frames = lax.optimization_barrier((last, frames))
+    return lax.ppermute(last, ("zh", "x", "c"), [(Q // X * i, Q + i) for i in range(PER)]), frames
+
+
+def block_of_input(frames, place):
     pieces = []
-    for p in range(Q):
-        dx, dc = divmod(p, 2)
-        piece = lax.dynamic_index_in_dim(frames, (lax.axis_index("x") + dx) % X, 1, False)
-        pairs = [(2 * x + c, 2 * ((x + dx) % X) + (c + dc) % 2) for x in range(X) for c in range(2)]
+    for p in range(PER):
+        piece = lax.dynamic_index_in_dim(frames, (place % PER) ^ p, 1, False)
+        pairs = [(t, t ^ p) for t in range(Q)]
         pieces.append(lax.ppermute(piece, ("x", "c"), pairs) if p else piece)
     return pieces
 
 
 def shards(voltages):
     frames = voltages.reshape(2, PER, SENT, N1, N2)
-    hist = last_frames(frames)
-    pieces = half_of_input(frames)
-    scalars = [lax.axis_index(name).astype(jnp.int32).reshape(1) for name in ("c", "x", "stn")]
-    spectra = channelise(scalars, pieces, hist)
+    place = Q // X * lax.axis_index("x") + lax.axis_index("c")
+    far, frames = last_frames(frames, place)
+    pieces = block_of_input(frames, place)
+    parts = [lax.dynamic_index_in_dim(jnp.stack(pieces), (place % PER) ^ s, 0, False) for s in (1, 2, 3)]
+    last = jnp.concatenate([parts[0][:, 3:], parts[1], parts[2]], 1)
+    near = lax.ppermute(last, ("x", "c"), [(t, t + PER) for t in range(PER)])
+    scalars = [a.astype(jnp.int32).reshape(1) for a in (place, lax.axis_index("stn"))]
+    spectra = channelise(scalars, pieces, far, near)
     spectra = lax.all_to_all(spectra.reshape(Q, 2 * N2 // Q, N1 * BLOCK), ("x", "c"), 0, 0, tiled=True)
     spectra = regroup(spectra).reshape(STN * ZH, BLOCK, 128)
     spectra = lax.all_to_all(spectra, ("stn", "zh"), 0, 0, tiled=True)
     products = correlate(spectra.reshape(STN, ZH, BLOCK, 128))
     products = lax.all_to_all(products.astype(jnp.float16), "stn", 0, 0, tiled=True)
-    return deliver(scalars[2], products.astype(F32))
+    return deliver(scalars[1], products.astype(F32))
 
 
 def solution(mesh):

time: 138 us -> 134 us (0.971)
  blocking collectives: 84.1 us -> 91.4 us
  waiting for transfers between devices: 14.5 us -> 7.37 us
  starting transfers between devices: 28.7 us -> 24.8 us
    ppermute x4, waiting for transfers between devices: 11.6 us -> 5.96 us  [last_frames(): rounds.append(lax.ppermute(piece, ('zh', 'x', 'c'), pairs))]
    all_to_all x1, blocking collectives: 39 us -> 44.6 us  [shards(): spectra = lax.all_to_all(spectra, ('stn', 'zh'), 0, 0, tiled=True)]
    ppermute x8 -> x5, starting transfers between devices: 24.1 us -> 20.3 us  [the longest x3 11.9 us: block_of_input(): pieces.append(lax.ppermute(piece, ('x', 'c'), pairs) if p else piece)]
    all_to_all x1, blocking collectives: 12 us -> 13.7 us  [shards(): lax.all_to_all(spectra.reshape(Q, 2 * N2 // Q, N1 * BLOCK), ('x', 'c'), 0...]
    ppermute x8 -> x5, waiting for transfers between devices: 2.93 us -> 1.42 us  [the longest x1 1.41 us: shards(): near = lax.ppermute(last, ('x', 'c'), [(t, t + PER) for t in range(PER)])]
  transfers between devices with their start and end apart: 12 -> 9, of which waited for: 4 -> 4; matrix products, arithmetic and copies ran while one was open for 0% -> 0% of each run, Pallas kernels for 2% -> 2%
where the time goes in v8:
time: 134 us
  blocking collectives  91.4 us (68%)
  starting transfers between devices  24.8 us (19%)
  Pallas kernels  8.03 us (6%)
  waiting for transfers between devices  7.37 us (6%)
  local copies, waits for them, and re-layouts  1.6 us (1%)
    all_to_all x1, blocking collectives, shards(): spectra = lax.all_to_all(spectra, ('stn', 'zh'), 0, 0, tiled=True)  44.6 us
    all_to_all x1, blocking collectives, shards(): lax.all_to_all(products.astype(jnp.float16), 'stn', 0, 0, tiled=True)  33.1 us
    all_to_all x1, blocking collectives, shards(): lax.all_to_all(spectra.reshape(Q, 2 * N2 // Q, N1 * BLOCK), ('x', 'c'), 0...  13.7 us
    ppermute x3, starting transfers between devices, block_of_input(): pieces.append(lax.ppermute(piece, ('x', 'c'), pairs) if p else piece)  11.9 us
    ppermute x4, waiting for transfers between devices, last_frames(): rounds.append(lax.ppermute(piece, ('zh', 'x', 'c'), pairs))  5.96 us
    ppermute x1, starting transfers between devices, shards(): near = lax.ppermute(last, ('x', 'c'), [(t, t + PER) for t in range(PER)])  5.01 us
    ppermute x4, starting transfers between devices, last_frames(): rounds.append(lax.ppermute(piece, ('zh', 'x', 'c'), pairs))  4.54 us
    pallas_call x2, Pallas kernels, kernel(): pl.pallas_call(body, out_shape=out_shape, in_specs=[pl.BlockSpec(memory_s...  4.39 us
  transfers between devices with their start and end apart: 9, of which 4 were waited for; matrix products, arithmetic and copies ran while one was open for 0% of the time, Pallas kernels for 2%

profile of v8, /device:TPU:2, one launch (start us, length us, event | category | flops | bytes accessed | tf_op | source)
XLA Modules:
  0.0 133.9 jit_solution(5002669605683692029)
XLA Ops:
  0.0 1.4 %reshape.21 = bf16[2,4,6,32,128]{4,3,2,1,0:T(8,128)(2,1)S(1)} reshape(bf16[2,4,24576]{2,1,0:T(4,128)(2,1)} %param.5) | data formatting | bytes 786432 | tf_op jit(solution)/shard_map/reshape | solution.py:297
  1.5 1.3 collective-permute-start
  2.8 1.3 collective-permute-start.3
  4.1 1.3 collective-permute-start.2
  5.4 0.7 collective-permute-start.1
  6.1 1.3 collective-permute-done
  7.4 4.2 %collective-permute-done.3 = bf16[2,6,32,128]{3,2,1,0:T(8,128)(2,1)S(1)} collective-permute-done((bf16[2,6,32,128]{3,2,1,0:T(8,128)(2,1)S(1)}, bf16[2,6,32,128]{3,2,1,0:T(8,128)(2,1)S(1)}, u32[]{:S(2)}, u32[]{:S(2)}) %collective-permute-start.3) | collective-permute-done | bytes 98336 | tf_op jit(solution)/shard_map/ppermute | solution.py:277
  11.6 0.5 collective-permute-done.2
  12.1 0.0 collective-permute-done.1
  12.1 0.1 pad_maximum_fusion
  12.2 0.1 dynamic-slice_bitcast_fusion.13
  12.3 1.9 %collective-permute-start.6 = (bf16[2,6,32,128]{3,2,1,0:T(8,128)(2,1)S(1)}, bf16[2,6,32,128]{3,2,1,0:T(8,128)(2,1)S(1)}, u32[]{:S(2)}, u32[]{:S(2)}) collective-permute-start(bf16[2,6,32,128]{3,2,1,0:T(8,128)(2,1)S(1)} %get-tuple-element.17), channel_id=1, source_target_pairs={{0,3},{1,2},{2,1},{3,0},{4,7},{5,6},{6,5},{7,4},{8,11},{9,10},{10,... | collective-permute-start | bytes 294920 | tf_op jit(solution)/shard_map/ppermute | solution.py:292
  14.2 8.0 %collective-permute-start.5 = (bf16[2,6,32,128]{3,2,1,0:T(8,128)(2,1)S(1)}, bf16[2,6,32,128]{3,2,1,0:T(8,128)(2,1)S(1)}, u32[]{:S(2)}, u32[]{:S(2)}) collective-permute-start(bf16[2,6,32,128]{3,2,1,0:T(8,128)(2,1)S(1)} %get-tuple-element.18), channel_id=1, source_target_pairs={{0,2},{1,3},{2,0},{3,1},{4,6},{5,7},{6,4},{7,5},{8,10},{9,11},{10,... | collective-permute-start | bytes 294920 | tf_op jit(solution)/shard_map/ppermute | solution.py:292
  22.2 2.0 %collective-permute-start.4 = (bf16[2,6,32,128]{3,2,1,0:T(8,128)(2,1)S(1)}, bf16[2,6,32,128]{3,2,1,0:T(8,128)(2,1)S(1)}, u32[]{:S(2)}, u32[]{:S(2)}) collective-permute-start(bf16[2,6,32,128]{3,2,1,0:T(8,128)(2,1)S(1)} %get-tuple-element.19), channel_id=1, source_target_pairs={{0,1},{1,0},{2,3},{3,2},{4,5},{5,4},{6,7},{7,6},{8,9},{9,8},{10,11... | collective-permute-start | bytes 294920 | tf_op jit(solution)/shard_map/ppermute | solution.py:292
  24.2 3.4 %collective-permute-start.7 = (bf16[2,15,32,128]{3,2,1,0:T(8,128)(2,1)S(1)}, bf16[2,15,32,128]{3,2,1,0:T(8,128)(2,1)S(1)}, u32[]{:S(2)}, u32[]{:S(2)}) collective-permute-start(bf16[2,15,32,128]{3,2,1,0:T(8,128)(2,1)S(1)} %pad_maximum_fusion.2), channel_id=1, source_target_pairs={{0,8},{2,9},{4,10},{6,11},{16,24},{18,25},{20,26},{22,27},{32,40},... | collective-permute-start | bytes 737288 | tf_op jit(solution)/shard_map/ppermute | solution.py:284
  27.6 0.0 collective-permute-done.6.refs_3_
  27.6 0.0 collective-permute-done.5.refs_2_
  27.6 0.0 collective-permute-done.4.refs_1_
  27.6 0.1 pad_maximum_fusion.1
  27.7 0.0 copy-start.1
  27.7 0.0 copy-start
  27.8 0.0 copy-start.2
  27.8 0.0 copy-start.3
  27.8 5.0 %collective-permute-start.8 = (bf16[2,15,32,128]{3,2,1,0:T(8,128)(2,1)S(1)}, bf16[2,15,32,128]{3,2,1,0:T(8,128)(2,1)S(1)}, u32[]{:S(2)}, u32[]{:S(2)}) collective-permute-start(bf16[2,15,32,128]{3,2,1,0:T(8,128)(2,1)S(1)} %pad_maximum_fusion.3), channel_id=1, source_target_pairs={{0,4},{1,5},{2,6},{3,7},{8,12},{9,13},{10,14},{11,15},{16,20},{17,... | collective-permute-start | bytes 737288 | tf_op jit(solution)/shard_map/ppermute | solution.py:303
  32.8 0.0 copy-done.1
  32.8 0.0 copy-done
  32.9 0.0 copy-done.2
  32.9 0.0 copy-done.3
  32.9 2.2 %early.1 = (f32[2,16,32,128]{3,2,1,0:T(8,128)S(1)}, bf16[256,256]{1,0:T(8,128)(2,1)S(1)}) custom-call(s32[1]{0:T(128)} %bitcast.1.place, s32[1]{0:T(128)} %bitcast.station, bf16[2,6,32,128]{3,2,1,0:T(8,128)(2,1)S(1)} %get-tuple-element.20.refs_0_, bf16[2,6,32,128]{3,2,1,0:T(8,128)(2,1)S(1)} %collective-permute-done.4.refs_1_, ...), custom_call_target="tpu_custom_call" | custom-call | tf_op jit(solution)/shard_map/early/pallas_call | solution.py:139
  35.1 0.0 collective-permute-done.7.far
  35.1 1.4 %collective-permute-done.8.near = bf16[2,15,32,128]{3,2,1,0:T(8,128)(2,1)S(1)} collective-permute-done((bf16[2,15,32,128]{3,2,1,0:T(8,128)(2,1)S(1)}, bf16[2,15,32,128]{3,2,1,0:T(8,128)(2,1)S(1)}, u32[]{:S(2)}, u32[]{:S(2)}) %collective-permute-start.8) | collective-permute-done | bytes 245792 | tf_op jit(solution)/shard_map/ppermute | solution.py:303
  36.5 2.2 %rest.1 = bf16[256,768]{1,0:T(8,128)(2,1)S(1)} custom-call(s32[1]{0:T(128)} %bitcast.1.place, s32[1]{0:T(128)} %bitcast.station, f32[2,16,32,128]{3,2,1,0:T(8,128)S(1)} %get-tuple-element.10.sums, bf16[2,15,32,128]{3,2,1,0:T(8,128)(2,1)S(1)} %collective-permute-done.7.far, bf16[2,15,32,128]{3,2,1,0:T(8,128)(2,1)S(1)} %collective-permute-done.8.near, ...), custom_call_target="tpu_custom_call" | custom-call | tf_op jit(solution)/shard_map/rest/pallas_call | solution.py:139
  38.7 13.7 %all_to_all.15.x = bf16[8,32,768]{2,1,0:T(8,128)(2,1)S(1)} all-to-all(bf16[8,32,768]{2,1,0:T(8,128)(2,1)S(1)} %bitcast.44), channel_id=1, replica_groups=mesh['stn'=32,'zh'=2,'x'=4,'c'=2] {'x','c'}, dimensions={0} | all-to-all | bytes 786432 | tf_op jit(solution)/shard_map/all_to_all | solution.py:306
  52.4 0.2 regroup.1
  52.6 44.6 %all_to_all.16 = bf16[64,24,128]{2,1,0:T(8,128)(2,1)S(1)} all-to-all(bf16[64,24,128]{2,1,0:T(8,128)(2,1)S(1)} %bitcast.42), channel_id=1, replica_groups=mesh['stn'=32,'zh'=2,'x'=4,'c'=2] {'stn','zh'}, dimensions={0} | all-to-all | bytes 786432 | tf_op jit(solution)/shard_map/all_to_all | solution.py:308
  97.2 1.6 %correlate.1 = f32[32,64,128]{2,1,0:T(8,128)S(1)} custom-call(bf16[32,2,24,128]{3,2,1,0:T(8,128)(2,1)S(1)} %bitcast.43), custom_call_target="tpu_custom_call" | custom-call | tf_op jit(solution)/shard_map/correlate/pallas_call | solution.py:223
  98.8 0.1 convert_element_type.6
  98.9 33.1 %all_to_all.17 = f16[32,64,128]{2,1,0:T(8,128)(2,1)S(1)} all-to-all(f16[32,64,128]{2,1,0:T(8,128)(2,1)S(1)} %convert_element_type.6), channel_id=1, replica_groups=mesh['stn'=32,'zh'=2,'x'=4,'c'=2] {'stn'}, dimensions={0} | all-to-all | bytes 1048576 | tf_op jit(solution)/shard_map/all_to_all | solution.py:310
  132.0 0.1 convert_element_type.7.x
  132.1 1.9 %deliver.1 = f32[2,4,128,256]{3,2,1,0:T(8,128)} custom-call(s32[1]{0:T(128)} %bitcast.station, f32[32,64,128]{2,1,0:T(8,128)S(1)} %convert_element_type.7.x), custom_call_target="tpu_custom_call" | custom-call | tf_op jit(solution)/shard_map/deliver/pallas_call | solution.py:260
  (7 shorter events, 0.2 us)
Async XLA Ops:
  1.5 5.9 %collective-permute-start = (bf16[2,6,32,128]{3,2,1,0:T(8,128)(2,1)S(1)}, bf16[2,6,32,128]{3,2,1,0:T(8,128)(2,1)S(1)}, u32[]{:S(2)}, u32[]{:S(2)}) collective-permute-start(bf16[2,6,32,128]{3,2,1,0:T(8,128)(2,1)S(1)} %get-tuple-element.24), channel_id=1, source_target_pairs={{5,2},{6,4},{7,6},{21,18},{22,20},{23,22},{37,34},{38,36},{39,38},... | collective-permute-start | bytes 294920 | tf_op jit(solution)/shard_map/ppermute | solution.py:277
  2.8 8.8 %collective-permute-start.3 = (bf16[2,6,32,128]{3,2,1,0:T(8,128)(2,1)S(1)}, bf16[2,6,32,128]{3,2,1,0:T(8,128)(2,1)S(1)}, u32[]{:S(2)}, u32[]{:S(2)}) collective-permute-start(bf16[2,6,32,128]{3,2,1,0:T(8,128)(2,1)S(1)} %get-tuple-element.25), channel_id=1, source_target_pairs={{5,0},{6,2},{7,4},{21,16},{22,18},{23,20},{37,32},{38,34},{39,36},... | collective-permute-start | bytes 294920 | tf_op jit(solution)/shard_map/ppermute | solution.py:277
  4.1 8.0 %collective-permute-start.2 = (bf16[2,6,32,128]{3,2,1,0:T(8,128)(2,1)S(1)}, bf16[2,6,32,128]{3,2,1,0:T(8,128)(2,1)S(1)}, u32[]{:S(2)}, u32[]{:S(2)}) collective-permute-start(bf16[2,6,32,128]{3,2,1,0:T(8,128)(2,1)S(1)} %get-tuple-element.26), channel_id=1, source_target_pairs={{5,6},{6,0},{7,2},{21,22},{22,16},{23,18},{37,38},{38,32},{39,34},... | collective-permute-start | bytes 294920 | tf_op jit(solution)/shard_map/ppermute | solution.py:277
  5.4 6.7 %collective-permute-start.1 = (bf16[2,6,32,128]{3,2,1,0:T(8,128)(2,1)S(1)}, bf16[2,6,32,128]{3,2,1,0:T(8,128)(2,1)S(1)}, u32[]{:S(2)}, u32[]{:S(2)}) collective-permute-start(bf16[2,6,32,128]{3,2,1,0:T(8,128)(2,1)S(1)} %get-tuple-element.27), channel_id=1, source_target_pairs={{5,4},{6,6},{7,0},{21,20},{22,22},{23,16},{37,36},{38,38},{39,32},... | collective-permute-start | bytes 294920 | tf_op jit(solution)/shard_map/ppermute | solution.py:277
  12.3 15.3 %collective-permute-start.6 = (bf16[2,6,32,128]{3,2,1,0:T(8,128)(2,1)S(1)}, bf16[2,6,32,128]{3,2,1,0:T(8,128)(2,1)S(1)}, u32[]{:S(2)}, u32[]{:S(2)}) collective-permute-start(bf16[2,6,32,128]{3,2,1,0:T(8,128)(2,1)S(1)} %get-tuple-element.17), channel_id=1, source_target_pairs={{0,3},{1,2},{2,1},{3,0},{4,7},{5,6},{6,5},{7,4},{8,11},{9,10},{10,... | collective-permute-start | bytes 294920 | tf_op jit(solution)/shard_map/ppermute | solution.py:292
  14.2 13.4 %collective-permute-start.5 = (bf16[2,6,32,128]{3,2,1,0:T(8,128)(2,1)S(1)}, bf16[2,6,32,128]{3,2,1,0:T(8,128)(2,1)S(1)}, u32[]{:S(2)}, u32[]{:S(2)}) collective-permute-start(bf16[2,6,32,128]{3,2,1,0:T(8,128)(2,1)S(1)} %get-tuple-element.18), channel_id=1, source_target_pairs={{0,2},{1,3},{2,0},{3,1},{4,6},{5,7},{6,4},{7,5},{8,10},{9,11},{10,... | collective-permute-start | bytes 294920 | tf_op jit(solution)/shard_map/ppermute | solution.py:292
  22.2 5.4 %collective-permute-start.4 = (bf16[2,6,32,128]{3,2,1,0:T(8,128)(2,1)S(1)}, bf16[2,6,32,128]{3,2,1,0:T(8,128)(2,1)S(1)}, u32[]{:S(2)}, u32[]{:S(2)}) collective-permute-start(bf16[2,6,32,128]{3,2,1,0:T(8,128)(2,1)S(1)} %get-tuple-element.19), channel_id=1, source_target_pairs={{0,1},{1,0},{2,3},{3,2},{4,5},{5,4},{6,7},{7,6},{8,9},{9,8},{10,11... | collective-permute-start | bytes 294920 | tf_op jit(solution)/shard_map/ppermute | solution.py:292
  24.2 10.9 %collective-permute-start.7 = (bf16[2,15,32,128]{3,2,1,0:T(8,128)(2,1)S(1)}, bf16[2,15,32,128]{3,2,1,0:T(8,128)(2,1)S(1)}, u32[]{:S(2)}, u32[]{:S(2)}) collective-permute-start(bf16[2,15,32,128]{3,2,1,0:T(8,128)(2,1)S(1)} %pad_maximum_fusion.2), channel_id=1, source_target_pairs={{0,8},{2,9},{4,10},{6,11},{16,24},{18,25},{20,26},{22,27},{32,40},... | collective-permute-start | bytes 737288 | tf_op jit(solution)/shard_map/ppermute | solution.py:284
  27.7 5.1 %copy-start.1 = (f32[16,32,128]{2,1,0:T(8,128)S(1)}, f32[16,32,128]{2,1,0:T(8,128)}, u32[]{:S(2)}) copy-start(f32[16,32,128]{2,1,0:T(8,128)} %constant.119.clone.refs_4_.taps) | copy-start | bytes 786436
  27.7 5.1 %copy-start = (bf16[512,256]{1,0:T(8,128)(2,1)S(1)}, bf16[512,256]{1,0:T(8,128)(2,1)}, u32[]{:S(2)}) copy-start(bf16[512,256]{1,0:T(8,128)(2,1)} %constant.121.clone.refs_6_.second) | copy-start | bytes 786436
  27.8 5.1 %copy-start.2 = (f32[2,32,128]{2,1,0:T(8,128)S(1)}, f32[2,32,128]{2,1,0:T(8,128)}, u32[]{:S(2)}) copy-start(f32[2,32,128]{2,1,0:T(8,128)} %constant.122.clone.refs_7_.twiddle) | copy-start | bytes 98308
  27.8 5.1 %copy-start.3 = (bf16[128,64]{1,0:T(8,128)(2,1)S(1)}, bf16[128,64]{1,0:T(8,128)(2,1)}, u32[]{:S(2)}) copy-start(bf16[128,64]{1,0:T(8,128)(2,1)} %constant.120.clone.refs_5_.first) | copy-start | bytes 49156
  27.8 8.7 %collective-permute-start.8 = (bf16[2,15,32,128]{3,2,1,0:T(8,128)(2,1)S(1)}, bf16[2,15,32,128]{3,2,1,0:T(8,128)(2,1)S(1)}, u32[]{:S(2)}, u32[]{:S(2)}) collective-permute-start(bf16[2,15,32,128]{3,2,1,0:T(8,128)(2,1)S(1)} %pad_maximum_fusion.3), channel_id=1, source_target_pairs={{0,4},{1,5},{2,6},{3,7},{8,12},{9,13},{10,14},{11,15},{16,20},{17,... | collective-permute-start | bytes 737288 | tf_op jit(solution)/shard_map/ppermute | solution.py:303

commit v9 on v7

--- a/solution.py
+++ b/solution.py
@@ -83,14 +83,14 @@
 
 
 def early_body(core, column, station, *refs):
-    pieces, refs = refs[:Q], refs[Q:]
+    pieces, refs = refs[:X], refs[X:]
     taps, first, second, twiddle, sums, out, frames, stage, turned_re, turned_im = refs
     start = BLOCK * core[0]
     for r in range(2):
         frames[r, :HIST] = jnp.zeros((HIST, N1, N2), F32)
         for p in range(Q):
             shard = Q // X * ((column[0] + X - p // 2) % X) + (core[0] + p) % 2
-            frames[r, pl.ds(HIST + SENT * shard, SENT)] = pieces[p][r].astype(F32)
+            frames[r, pl.ds(HIST + SENT * shard, SENT)] = pieces[p // 2][p % 2, r].astype(F32)
 
     def filtered(r, f):
         acc = taps[0] * frames[r, start + f]
@@ -281,12 +281,12 @@
 
 
 def half_of_input(frames):
+    other = lax.ppermute(frames, "c", [(0, 1), (1, 0)])
     pieces = []
-    for p in range(Q):
-        dx, dc = divmod(p, 2)
-        piece = lax.dynamic_index_in_dim(frames, (lax.axis_index("x") + dx) % X, 1, False)
-        pairs = [(2 * x + c, 2 * ((x + dx) % X) + (c + dc) % 2) for x in range(X) for c in range(2)]
-        pieces.append(lax.ppermute(piece, ("x", "c"), pairs) if p else piece)
+    for p in range(X):
+        i = (lax.axis_index("x") + p) % X
+        piece = jnp.stack([lax.dynamic_index_in_dim(a, i, 1, False) for a in (frames, other)])
+        pieces.append(lax.ppermute(piece, "x", [(x, (x + p) % X) for x in range(X)]) if p else piece)
     return pieces
 
 

time: 138 us -> 129 us (0.935)
  starting transfers between devices: 28.7 us -> 21.5 us
    ppermute x7 -> x4, starting transfers between devices: 21.7 us -> 12.5 us  [the longest x3 10.6 us: half_of_input(): lax.ppermute(piece, 'x', [(x, (x + p) % X) for x in range(X)])]
    all_to_all x1, blocking collectives: 39 us -> 36.9 us  [shards(): spectra = lax.all_to_all(spectra, ('stn', 'zh'), 0, 0, tiled=True)]
    ppermute x4, waiting for transfers between devices: 11.6 us -> 9.51 us  [last_frames(): rounds.append(lax.ppermute(piece, ('zh', 'x', 'c'), pairs))]
    ppermute x1, starting transfers between devices: 2.44 us -> 4.38 us  [last_frames(): lax.ppermute(last, ('zh', 'x', 'c'), [(Q // X * x, Q + Q // X * x) for x...]
    ppermute x7 -> x4, waiting for transfers between devices: 2.92 us -> 3.83 us  [the longest x3 3.82 us: half_of_input(): lax.ppermute(piece, 'x', [(x, (x + p) % X) for x in range(X)])]
  transfers between devices with their start and end apart: 12 -> 9, of which waited for: 4 -> 4; matrix products, arithmetic and copies ran while one was open for 0% -> 0% of each run, Pallas kernels for 2% -> 2%
where the time goes in v9:
time: 129 us; the launch traced here: 128 us
  blocking collectives  82.9 us (64%)
  starting transfers between devices  21.5 us (17%)
  waiting for transfers between devices  13.3 us (10%)
  Pallas kernels  8.06 us (6%)
  local copies, waits for them, and re-layouts  1.61 us (1%)
    all_to_all x1, blocking collectives, shards(): spectra = lax.all_to_all(spectra, ('stn', 'zh'), 0, 0, tiled=True)  36.9 us
    all_to_all x1, blocking collectives, shards(): lax.all_to_all(products.astype(jnp.float16), 'stn', 0, 0, tiled=True)  33.1 us
    all_to_all x1, blocking collectives, shards(): lax.all_to_all(spectra.reshape(Q, 2 * N2 // Q, N1 * BLOCK), ('x', 'c'), 0...  13 us
    ppermute x3, starting transfers between devices, half_of_input(): lax.ppermute(piece, 'x', [(x, (x + p) % X) for x in range(X)])  10.6 us
    ppermute x4, waiting for transfers between devices, last_frames(): rounds.append(lax.ppermute(piece, ('zh', 'x', 'c'), pairs))  9.51 us
    ppermute x4, starting transfers between devices, last_frames(): rounds.append(lax.ppermute(piece, ('zh', 'x', 'c'), pairs))  4.54 us
    pallas_call x2, Pallas kernels, kernel(): pl.pallas_call(body, out_shape=out_shape, in_specs=[pl.BlockSpec(memory_s...  4.42 us
    ppermute x1, starting transfers between devices, last_frames(): lax.ppermute(last, ('zh', 'x', 'c'), [(Q // X * x, Q + Q // X * x) for x...  4.38 us
  transfers between devices with their start and end apart: 9, of which 4 were waited for; matrix products, arithmetic and copies ran while one was open for 0% of the time, Pallas kernels for 2%

profile of v9, /device:TPU:2, one launch (start us, length us, event | category | flops | bytes accessed | tf_op | source)
XLA Modules:
  0.0 128.2 jit_solution(4042430783211672999)
XLA Ops:
  0.0 1.4 %reshape.32 = bf16[2,4,6,32,128]{4,3,2,1,0:T(8,128)(2,1)S(1)} reshape(bf16[2,4,24576]{2,1,0:T(4,128)(2,1)} %param.5) | data formatting | bytes 786432 | tf_op jit(solution)/shard_map/reshape | solution.py:294
  1.5 1.3 %collective-permute-start.4 = (bf16[2,6,32,128]{3,2,1,0:T(8,128)(2,1)S(1)}, bf16[2,6,32,128]{3,2,1,0:T(8,128)(2,1)S(1)}, u32[]{:S(2)}, u32[]{:S(2)}) collective-permute-start(bf16[2,6,32,128]{3,2,1,0:T(8,128)(2,1)S(1)} %get-tuple-element.12), channel_id=1, source_target_pairs={{5,2},{6,4},{7,6},{21,18},{22,20},{23,22},{37,34},{38,36},{39,38},... | collective-permute-start | bytes 294920 | tf_op jit(solution)/shard_map/ppermute | solution.py:274
  2.8 0.7 collective-permute-start.5
  3.5 1.3 %collective-permute-start.6 = (bf16[2,6,32,128]{3,2,1,0:T(8,128)(2,1)S(1)}, bf16[2,6,32,128]{3,2,1,0:T(8,128)(2,1)S(1)}, u32[]{:S(2)}, u32[]{:S(2)}) collective-permute-start(bf16[2,6,32,128]{3,2,1,0:T(8,128)(2,1)S(1)} %get-tuple-element.14), channel_id=1, source_target_pairs={{5,6},{6,0},{7,2},{21,22},{22,16},{23,18},{37,38},{38,32},{39,34},... | collective-permute-start | bytes 294920 | tf_op jit(solution)/shard_map/ppermute | solution.py:274
  4.8 1.3 %collective-permute-start.7 = (bf16[2,6,32,128]{3,2,1,0:T(8,128)(2,1)S(1)}, bf16[2,6,32,128]{3,2,1,0:T(8,128)(2,1)S(1)}, u32[]{:S(2)}, u32[]{:S(2)}) collective-permute-start(bf16[2,6,32,128]{3,2,1,0:T(8,128)(2,1)S(1)} %get-tuple-element.15), channel_id=1, source_target_pairs={{5,0},{6,2},{7,4},{21,16},{22,18},{23,20},{37,32},{38,34},{39,36},... | collective-permute-start | bytes 294920 | tf_op jit(solution)/shard_map/ppermute | solution.py:274
  6.1 1.9 %collective-permute-start = (bf16[2,4,6,32,128]{4,3,2,0,1:T(8,128)(2,1)S(1)}, bf16[2,4,6,32,128]{4,3,2,0,1:T(8,128)(2,1)S(1)}, u32[]{:S(2)}, u32[]{:S(2)}) collective-permute-start(bf16[2,4,6,32,128]{4,3,2,0,1:T(8,128)(2,1)S(1)} %copy.6), channel_id=1, source_target_pairs={{0,1},{1,0},{2,3},{3,2},{4,5},{5,4},{6,7},{7,6},{8,9},{9,8},{10,11... | collective-permute-start | bytes 1179656 | tf_op jit(solution)/shard_map/ppermute | solution.py:284
  8.2 0.0 collective-permute-done.4
  8.2 0.0 collective-permute-done.5
  8.2 7.2 %collective-permute-done.6 = bf16[2,6,32,128]{3,2,1,0:T(8,128)(2,1)S(1)} collective-permute-done((bf16[2,6,32,128]{3,2,1,0:T(8,128)(2,1)S(1)}, bf16[2,6,32,128]{3,2,1,0:T(8,128)(2,1)S(1)}, u32[]{:S(2)}, u32[]{:S(2)}) %collective-permute-start.6) | collective-permute-done | bytes 98336 | tf_op jit(solution)/shard_map/ppermute | solution.py:274
  15.3 2.4 %collective-permute-done.7 = bf16[2,6,32,128]{3,2,1,0:T(8,128)(2,1)S(1)} collective-permute-done((bf16[2,6,32,128]{3,2,1,0:T(8,128)(2,1)S(1)}, bf16[2,6,32,128]{3,2,1,0:T(8,128)(2,1)S(1)}, u32[]{:S(2)}, u32[]{:S(2)}) %collective-permute-start.7) | collective-permute-done | bytes 98336 | tf_op jit(solution)/shard_map/ppermute | solution.py:274
  17.7 0.1 pad_maximum_fusion
  17.8 4.4 %collective-permute-start.8 = (bf16[2,15,32,128]{3,2,1,0:T(8,128)(2,1)S(1)}, bf16[2,15,32,128]{3,2,1,0:T(8,128)(2,1)S(1)}, u32[]{:S(2)}, u32[]{:S(2)}) collective-permute-start(bf16[2,15,32,128]{3,2,1,0:T(8,128)(2,1)S(1)} %pad_maximum_fusion.1), channel_id=1, source_target_pairs={{0,8},{2,10},{4,12},{6,14},{16,24},{18,26},{20,28},{22,30},{32,40}... | collective-permute-start | bytes 737288 | tf_op jit(solution)/shard_map/ppermute | solution.py:280
  22.2 0.0 collective-permute-done
  22.3 3.4 %collective-permute-start.1 = (bf16[2,2,6,32,128]{4,3,2,1,0:T(8,128)(2,1)S(1)}, bf16[2,2,6,32,128]{4,3,2,1,0:T(8,128)(2,1)S(1)}, u32[]{:S(2)}, u32[]{:S(2)}) collective-permute-start(bf16[2,2,6,32,128]{4,3,2,1,0:T(8,128)(2,1)S(1)} %pad_maximum_fusion.3), channel_id=1, source_target_pairs={{0,2},{2,4},{4,6},{6,0},{1,3},{3,5},{5,7},{7,1},{8,10},{10,12},{12... | collective-permute-start | bytes 589832 | tf_op jit(solution)/shard_map/ppermute | solution.py:289
  25.7 3.0 %collective-permute-start.2 = (bf16[2,2,6,32,128]{4,3,2,1,0:T(8,128)(2,1)S(1)}, bf16[2,2,6,32,128]{4,3,2,1,0:T(8,128)(2,1)S(1)}, u32[]{:S(2)}, u32[]{:S(2)}) collective-permute-start(bf16[2,2,6,32,128]{4,3,2,1,0:T(8,128)(2,1)S(1)} %pad_maximum_fusion.4), channel_id=1, source_target_pairs={{0,4},{2,6},{4,0},{6,2},{1,5},{3,7},{5,1},{7,3},{8,12},{10,14},{12... | collective-permute-start | bytes 589832 | tf_op jit(solution)/shard_map/ppermute | solution.py:289
  28.8 0.0 copy-start.1
  28.8 0.0 copy-start
  28.8 4.2 %collective-permute-start.3 = (bf16[2,2,6,32,128]{4,3,2,1,0:T(8,128)(2,1)S(1)}, bf16[2,2,6,32,128]{4,3,2,1,0:T(8,128)(2,1)S(1)}, u32[]{:S(2)}, u32[]{:S(2)}) collective-permute-start(bf16[2,2,6,32,128]{4,3,2,1,0:T(8,128)(2,1)S(1)} %pad_maximum_fusion.5), channel_id=1, source_target_pairs={{0,6},{2,0},{4,2},{6,4},{1,7},{3,1},{5,3},{7,5},{8,14},{10,8},{12,... | collective-permute-start | bytes 589832 | tf_op jit(solution)/shard_map/ppermute | solution.py:289
  33.0 0.0 copy-start.2
  33.0 0.0 copy-start.3
  33.1 0.0 collective-permute-done.1.refs_1_
  33.1 1.8 %collective-permute-done.2.refs_2_ = bf16[2,2,6,32,128]{4,3,2,1,0:T(8,128)(2,1)S(1)} collective-permute-done((bf16[2,2,6,32,128]{4,3,2,1,0:T(8,128)(2,1)S(1)}, bf16[2,2,6,32,128]{4,3,2,1,0:T(8,128)(2,1)S(1)}, u32[]{:S(2)}, u32[]{:S(2)}) %collective-permute-start.2) | collective-permute-done | bytes 196640 | tf_op jit(solution)/shard_map/ppermute | solution.py:289
  34.9 2.1 %collective-permute-done.3.refs_3_ = bf16[2,2,6,32,128]{4,3,2,1,0:T(8,128)(2,1)S(1)} collective-permute-done((bf16[2,2,6,32,128]{4,3,2,1,0:T(8,128)(2,1)S(1)}, bf16[2,2,6,32,128]{4,3,2,1,0:T(8,128)(2,1)S(1)}, u32[]{:S(2)}, u32[]{:S(2)}) %collective-permute-start.3) | collective-permute-done | bytes 196640 | tf_op jit(solution)/shard_map/ppermute | solution.py:289
  36.9 0.0 copy-done.1
  36.9 0.0 copy-done
  36.9 0.0 copy-done.2
  36.9 0.0 copy-done.3
  36.9 2.3 %early.1 = (f32[2,16,32,128]{3,2,1,0:T(8,128)S(1)}, bf16[256,256]{1,0:T(8,128)(2,1)S(1)}) custom-call(s32[1]{0:T(128)} %bitcast.1.core, s32[1]{0:T(128)} %bitcast.2.column, s32[1]{0:T(128)} %bitcast.station, bf16[2,2,6,32,128]{4,3,2,1,0:T(8,128)(2,1)S(1)} %pad_maximum_fusion.2.refs_0_, bf16[2,2,6,32,128]{4,3,2,1,0:T(8,128)(2,1)S(1)} %collective-permute-done.1.refs_1_, ...), custom_call_target="tpu_custom_call" | custom-call | tf_op jit(solution)/shard_map/early/pallas_call | solution.py:135
  39.2 0.0 collective-permute-done.8.hist
  39.2 2.2 %rest.1 = bf16[256,768]{1,0:T(8,128)(2,1)S(1)} custom-call(s32[1]{0:T(128)} %bitcast.1.core, s32[1]{0:T(128)} %bitcast.2.column, s32[1]{0:T(128)} %bitcast.station, f32[2,16,32,128]{3,2,1,0:T(8,128)S(1)} %get-tuple-element.7.sums, bf16[2,15,32,128]{3,2,1,0:T(8,128)(2,1)S(1)} %collective-permute-done.8.hist, bf16[256,256]{1,0:T(8,128)(2,1)S(1)} %get-tuple-element.8.done, ...), custom_call_target="tpu_custom_call" | custom-call | tf_op jit(solution)/shard_map/rest/pallas_call | solution.py:135
  41.4 13.0 %all_to_all.15.x = bf16[8,32,768]{2,1,0:T(8,128)(2,1)S(1)} all-to-all(bf16[8,32,768]{2,1,0:T(8,128)(2,1)S(1)} %bitcast.42), channel_id=1, replica_groups=mesh['stn'=32,'zh'=2,'x'=4,'c'=2] {'x','c'}, dimensions={0} | all-to-all | bytes 786432 | tf_op jit(solution)/shard_map/all_to_all | solution.py:299
  54.4 0.2 regroup.1
  54.5 36.9 %all_to_all.16 = bf16[64,24,128]{2,1,0:T(8,128)(2,1)S(1)} all-to-all(bf16[64,24,128]{2,1,0:T(8,128)(2,1)S(1)} %bitcast.40), channel_id=1, replica_groups=mesh['stn'=32,'zh'=2,'x'=4,'c'=2] {'stn','zh'}, dimensions={0} | all-to-all | bytes 786432 | tf_op jit(solution)/shard_map/all_to_all | solution.py:301
  91.4 1.6 %correlate.1 = f32[32,64,128]{2,1,0:T(8,128)S(1)} custom-call(bf16[32,2,24,128]{3,2,1,0:T(8,128)(2,1)S(1)} %bitcast.41), custom_call_target="tpu_custom_call" | custom-call | tf_op jit(solution)/shard_map/correlate/pallas_call | solution.py:219
  93.0 0.1 convert_element_type.6
  93.1 33.1 %all_to_all.17 = f16[32,64,128]{2,1,0:T(8,128)(2,1)S(1)} all-to-all(f16[32,64,128]{2,1,0:T(8,128)(2,1)S(1)} %convert_element_type.6), channel_id=1, replica_groups=mesh['stn'=32,'zh'=2,'x'=4,'c'=2] {'stn'}, dimensions={0} | all-to-all | bytes 1048576 | tf_op jit(solution)/shard_map/all_to_all | solution.py:303
  126.2 0.1 convert_element_type.7.x
  126.3 1.9 %deliver.1 = f32[2,4,128,256]{3,2,1,0:T(8,128)} custom-call(s32[1]{0:T(128)} %bitcast.station, f32[32,64,128]{2,1,0:T(8,128)S(1)} %convert_element_type.7.x), custom_call_target="tpu_custom_call" | custom-call | tf_op jit(solution)/shard_map/deliver/pallas_call | solution.py:256
  (11 shorter events, 0.3 us)
Async XLA Ops:
  1.5 6.7 %collective-permute-start.4 = (bf16[2,6,32,128]{3,2,1,0:T(8,128)(2,1)S(1)}, bf16[2,6,32,128]{3,2,1,0:T(8,128)(2,1)S(1)}, u32[]{:S(2)}, u32[]{:S(2)}) collective-permute-start(bf16[2,6,32,128]{3,2,1,0:T(8,128)(2,1)S(1)} %get-tuple-element.12), channel_id=1, source_target_pairs={{5,2},{6,4},{7,6},{21,18},{22,20},{23,22},{37,34},{38,36},{39,38},... | collective-permute-start | bytes 294920 | tf_op jit(solution)/shard_map/ppermute | solution.py:274
  2.8 5.4 %collective-permute-start.5 = (bf16[2,6,32,128]{3,2,1,0:T(8,128)(2,1)S(1)}, bf16[2,6,32,128]{3,2,1,0:T(8,128)(2,1)S(1)}, u32[]{:S(2)}, u32[]{:S(2)}) collective-permute-start(bf16[2,6,32,128]{3,2,1,0:T(8,128)(2,1)S(1)} %get-tuple-element.13), channel_id=1, source_target_pairs={{5,4},{6,6},{7,0},{21,20},{22,22},{23,16},{37,36},{38,38},{39,32},... | collective-permute-start | bytes 294920 | tf_op jit(solution)/shard_map/ppermute | solution.py:274
  3.5 11.9 %collective-permute-start.6 = (bf16[2,6,32,128]{3,2,1,0:T(8,128)(2,1)S(1)}, bf16[2,6,32,128]{3,2,1,0:T(8,128)(2,1)S(1)}, u32[]{:S(2)}, u32[]{:S(2)}) collective-permute-start(bf16[2,6,32,128]{3,2,1,0:T(8,128)(2,1)S(1)} %get-tuple-element.14), channel_id=1, source_target_pairs={{5,6},{6,0},{7,2},{21,22},{22,16},{23,18},{37,38},{38,32},{39,34},... | collective-permute-start | bytes 294920 | tf_op jit(solution)/shard_map/ppermute | solution.py:274
  4.8 12.9 %collective-permute-start.7 = (bf16[2,6,32,128]{3,2,1,0:T(8,128)(2,1)S(1)}, bf16[2,6,32,128]{3,2,1,0:T(8,128)(2,1)S(1)}, u32[]{:S(2)}, u32[]{:S(2)}) collective-permute-start(bf16[2,6,32,128]{3,2,1,0:T(8,128)(2,1)S(1)} %get-tuple-element.15), channel_id=1, source_target_pairs={{5,0},{6,2},{7,4},{21,16},{22,18},{23,20},{37,32},{38,34},{39,36},... | collective-permute-start | bytes 294920 | tf_op jit(solution)/shard_map/ppermute | solution.py:274
  6.1 16.1 %collective-permute-start = (bf16[2,4,6,32,128]{4,3,2,0,1:T(8,128)(2,1)S(1)}, bf16[2,4,6,32,128]{4,3,2,0,1:T(8,128)(2,1)S(1)}, u32[]{:S(2)}, u32[]{:S(2)}) collective-permute-start(bf16[2,4,6,32,128]{4,3,2,0,1:T(8,128)(2,1)S(1)} %copy.6), channel_id=1, source_target_pairs={{0,1},{1,0},{2,3},{3,2},{4,5},{5,4},{6,7},{7,6},{8,9},{9,8},{10,11... | collective-permute-start | bytes 1179656 | tf_op jit(solution)/shard_map/ppermute | solution.py:284
  17.8 21.4 %collective-permute-start.8 = (bf16[2,15,32,128]{3,2,1,0:T(8,128)(2,1)S(1)}, bf16[2,15,32,128]{3,2,1,0:T(8,128)(2,1)S(1)}, u32[]{:S(2)}, u32[]{:S(2)}) collective-permute-start(bf16[2,15,32,128]{3,2,1,0:T(8,128)(2,1)S(1)} %pad_maximum_fusion.1), channel_id=1, source_target_pairs={{0,8},{2,10},{4,12},{6,14},{16,24},{18,26},{20,28},{22,30},{32,40}... | collective-permute-start | bytes 737288 | tf_op jit(solution)/shard_map/ppermute | solution.py:280
  22.3 10.8 %collective-permute-start.1 = (bf16[2,2,6,32,128]{4,3,2,1,0:T(8,128)(2,1)S(1)}, bf16[2,2,6,32,128]{4,3,2,1,0:T(8,128)(2,1)S(1)}, u32[]{:S(2)}, u32[]{:S(2)}) collective-permute-start(bf16[2,2,6,32,128]{4,3,2,1,0:T(8,128)(2,1)S(1)} %pad_maximum_fusion.3), channel_id=1, source_target_pairs={{0,2},{2,4},{4,6},{6,0},{1,3},{3,5},{5,7},{7,1},{8,10},{10,12},{12... | collective-permute-start | bytes 589832 | tf_op jit(solution)/shard_map/ppermute | solution.py:289
  25.7 9.1 %collective-permute-start.2 = (bf16[2,2,6,32,128]{4,3,2,1,0:T(8,128)(2,1)S(1)}, bf16[2,2,6,32,128]{4,3,2,1,0:T(8,128)(2,1)S(1)}, u32[]{:S(2)}, u32[]{:S(2)}) collective-permute-start(bf16[2,2,6,32,128]{4,3,2,1,0:T(8,128)(2,1)S(1)} %pad_maximum_fusion.4), channel_id=1, source_target_pairs={{0,4},{2,6},{4,0},{6,2},{1,5},{3,7},{5,1},{7,3},{8,12},{10,14},{12... | collective-permute-start | bytes 589832 | tf_op jit(solution)/shard_map/ppermute | solution.py:289
  28.8 8.1 %copy-start.1 = (f32[16,32,128]{2,1,0:T(8,128)S(1)}, f32[16,32,128]{2,1,0:T(8,128)}, u32[]{:S(2)}) copy-start(f32[16,32,128]{2,1,0:T(8,128)} %constant.123.clone.refs_4_.taps) | copy-start | bytes 786436
  28.8 8.1 %copy-start = (bf16[512,256]{1,0:T(8,128)(2,1)S(1)}, bf16[512,256]{1,0:T(8,128)(2,1)}, u32[]{:S(2)}) copy-start(bf16[512,256]{1,0:T(8,128)(2,1)} %constant.125.clone.refs_6_.second) | copy-start | bytes 786436
  28.8 8.1 %collective-permute-start.3 = (bf16[2,2,6,32,128]{4,3,2,1,0:T(8,128)(2,1)S(1)}, bf16[2,2,6,32,128]{4,3,2,1,0:T(8,128)(2,1)S(1)}, u32[]{:S(2)}, u32[]{:S(2)}) collective-permute-start(bf16[2,2,6,32,128]{4,3,2,1,0:T(8,128)(2,1)S(1)} %pad_maximum_fusion.5), channel_id=1, source_target_pairs={{0,6},{2,0},{4,2},{6,4},{1,7},{3,1},{5,3},{7,5},{8,14},{10,8},{12,... | collective-permute-start | bytes 589832 | tf_op jit(solution)/shard_map/ppermute | solution.py:289
  33.0 3.9 %copy-start.2 = (f32[2,32,128]{2,1,0:T(8,128)S(1)}, f32[2,32,128]{2,1,0:T(8,128)}, u32[]{:S(2)}) copy-start(f32[2,32,128]{2,1,0:T(8,128)} %constant.126.clone.refs_7_.twiddle) | copy-start | bytes 98308
  33.0 3.9 %copy-start.3 = (bf16[128,64]{1,0:T(8,128)(2,1)S(1)}, bf16[128,64]{1,0:T(8,128)(2,1)}, u32[]{:S(2)}) copy-start(bf16[128,64]{1,0:T(8,128)(2,1)} %constant.124.clone.refs_5_.first) | copy-start | bytes 49156

commit v10 on v9

--- a/solution.py
+++ b/solution.py
@@ -19,6 +19,7 @@
 HIST = TAPS - 1
 LATE = 8
 FEW = BLOCK - LATE
+ORDER = (0, 2, 1, 3)
 SENT = 6
 PER = 4
 PARAMS = pltpu.CompilerParams(vmem_limit_bytes=48 * 1024 * 1024)
@@ -88,9 +89,10 @@
     start = BLOCK * core[0]
     for r in range(2):
         frames[r, :HIST] = jnp.zeros((HIST, N1, N2), F32)
-        for p in range(Q):
-            shard = Q // X * ((column[0] + X - p // 2) % X) + (core[0] + p) % 2
-            frames[r, pl.ds(HIST + SENT * shard, SENT)] = pieces[p // 2][p % 2, r].astype(F32)
+        for piece, p in zip(pieces, ORDER):
+            for d in range(2):
+                shard = Q // X * ((column[0] + X - p) % X) + (core[0] + d) % 2
+                frames[r, pl.ds(HIST + SENT * shard, SENT)] = piece[d, r].astype(F32)
 
     def filtered(r, f):
         acc = taps[0] * frames[r, start + f]
@@ -283,10 +285,11 @@
 def half_of_input(frames):
     other = lax.ppermute(frames, "c", [(0, 1), (1, 0)])
     pieces = []
-    for p in range(X):
+    for p in ORDER:
         i = (lax.axis_index("x") + p) % X
         piece = jnp.stack([lax.dynamic_index_in_dim(a, i, 1, False) for a in (frames, other)])
-        pieces.append(lax.ppermute(piece, "x", [(x, (x + p) % X) for x in range(X)]) if p else piece)
+        pairs = [(2 * x + c, 2 * ((x + p) % X) + c) for x in range(X) for c in range(2) if c or x < X // 2]
+        pieces.append(lax.ppermute(piece, ("x", "c"), pairs) if p else piece)
     return pieces
 
 

time: 129 us -> 128 us (level)
    all_to_all x1, blocking collectives: 36.9 us -> 38.5 us  [shards(): spectra = lax.all_to_all(spectra, ('stn', 'zh'), 0, 0, tiled=True)]
where the time goes in v10:
time: 128 us
  blocking collectives  84 us (66%)
  starting transfers between devices  20.9 us (16%)
  waiting for transfers between devices  12.6 us (10%)
  Pallas kernels  8.05 us (6%)
  local copies, waits for them, and re-layouts  1.61 us (1%)
    all_to_all x1, blocking collectives, shards(): spectra = lax.all_to_all(spectra, ('stn', 'zh'), 0, 0, tiled=True)  38.5 us
    all_to_all x1, blocking collectives, shards(): lax.all_to_all(products.astype(jnp.float16), 'stn', 0, 0, tiled=True)  33.1 us
    all_to_all x1, blocking collectives, shards(): lax.all_to_all(spectra.reshape(Q, 2 * N2 // Q, N1 * BLOCK), ('x', 'c'), 0...  12.4 us
    ppermute x3, starting transfers between devices, half_of_input(): pieces.append(lax.ppermute(piece, ('x', 'c'), pairs) if p else piece)  10 us
    ppermute x4, waiting for transfers between devices, last_frames(): rounds.append(lax.ppermute(piece, ('zh', 'x', 'c'), pairs))  9.51 us
    ppermute x4, starting transfers between devices, last_frames(): rounds.append(lax.ppermute(piece, ('zh', 'x', 'c'), pairs))  4.54 us
    pallas_call x2, Pallas kernels, kernel(): pl.pallas_call(body, out_shape=out_shape, in_specs=[pl.BlockSpec(memory_s...  4.41 us
    ppermute x1, starting transfers between devices, last_frames(): lax.ppermute(last, ('zh', 'x', 'c'), [(Q // X * x, Q + Q // X * x) for x...  4.38 us
  transfers between devices with their start and end apart: 9, of which 4 were waited for; matrix products, arithmetic and copies ran while one was open for 0% of the time, Pallas kernels for 2%

profile of v10, /device:TPU:2, one launch (start us, length us, event | category | flops | bytes accessed | tf_op | source)
XLA Modules:
  0.0 127.9 jit_solution(9028894238827732656)
XLA Ops:
  0.0 1.4 %reshape.32 = bf16[2,4,6,32,128]{4,3,2,1,0:T(8,128)(2,1)S(1)} reshape(bf16[2,4,24576]{2,1,0:T(4,128)(2,1)} %param.5) | data formatting | bytes 786432 | tf_op jit(solution)/shard_map/reshape | solution.py:297
  1.5 1.3 %collective-permute-start.4 = (bf16[2,6,32,128]{3,2,1,0:T(8,128)(2,1)S(1)}, bf16[2,6,32,128]{3,2,1,0:T(8,128)(2,1)S(1)}, u32[]{:S(2)}, u32[]{:S(2)}) collective-permute-start(bf16[2,6,32,128]{3,2,1,0:T(8,128)(2,1)S(1)} %get-tuple-element.12), channel_id=1, source_target_pairs={{5,2},{6,4},{7,6},{21,18},{22,20},{23,22},{37,34},{38,36},{39,38},... | collective-permute-start | bytes 294920 | tf_op jit(solution)/shard_map/ppermute | solution.py:276
  2.8 0.7 collective-permute-start.5
  3.5 1.3 %collective-permute-start.6 = (bf16[2,6,32,128]{3,2,1,0:T(8,128)(2,1)S(1)}, bf16[2,6,32,128]{3,2,1,0:T(8,128)(2,1)S(1)}, u32[]{:S(2)}, u32[]{:S(2)}) collective-permute-start(bf16[2,6,32,128]{3,2,1,0:T(8,128)(2,1)S(1)} %get-tuple-element.14), channel_id=1, source_target_pairs={{5,6},{6,0},{7,2},{21,22},{22,16},{23,18},{37,38},{38,32},{39,34},... | collective-permute-start | bytes 294920 | tf_op jit(solution)/shard_map/ppermute | solution.py:276
  4.8 1.3 %collective-permute-start.7 = (bf16[2,6,32,128]{3,2,1,0:T(8,128)(2,1)S(1)}, bf16[2,6,32,128]{3,2,1,0:T(8,128)(2,1)S(1)}, u32[]{:S(2)}, u32[]{:S(2)}) collective-permute-start(bf16[2,6,32,128]{3,2,1,0:T(8,128)(2,1)S(1)} %get-tuple-element.15), channel_id=1, source_target_pairs={{5,0},{6,2},{7,4},{21,16},{22,18},{23,20},{37,32},{38,34},{39,36},... | collective-permute-start | bytes 294920 | tf_op jit(solution)/shard_map/ppermute | solution.py:276
  6.1 1.9 %collective-permute-start = (bf16[2,4,6,32,128]{4,3,2,0,1:T(8,128)(2,1)S(1)}, bf16[2,4,6,32,128]{4,3,2,0,1:T(8,128)(2,1)S(1)}, u32[]{:S(2)}, u32[]{:S(2)}) collective-permute-start(bf16[2,4,6,32,128]{4,3,2,0,1:T(8,128)(2,1)S(1)} %copy.6), channel_id=1, source_target_pairs={{0,1},{1,0},{2,3},{3,2},{4,5},{5,4},{6,7},{7,6},{8,9},{9,8},{10,11... | collective-permute-start | bytes 1179656 | tf_op jit(solution)/shard_map/ppermute | solution.py:286
  8.2 0.0 collective-permute-done.4
  8.2 0.0 collective-permute-done.5
  8.2 7.2 %collective-permute-done.6 = bf16[2,6,32,128]{3,2,1,0:T(8,128)(2,1)S(1)} collective-permute-done((bf16[2,6,32,128]{3,2,1,0:T(8,128)(2,1)S(1)}, bf16[2,6,32,128]{3,2,1,0:T(8,128)(2,1)S(1)}, u32[]{:S(2)}, u32[]{:S(2)}) %collective-permute-start.6) | collective-permute-done | bytes 98336 | tf_op jit(solution)/shard_map/ppermute | solution.py:276
  15.3 2.4 %collective-permute-done.7 = bf16[2,6,32,128]{3,2,1,0:T(8,128)(2,1)S(1)} collective-permute-done((bf16[2,6,32,128]{3,2,1,0:T(8,128)(2,1)S(1)}, bf16[2,6,32,128]{3,2,1,0:T(8,128)(2,1)S(1)}, u32[]{:S(2)}, u32[]{:S(2)}) %collective-permute-start.7) | collective-permute-done | bytes 98336 | tf_op jit(solution)/shard_map/ppermute | solution.py:276
  17.7 0.1 pad_maximum_fusion
  17.8 4.4 %collective-permute-start.8 = (bf16[2,15,32,128]{3,2,1,0:T(8,128)(2,1)S(1)}, bf16[2,15,32,128]{3,2,1,0:T(8,128)(2,1)S(1)}, u32[]{:S(2)}, u32[]{:S(2)}) collective-permute-start(bf16[2,15,32,128]{3,2,1,0:T(8,128)(2,1)S(1)} %pad_maximum_fusion.1), channel_id=1, source_target_pairs={{0,8},{2,10},{4,12},{6,14},{16,24},{18,26},{20,28},{22,30},{32,40}... | collective-permute-start | bytes 737288 | tf_op jit(solution)/shard_map/ppermute | solution.py:282
  22.2 0.0 collective-permute-done
  22.3 4.0 %collective-permute-start.1 = (bf16[2,2,6,32,128]{4,3,2,1,0:T(8,128)(2,1)S(1)}, bf16[2,2,6,32,128]{4,3,2,1,0:T(8,128)(2,1)S(1)}, u32[]{:S(2)}, u32[]{:S(2)}) collective-permute-start(bf16[2,2,6,32,128]{4,3,2,1,0:T(8,128)(2,1)S(1)} %pad_maximum_fusion.3), channel_id=1, source_target_pairs={{0,4},{1,5},{2,6},{3,7},{5,1},{7,3},{8,12},{9,13},{10,14},{11,15},... | collective-permute-start | bytes 589832 | tf_op jit(solution)/shard_map/ppermute | solution.py:292
  26.4 1.9 %collective-permute-start.2 = (bf16[2,2,6,32,128]{4,3,2,1,0:T(8,128)(2,1)S(1)}, bf16[2,2,6,32,128]{4,3,2,1,0:T(8,128)(2,1)S(1)}, u32[]{:S(2)}, u32[]{:S(2)}) collective-permute-start(bf16[2,2,6,32,128]{4,3,2,1,0:T(8,128)(2,1)S(1)} %pad_maximum_fusion.4), channel_id=1, source_target_pairs={{0,2},{1,3},{2,4},{3,5},{5,7},{7,1},{8,10},{9,11},{10,12},{11,13},... | collective-permute-start | bytes 589832 | tf_op jit(solution)/shard_map/ppermute | solution.py:292
  28.3 0.0 copy-start.1
  28.4 0.0 copy-start
  28.4 4.1 %collective-permute-start.3 = (bf16[2,2,6,32,128]{4,3,2,1,0:T(8,128)(2,1)S(1)}, bf16[2,2,6,32,128]{4,3,2,1,0:T(8,128)(2,1)S(1)}, u32[]{:S(2)}, u32[]{:S(2)}) collective-permute-start(bf16[2,2,6,32,128]{4,3,2,1,0:T(8,128)(2,1)S(1)} %pad_maximum_fusion.5), channel_id=1, source_target_pairs={{0,6},{1,7},{2,0},{3,1},{5,3},{7,5},{8,14},{9,15},{10,8},{11,9},{1... | collective-permute-start | bytes 589832 | tf_op jit(solution)/shard_map/ppermute | solution.py:292
  32.5 0.0 copy-start.2
  32.5 0.0 copy-start.3
  32.5 0.0 collective-permute-done.1.refs_1_
  32.5 1.4 %collective-permute-done.2.refs_2_ = bf16[2,2,6,32,128]{4,3,2,1,0:T(8,128)(2,1)S(1)} collective-permute-done((bf16[2,2,6,32,128]{4,3,2,1,0:T(8,128)(2,1)S(1)}, bf16[2,2,6,32,128]{4,3,2,1,0:T(8,128)(2,1)S(1)}, u32[]{:S(2)}, u32[]{:S(2)}) %collective-permute-start.2) | collective-permute-done | bytes 196640 | tf_op jit(solution)/shard_map/ppermute | solution.py:292
  34.0 1.7 %collective-permute-done.3.refs_3_ = bf16[2,2,6,32,128]{4,3,2,1,0:T(8,128)(2,1)S(1)} collective-permute-done((bf16[2,2,6,32,128]{4,3,2,1,0:T(8,128)(2,1)S(1)}, bf16[2,2,6,32,128]{4,3,2,1,0:T(8,128)(2,1)S(1)}, u32[]{:S(2)}, u32[]{:S(2)}) %collective-permute-start.3) | collective-permute-done | bytes 196640 | tf_op jit(solution)/shard_map/ppermute | solution.py:292
  35.6 0.0 copy-done.1
  35.6 0.0 copy-done
  35.6 0.0 copy-done.2
  35.6 0.0 copy-done.3
  35.6 2.3 %early.1 = (f32[2,16,32,128]{3,2,1,0:T(8,128)S(1)}, bf16[256,256]{1,0:T(8,128)(2,1)S(1)}) custom-call(s32[1]{0:T(128)} %bitcast.1.core, s32[1]{0:T(128)} %bitcast.2.column, s32[1]{0:T(128)} %bitcast.station, bf16[2,2,6,32,128]{4,3,2,1,0:T(8,128)(2,1)S(1)} %pad_maximum_fusion.2.refs_0_, bf16[2,2,6,32,128]{4,3,2,1,0:T(8,128)(2,1)S(1)} %collective-permute-done.1.refs_1_, ...), custom_call_target="tpu_custom_call" | custom-call | tf_op jit(solution)/shard_map/early/pallas_call | solution.py:137
  37.9 0.0 collective-permute-done.8.hist
  37.9 2.2 %rest.1 = bf16[256,768]{1,0:T(8,128)(2,1)S(1)} custom-call(s32[1]{0:T(128)} %bitcast.1.core, s32[1]{0:T(128)} %bitcast.2.column, s32[1]{0:T(128)} %bitcast.station, f32[2,16,32,128]{3,2,1,0:T(8,128)S(1)} %get-tuple-element.7.sums, bf16[2,15,32,128]{3,2,1,0:T(8,128)(2,1)S(1)} %collective-permute-done.8.hist, bf16[256,256]{1,0:T(8,128)(2,1)S(1)} %get-tuple-element.8.done, ...), custom_call_target="tpu_custom_call" | custom-call | tf_op jit(solution)/shard_map/rest/pallas_call | solution.py:137
  40.1 12.4 %all_to_all.15.x = bf16[8,32,768]{2,1,0:T(8,128)(2,1)S(1)} all-to-all(bf16[8,32,768]{2,1,0:T(8,128)(2,1)S(1)} %bitcast.42), channel_id=1, replica_groups=mesh['stn'=32,'zh'=2,'x'=4,'c'=2] {'x','c'}, dimensions={0} | all-to-all | bytes 786432 | tf_op jit(solution)/shard_map/all_to_all | solution.py:302
  52.4 0.2 regroup.1
  52.6 38.5 %all_to_all.16 = bf16[64,24,128]{2,1,0:T(8,128)(2,1)S(1)} all-to-all(bf16[64,24,128]{2,1,0:T(8,128)(2,1)S(1)} %bitcast.40), channel_id=1, replica_groups=mesh['stn'=32,'zh'=2,'x'=4,'c'=2] {'stn','zh'}, dimensions={0} | all-to-all | bytes 786432 | tf_op jit(solution)/shard_map/all_to_all | solution.py:304
  91.1 1.6 %correlate.1 = f32[32,64,128]{2,1,0:T(8,128)S(1)} custom-call(bf16[32,2,24,128]{3,2,1,0:T(8,128)(2,1)S(1)} %bitcast.41), custom_call_target="tpu_custom_call" | custom-call | tf_op jit(solution)/shard_map/correlate/pallas_call | solution.py:221
  92.7 0.1 convert_element_type.6
  92.8 33.1 %all_to_all.17 = f16[32,64,128]{2,1,0:T(8,128)(2,1)S(1)} all-to-all(f16[32,64,128]{2,1,0:T(8,128)(2,1)S(1)} %convert_element_type.6), channel_id=1, replica_groups=mesh['stn'=32,'zh'=2,'x'=4,'c'=2] {'stn'}, dimensions={0} | all-to-all | bytes 1048576 | tf_op jit(solution)/shard_map/all_to_all | solution.py:306
  125.9 0.1 convert_element_type.7.x
  126.0 1.9 %deliver.1 = f32[2,4,128,256]{3,2,1,0:T(8,128)} custom-call(s32[1]{0:T(128)} %bitcast.station, f32[32,64,128]{2,1,0:T(8,128)S(1)} %convert_element_type.7.x), custom_call_target="tpu_custom_call" | custom-call | tf_op jit(solution)/shard_map/deliver/pallas_call | solution.py:258
  (11 shorter events, 0.3 us)
Async XLA Ops:
  1.5 6.7 %collective-permute-start.4 = (bf16[2,6,32,128]{3,2,1,0:T(8,128)(2,1)S(1)}, bf16[2,6,32,128]{3,2,1,0:T(8,128)(2,1)S(1)}, u32[]{:S(2)}, u32[]{:S(2)}) collective-permute-start(bf16[2,6,32,128]{3,2,1,0:T(8,128)(2,1)S(1)} %get-tuple-element.12), channel_id=1, source_target_pairs={{5,2},{6,4},{7,6},{21,18},{22,20},{23,22},{37,34},{38,36},{39,38},... | collective-permute-start | bytes 294920 | tf_op jit(solution)/shard_map/ppermute | solution.py:276
  2.8 5.4 %collective-permute-start.5 = (bf16[2,6,32,128]{3,2,1,0:T(8,128)(2,1)S(1)}, bf16[2,6,32,128]{3,2,1,0:T(8,128)(2,1)S(1)}, u32[]{:S(2)}, u32[]{:S(2)}) collective-permute-start(bf16[2,6,32,128]{3,2,1,0:T(8,128)(2,1)S(1)} %get-tuple-element.13), channel_id=1, source_target_pairs={{5,4},{6,6},{7,0},{21,20},{22,22},{23,16},{37,36},{38,38},{39,32},... | collective-permute-start | bytes 294920 | tf_op jit(solution)/shard_map/ppermute | solution.py:276
  3.5 11.9 %collective-permute-start.6 = (bf16[2,6,32,128]{3,2,1,0:T(8,128)(2,1)S(1)}, bf16[2,6,32,128]{3,2,1,0:T(8,128)(2,1)S(1)}, u32[]{:S(2)}, u32[]{:S(2)}) collective-permute-start(bf16[2,6,32,128]{3,2,1,0:T(8,128)(2,1)S(1)} %get-tuple-element.14), channel_id=1, source_target_pairs={{5,6},{6,0},{7,2},{21,22},{22,16},{23,18},{37,38},{38,32},{39,34},... | collective-permute-start | bytes 294920 | tf_op jit(solution)/shard_map/ppermute | solution.py:276
  4.8 12.9 %collective-permute-start.7 = (bf16[2,6,32,128]{3,2,1,0:T(8,128)(2,1)S(1)}, bf16[2,6,32,128]{3,2,1,0:T(8,128)(2,1)S(1)}, u32[]{:S(2)}, u32[]{:S(2)}) collective-permute-start(bf16[2,6,32,128]{3,2,1,0:T(8,128)(2,1)S(1)} %get-tuple-element.15), channel_id=1, source_target_pairs={{5,0},{6,2},{7,4},{21,16},{22,18},{23,20},{37,32},{38,34},{39,36},... | collective-permute-start | bytes 294920 | tf_op jit(solution)/shard_map/ppermute | solution.py:276
  6.1 16.1 %collective-permute-start = (bf16[2,4,6,32,128]{4,3,2,0,1:T(8,128)(2,1)S(1)}, bf16[2,4,6,32,128]{4,3,2,0,1:T(8,128)(2,1)S(1)}, u32[]{:S(2)}, u32[]{:S(2)}) collective-permute-start(bf16[2,4,6,32,128]{4,3,2,0,1:T(8,128)(2,1)S(1)} %copy.6), channel_id=1, source_target_pairs={{0,1},{1,0},{2,3},{3,2},{4,5},{5,4},{6,7},{7,6},{8,9},{9,8},{10,11... | collective-permute-start | bytes 1179656 | tf_op jit(solution)/shard_map/ppermute | solution.py:286
  17.8 20.0 %collective-permute-start.8 = (bf16[2,15,32,128]{3,2,1,0:T(8,128)(2,1)S(1)}, bf16[2,15,32,128]{3,2,1,0:T(8,128)(2,1)S(1)}, u32[]{:S(2)}, u32[]{:S(2)}) collective-permute-start(bf16[2,15,32,128]{3,2,1,0:T(8,128)(2,1)S(1)} %pad_maximum_fusion.1), channel_id=1, source_target_pairs={{0,8},{2,10},{4,12},{6,14},{16,24},{18,26},{20,28},{22,30},{32,40}... | collective-permute-start | bytes 737288 | tf_op jit(solution)/shard_map/ppermute | solution.py:282
  22.3 10.2 %collective-permute-start.1 = (bf16[2,2,6,32,128]{4,3,2,1,0:T(8,128)(2,1)S(1)}, bf16[2,2,6,32,128]{4,3,2,1,0:T(8,128)(2,1)S(1)}, u32[]{:S(2)}, u32[]{:S(2)}) collective-permute-start(bf16[2,2,6,32,128]{4,3,2,1,0:T(8,128)(2,1)S(1)} %pad_maximum_fusion.3), channel_id=1, source_target_pairs={{0,4},{1,5},{2,6},{3,7},{5,1},{7,3},{8,12},{9,13},{10,14},{11,15},... | collective-permute-start | bytes 589832 | tf_op jit(solution)/shard_map/ppermute | solution.py:292
  26.4 7.6 %collective-permute-start.2 = (bf16[2,2,6,32,128]{4,3,2,1,0:T(8,128)(2,1)S(1)}, bf16[2,2,6,32,128]{4,3,2,1,0:T(8,128)(2,1)S(1)}, u32[]{:S(2)}, u32[]{:S(2)}) collective-permute-start(bf16[2,2,6,32,128]{4,3,2,1,0:T(8,128)(2,1)S(1)} %pad_maximum_fusion.4), channel_id=1, source_target_pairs={{0,2},{1,3},{2,4},{3,5},{5,7},{7,1},{8,10},{9,11},{10,12},{11,13},... | collective-permute-start | bytes 589832 | tf_op jit(solution)/shard_map/ppermute | solution.py:292
  28.3 7.3 %copy-start.1 = (f32[16,32,128]{2,1,0:T(8,128)S(1)}, f32[16,32,128]{2,1,0:T(8,128)}, u32[]{:S(2)}) copy-start(f32[16,32,128]{2,1,0:T(8,128)} %constant.123.clone.refs_4_.taps) | copy-start | bytes 786436
  28.4 7.3 %copy-start = (bf16[512,256]{1,0:T(8,128)(2,1)S(1)}, bf16[512,256]{1,0:T(8,128)(2,1)}, u32[]{:S(2)}) copy-start(bf16[512,256]{1,0:T(8,128)(2,1)} %constant.125.clone.refs_6_.second) | copy-start | bytes 786436
  28.4 7.2 %collective-permute-start.3 = (bf16[2,2,6,32,128]{4,3,2,1,0:T(8,128)(2,1)S(1)}, bf16[2,2,6,32,128]{4,3,2,1,0:T(8,128)(2,1)S(1)}, u32[]{:S(2)}, u32[]{:S(2)}) collective-permute-start(bf16[2,2,6,32,128]{4,3,2,1,0:T(8,128)(2,1)S(1)} %pad_maximum_fusion.5), channel_id=1, source_target_pairs={{0,6},{1,7},{2,0},{3,1},{5,3},{7,5},{8,14},{9,15},{10,8},{11,9},{1... | collective-permute-start | bytes 589832 | tf_op jit(solution)/shard_map/ppermute | solution.py:292
  32.5 3.2 %copy-start.2 = (f32[2,32,128]{2,1,0:T(8,128)S(1)}, f32[2,32,128]{2,1,0:T(8,128)}, u32[]{:S(2)}) copy-start(f32[2,32,128]{2,1,0:T(8,128)} %constant.126.clone.refs_7_.twiddle) | copy-start | bytes 98308
  32.5 3.2 %copy-start.3 = (bf16[128,64]{1,0:T(8,128)(2,1)S(1)}, bf16[128,64]{1,0:T(8,128)(2,1)}, u32[]{:S(2)}) copy-start(bf16[128,64]{1,0:T(8,128)(2,1)} %constant.124.clone.refs_5_.first) | copy-start | bytes 49156

commit v11 on v10

--- a/solution.py
+++ b/solution.py
@@ -283,7 +283,8 @@
 
 
 def half_of_input(frames):
-    other = lax.ppermute(frames, "c", [(0, 1), (1, 0)])
+    swap = [(2 * x + c, 2 * x + 1 - c) for x in range(X) for c in range(2) if not c or x < X // 2]
+    other = lax.ppermute(frames, ("x", "c"), swap)
     pieces = []
     for p in ORDER:
         i = (lax.axis_index("x") + p) % X

time: 128 us -> 128 us (level)
  no operation moved by 1% of the time
where the time goes in v11:
time: 128 us
  blocking collectives  84 us (66%)
  starting transfers between devices  20.7 us (16%)
  waiting for transfers between devices  12.6 us (10%)
  Pallas kernels  8.05 us (6%)
  local copies, waits for them, and re-layouts  1.61 us (1%)
    all_to_all x1, blocking collectives, shards(): spectra = lax.all_to_all(spectra, ('stn', 'zh'), 0, 0, tiled=True)  38.5 us
    all_to_all x1, blocking collectives, shards(): lax.all_to_all(products.astype(jnp.float16), 'stn', 0, 0, tiled=True)  33.1 us
    all_to_all x1, blocking collectives, shards(): lax.all_to_all(spectra.reshape(Q, 2 * N2 // Q, N1 * BLOCK), ('x', 'c'), 0...  12.4 us
    ppermute x3, starting transfers between devices, half_of_input(): pieces.append(lax.ppermute(piece, ('x', 'c'), pairs) if p else piece)  9.87 us
    ppermute x4, waiting for transfers between devices, last_frames(): rounds.append(lax.ppermute(piece, ('zh', 'x', 'c'), pairs))  9.51 us
    ppermute x4, starting transfers between devices, last_frames(): rounds.append(lax.ppermute(piece, ('zh', 'x', 'c'), pairs))  4.54 us
    pallas_call x2, Pallas kernels, kernel(): pl.pallas_call(body, out_shape=out_shape, in_specs=[pl.BlockSpec(memory_s...  4.41 us
    ppermute x1, starting transfers between devices, last_frames(): lax.ppermute(last, ('zh', 'x', 'c'), [(Q // X * x, Q + Q // X * x) for x...  4.38 us
  transfers between devices with their start and end apart: 9, of which 4 were waited for; matrix products, arithmetic and copies ran while one was open for 0% of the time, Pallas kernels for 2%

profile of v11, /device:TPU:2, one launch (start us, length us, event | category | flops | bytes accessed | tf_op | source)
XLA Modules:
  0.0 127.7 jit_solution(9466548322694633995)
XLA Ops:
  0.0 1.4 %reshape.32 = bf16[2,4,6,32,128]{4,3,2,1,0:T(8,128)(2,1)S(1)} reshape(bf16[2,4,24576]{2,1,0:T(4,128)(2,1)} %param.5) | data formatting | bytes 786432 | tf_op jit(solution)/shard_map/reshape | solution.py:298
  1.5 1.3 %collective-permute-start.4 = (bf16[2,6,32,128]{3,2,1,0:T(8,128)(2,1)S(1)}, bf16[2,6,32,128]{3,2,1,0:T(8,128)(2,1)S(1)}, u32[]{:S(2)}, u32[]{:S(2)}) collective-permute-start(bf16[2,6,32,128]{3,2,1,0:T(8,128)(2,1)S(1)} %get-tuple-element.12), channel_id=1, source_target_pairs={{5,2},{6,4},{7,6},{21,18},{22,20},{23,22},{37,34},{38,36},{39,38},... | collective-permute-start | bytes 294920 | tf_op jit(solution)/shard_map/ppermute | solution.py:276
  2.8 0.7 collective-permute-start.5
  3.5 1.3 %collective-permute-start.6 = (bf16[2,6,32,128]{3,2,1,0:T(8,128)(2,1)S(1)}, bf16[2,6,32,128]{3,2,1,0:T(8,128)(2,1)S(1)}, u32[]{:S(2)}, u32[]{:S(2)}) collective-permute-start(bf16[2,6,32,128]{3,2,1,0:T(8,128)(2,1)S(1)} %get-tuple-element.14), channel_id=1, source_target_pairs={{5,6},{6,0},{7,2},{21,22},{22,16},{23,18},{37,38},{38,32},{39,34},... | collective-permute-start | bytes 294920 | tf_op jit(solution)/shard_map/ppermute | solution.py:276
  4.8 1.3 %collective-permute-start.7 = (bf16[2,6,32,128]{3,2,1,0:T(8,128)(2,1)S(1)}, bf16[2,6,32,128]{3,2,1,0:T(8,128)(2,1)S(1)}, u32[]{:S(2)}, u32[]{:S(2)}) collective-permute-start(bf16[2,6,32,128]{3,2,1,0:T(8,128)(2,1)S(1)} %get-tuple-element.15), channel_id=1, source_target_pairs={{5,0},{6,2},{7,4},{21,16},{22,18},{23,20},{37,32},{38,34},{39,36},... | collective-permute-start | bytes 294920 | tf_op jit(solution)/shard_map/ppermute | solution.py:276
  6.1 1.9 %collective-permute-start = (bf16[2,4,6,32,128]{4,3,2,0,1:T(8,128)(2,1)S(1)}, bf16[2,4,6,32,128]{4,3,2,0,1:T(8,128)(2,1)S(1)}, u32[]{:S(2)}, u32[]{:S(2)}) collective-permute-start(bf16[2,4,6,32,128]{4,3,2,0,1:T(8,128)(2,1)S(1)} %copy.6), channel_id=1, source_target_pairs={{0,1},{1,0},{2,3},{3,2},{4,5},{6,7},{8,9},{9,8},{10,11},{11,10},{1... | collective-permute-start | bytes 1179656 | tf_op jit(solution)/shard_map/ppermute | solution.py:287
  8.2 0.0 collective-permute-done.4
  8.2 0.0 collective-permute-done.5
  8.2 7.2 %collective-permute-done.6 = bf16[2,6,32,128]{3,2,1,0:T(8,128)(2,1)S(1)} collective-permute-done((bf16[2,6,32,128]{3,2,1,0:T(8,128)(2,1)S(1)}, bf16[2,6,32,128]{3,2,1,0:T(8,128)(2,1)S(1)}, u32[]{:S(2)}, u32[]{:S(2)}) %collective-permute-start.6) | collective-permute-done | bytes 98336 | tf_op jit(solution)/shard_map/ppermute | solution.py:276
  15.3 2.4 %collective-permute-done.7 = bf16[2,6,32,128]{3,2,1,0:T(8,128)(2,1)S(1)} collective-permute-done((bf16[2,6,32,128]{3,2,1,0:T(8,128)(2,1)S(1)}, bf16[2,6,32,128]{3,2,1,0:T(8,128)(2,1)S(1)}, u32[]{:S(2)}, u32[]{:S(2)}) %collective-permute-start.7) | collective-permute-done | bytes 98336 | tf_op jit(solution)/shard_map/ppermute | solution.py:276
  17.7 0.1 pad_maximum_fusion
  17.8 4.4 %collective-permute-start.8 = (bf16[2,15,32,128]{3,2,1,0:T(8,128)(2,1)S(1)}, bf16[2,15,32,128]{3,2,1,0:T(8,128)(2,1)S(1)}, u32[]{:S(2)}, u32[]{:S(2)}) collective-permute-start(bf16[2,15,32,128]{3,2,1,0:T(8,128)(2,1)S(1)} %pad_maximum_fusion.1), channel_id=1, source_target_pairs={{0,8},{2,10},{4,12},{6,14},{16,24},{18,26},{20,28},{22,30},{32,40}... | collective-permute-start | bytes 737288 | tf_op jit(solution)/shard_map/ppermute | solution.py:282
  22.2 0.0 collective-permute-done
  22.3 3.9 %collective-permute-start.1 = (bf16[2,2,6,32,128]{4,3,2,1,0:T(8,128)(2,1)S(1)}, bf16[2,2,6,32,128]{4,3,2,1,0:T(8,128)(2,1)S(1)}, u32[]{:S(2)}, u32[]{:S(2)}) collective-permute-start(bf16[2,2,6,32,128]{4,3,2,1,0:T(8,128)(2,1)S(1)} %pad_maximum_fusion.3), channel_id=1, source_target_pairs={{0,4},{1,5},{2,6},{3,7},{5,1},{7,3},{8,12},{9,13},{10,14},{11,15},... | collective-permute-start | bytes 589832 | tf_op jit(solution)/shard_map/ppermute | solution.py:293
  26.2 1.9 %collective-permute-start.2 = (bf16[2,2,6,32,128]{4,3,2,1,0:T(8,128)(2,1)S(1)}, bf16[2,2,6,32,128]{4,3,2,1,0:T(8,128)(2,1)S(1)}, u32[]{:S(2)}, u32[]{:S(2)}) collective-permute-start(bf16[2,2,6,32,128]{4,3,2,1,0:T(8,128)(2,1)S(1)} %pad_maximum_fusion.4), channel_id=1, source_target_pairs={{0,2},{1,3},{2,4},{3,5},{5,7},{7,1},{8,10},{9,11},{10,12},{11,13},... | collective-permute-start | bytes 589832 | tf_op jit(solution)/shard_map/ppermute | solution.py:293
  28.2 0.0 copy-start.1
  28.2 0.0 copy-start
  28.2 4.1 %collective-permute-start.3 = (bf16[2,2,6,32,128]{4,3,2,1,0:T(8,128)(2,1)S(1)}, bf16[2,2,6,32,128]{4,3,2,1,0:T(8,128)(2,1)S(1)}, u32[]{:S(2)}, u32[]{:S(2)}) collective-permute-start(bf16[2,2,6,32,128]{4,3,2,1,0:T(8,128)(2,1)S(1)} %pad_maximum_fusion.5), channel_id=1, source_target_pairs={{0,6},{1,7},{2,0},{3,1},{5,3},{7,5},{8,14},{9,15},{10,8},{11,9},{1... | collective-permute-start | bytes 589832 | tf_op jit(solution)/shard_map/ppermute | solution.py:293
  32.3 0.0 copy-start.2
  32.3 0.0 copy-start.3
  32.3 0.0 collective-permute-done.1.refs_1_
  32.4 1.4 %collective-permute-done.2.refs_2_ = bf16[2,2,6,32,128]{4,3,2,1,0:T(8,128)(2,1)S(1)} collective-permute-done((bf16[2,2,6,32,128]{4,3,2,1,0:T(8,128)(2,1)S(1)}, bf16[2,2,6,32,128]{4,3,2,1,0:T(8,128)(2,1)S(1)}, u32[]{:S(2)}, u32[]{:S(2)}) %collective-permute-start.2) | collective-permute-done | bytes 196640 | tf_op jit(solution)/shard_map/ppermute | solution.py:293
  33.8 1.7 %collective-permute-done.3.refs_3_ = bf16[2,2,6,32,128]{4,3,2,1,0:T(8,128)(2,1)S(1)} collective-permute-done((bf16[2,2,6,32,128]{4,3,2,1,0:T(8,128)(2,1)S(1)}, bf16[2,2,6,32,128]{4,3,2,1,0:T(8,128)(2,1)S(1)}, u32[]{:S(2)}, u32[]{:S(2)}) %collective-permute-start.3) | collective-permute-done | bytes 196640 | tf_op jit(solution)/shard_map/ppermute | solution.py:293
  35.4 0.0 copy-done.1
  35.5 0.0 copy-done
  35.5 0.0 copy-done.2
  35.5 0.0 copy-done.3
  35.5 2.2 %early.1 = (f32[2,16,32,128]{3,2,1,0:T(8,128)S(1)}, bf16[256,256]{1,0:T(8,128)(2,1)S(1)}) custom-call(s32[1]{0:T(128)} %bitcast.1.core, s32[1]{0:T(128)} %bitcast.2.column, s32[1]{0:T(128)} %bitcast.station, bf16[2,2,6,32,128]{4,3,2,1,0:T(8,128)(2,1)S(1)} %pad_maximum_fusion.2.refs_0_, bf16[2,2,6,32,128]{4,3,2,1,0:T(8,128)(2,1)S(1)} %collective-permute-done.1.refs_1_, ...), custom_call_target="tpu_custom_call" | custom-call | tf_op jit(solution)/shard_map/early/pallas_call | solution.py:137
  37.7 0.0 collective-permute-done.8.hist
  37.7 2.2 %rest.1 = bf16[256,768]{1,0:T(8,128)(2,1)S(1)} custom-call(s32[1]{0:T(128)} %bitcast.1.core, s32[1]{0:T(128)} %bitcast.2.column, s32[1]{0:T(128)} %bitcast.station, f32[2,16,32,128]{3,2,1,0:T(8,128)S(1)} %get-tuple-element.7.sums, bf16[2,15,32,128]{3,2,1,0:T(8,128)(2,1)S(1)} %collective-permute-done.8.hist, bf16[256,256]{1,0:T(8,128)(2,1)S(1)} %get-tuple-element.8.done, ...), custom_call_target="tpu_custom_call" | custom-call | tf_op jit(solution)/shard_map/rest/pallas_call | solution.py:137
  39.9 12.4 %all_to_all.15.x = bf16[8,32,768]{2,1,0:T(8,128)(2,1)S(1)} all-to-all(bf16[8,32,768]{2,1,0:T(8,128)(2,1)S(1)} %bitcast.42), channel_id=1, replica_groups=mesh['stn'=32,'zh'=2,'x'=4,'c'=2] {'x','c'}, dimensions={0} | all-to-all | bytes 786432 | tf_op jit(solution)/shard_map/all_to_all | solution.py:303
  52.3 0.2 regroup.1
  52.4 38.5 %all_to_all.16 = bf16[64,24,128]{2,1,0:T(8,128)(2,1)S(1)} all-to-all(bf16[64,24,128]{2,1,0:T(8,128)(2,1)S(1)} %bitcast.40), channel_id=1, replica_groups=mesh['stn'=32,'zh'=2,'x'=4,'c'=2] {'stn','zh'}, dimensions={0} | all-to-all | bytes 786432 | tf_op jit(solution)/shard_map/all_to_all | solution.py:305
  91.0 1.6 %correlate.1 = f32[32,64,128]{2,1,0:T(8,128)S(1)} custom-call(bf16[32,2,24,128]{3,2,1,0:T(8,128)(2,1)S(1)} %bitcast.41), custom_call_target="tpu_custom_call" | custom-call | tf_op jit(solution)/shard_map/correlate/pallas_call | solution.py:221
  92.6 0.1 convert_element_type.6
  92.7 33.1 %all_to_all.17 = f16[32,64,128]{2,1,0:T(8,128)(2,1)S(1)} all-to-all(f16[32,64,128]{2,1,0:T(8,128)(2,1)S(1)} %convert_element_type.6), channel_id=1, replica_groups=mesh['stn'=32,'zh'=2,'x'=4,'c'=2] {'stn'}, dimensions={0} | all-to-all | bytes 1048576 | tf_op jit(solution)/shard_map/all_to_all | solution.py:307
  125.8 0.1 convert_element_type.7.x
  125.8 1.9 %deliver.1 = f32[2,4,128,256]{3,2,1,0:T(8,128)} custom-call(s32[1]{0:T(128)} %bitcast.station, f32[32,64,128]{2,1,0:T(8,128)S(1)} %convert_element_type.7.x), custom_call_target="tpu_custom_call" | custom-call | tf_op jit(solution)/shard_map/deliver/pallas_call | solution.py:258
  (11 shorter events, 0.3 us)
Async XLA Ops:
  1.5 6.7 %collective-permute-start.4 = (bf16[2,6,32,128]{3,2,1,0:T(8,128)(2,1)S(1)}, bf16[2,6,32,128]{3,2,1,0:T(8,128)(2,1)S(1)}, u32[]{:S(2)}, u32[]{:S(2)}) collective-permute-start(bf16[2,6,32,128]{3,2,1,0:T(8,128)(2,1)S(1)} %get-tuple-element.12), channel_id=1, source_target_pairs={{5,2},{6,4},{7,6},{21,18},{22,20},{23,22},{37,34},{38,36},{39,38},... | collective-permute-start | bytes 294920 | tf_op jit(solution)/shard_map/ppermute | solution.py:276
  2.8 5.4 %collective-permute-start.5 = (bf16[2,6,32,128]{3,2,1,0:T(8,128)(2,1)S(1)}, bf16[2,6,32,128]{3,2,1,0:T(8,128)(2,1)S(1)}, u32[]{:S(2)}, u32[]{:S(2)}) collective-permute-start(bf16[2,6,32,128]{3,2,1,0:T(8,128)(2,1)S(1)} %get-tuple-element.13), channel_id=1, source_target_pairs={{5,4},{6,6},{7,0},{21,20},{22,22},{23,16},{37,36},{38,38},{39,32},... | collective-permute-start | bytes 294920 | tf_op jit(solution)/shard_map/ppermute | solution.py:276
  3.5 11.9 %collective-permute-start.6 = (bf16[2,6,32,128]{3,2,1,0:T(8,128)(2,1)S(1)}, bf16[2,6,32,128]{3,2,1,0:T(8,128)(2,1)S(1)}, u32[]{:S(2)}, u32[]{:S(2)}) collective-permute-start(bf16[2,6,32,128]{3,2,1,0:T(8,128)(2,1)S(1)} %get-tuple-element.14), channel_id=1, source_target_pairs={{5,6},{6,0},{7,2},{21,22},{22,16},{23,18},{37,38},{38,32},{39,34},... | collective-permute-start | bytes 294920 | tf_op jit(solution)/shard_map/ppermute | solution.py:276
  4.8 12.9 %collective-permute-start.7 = (bf16[2,6,32,128]{3,2,1,0:T(8,128)(2,1)S(1)}, bf16[2,6,32,128]{3,2,1,0:T(8,128)(2,1)S(1)}, u32[]{:S(2)}, u32[]{:S(2)}) collective-permute-start(bf16[2,6,32,128]{3,2,1,0:T(8,128)(2,1)S(1)} %get-tuple-element.15), channel_id=1, source_target_pairs={{5,0},{6,2},{7,4},{21,16},{22,18},{23,20},{37,32},{38,34},{39,36},... | collective-permute-start | bytes 294920 | tf_op jit(solution)/shard_map/ppermute | solution.py:276
  6.1 16.1 %collective-permute-start = (bf16[2,4,6,32,128]{4,3,2,0,1:T(8,128)(2,1)S(1)}, bf16[2,4,6,32,128]{4,3,2,0,1:T(8,128)(2,1)S(1)}, u32[]{:S(2)}, u32[]{:S(2)}) collective-permute-start(bf16[2,4,6,32,128]{4,3,2,0,1:T(8,128)(2,1)S(1)} %copy.6), channel_id=1, source_target_pairs={{0,1},{1,0},{2,3},{3,2},{4,5},{6,7},{8,9},{9,8},{10,11},{11,10},{1... | collective-permute-start | bytes 1179656 | tf_op jit(solution)/shard_map/ppermute | solution.py:287
  17.8 19.9 %collective-permute-start.8 = (bf16[2,15,32,128]{3,2,1,0:T(8,128)(2,1)S(1)}, bf16[2,15,32,128]{3,2,1,0:T(8,128)(2,1)S(1)}, u32[]{:S(2)}, u32[]{:S(2)}) collective-permute-start(bf16[2,15,32,128]{3,2,1,0:T(8,128)(2,1)S(1)} %pad_maximum_fusion.1), channel_id=1, source_target_pairs={{0,8},{2,10},{4,12},{6,14},{16,24},{18,26},{20,28},{22,30},{32,40}... | collective-permute-start | bytes 737288 | tf_op jit(solution)/shard_map/ppermute | solution.py:282
  22.3 10.0 %collective-permute-start.1 = (bf16[2,2,6,32,128]{4,3,2,1,0:T(8,128)(2,1)S(1)}, bf16[2,2,6,32,128]{4,3,2,1,0:T(8,128)(2,1)S(1)}, u32[]{:S(2)}, u32[]{:S(2)}) collective-permute-start(bf16[2,2,6,32,128]{4,3,2,1,0:T(8,128)(2,1)S(1)} %pad_maximum_fusion.3), channel_id=1, source_target_pairs={{0,4},{1,5},{2,6},{3,7},{5,1},{7,3},{8,12},{9,13},{10,14},{11,15},... | collective-permute-start | bytes 589832 | tf_op jit(solution)/shard_map/ppermute | solution.py:293
  26.2 7.6 %collective-permute-start.2 = (bf16[2,2,6,32,128]{4,3,2,1,0:T(8,128)(2,1)S(1)}, bf16[2,2,6,32,128]{4,3,2,1,0:T(8,128)(2,1)S(1)}, u32[]{:S(2)}, u32[]{:S(2)}) collective-permute-start(bf16[2,2,6,32,128]{4,3,2,1,0:T(8,128)(2,1)S(1)} %pad_maximum_fusion.4), channel_id=1, source_target_pairs={{0,2},{1,3},{2,4},{3,5},{5,7},{7,1},{8,10},{9,11},{10,12},{11,13},... | collective-permute-start | bytes 589832 | tf_op jit(solution)/shard_map/ppermute | solution.py:293
  28.2 7.3 %copy-start.1 = (f32[16,32,128]{2,1,0:T(8,128)S(1)}, f32[16,32,128]{2,1,0:T(8,128)}, u32[]{:S(2)}) copy-start(f32[16,32,128]{2,1,0:T(8,128)} %constant.123.clone.refs_4_.taps) | copy-start | bytes 786436
  28.2 7.3 %copy-start = (bf16[512,256]{1,0:T(8,128)(2,1)S(1)}, bf16[512,256]{1,0:T(8,128)(2,1)}, u32[]{:S(2)}) copy-start(bf16[512,256]{1,0:T(8,128)(2,1)} %constant.125.clone.refs_6_.second) | copy-start | bytes 786436
  28.2 7.2 %collective-permute-start.3 = (bf16[2,2,6,32,128]{4,3,2,1,0:T(8,128)(2,1)S(1)}, bf16[2,2,6,32,128]{4,3,2,1,0:T(8,128)(2,1)S(1)}, u32[]{:S(2)}, u32[]{:S(2)}) collective-permute-start(bf16[2,2,6,32,128]{4,3,2,1,0:T(8,128)(2,1)S(1)} %pad_maximum_fusion.5), channel_id=1, source_target_pairs={{0,6},{1,7},{2,0},{3,1},{5,3},{7,5},{8,14},{9,15},{10,8},{11,9},{1... | collective-permute-start | bytes 589832 | tf_op jit(solution)/shard_map/ppermute | solution.py:293
  32.3 3.2 %copy-start.2 = (f32[2,32,128]{2,1,0:T(8,128)S(1)}, f32[2,32,128]{2,1,0:T(8,128)}, u32[]{:S(2)}) copy-start(f32[2,32,128]{2,1,0:T(8,128)} %constant.126.clone.refs_7_.twiddle) | copy-start | bytes 98308
  32.3 3.2 %copy-start.3 = (bf16[128,64]{1,0:T(8,128)(2,1)S(1)}, bf16[128,64]{1,0:T(8,128)(2,1)}, u32[]{:S(2)}) copy-start(bf16[128,64]{1,0:T(8,128)(2,1)} %constant.124.clone.refs_5_.first) | copy-start | bytes 49156

commit v12 on v11

--- a/solution.py
+++ b/solution.py
@@ -204,7 +204,7 @@
             rows = [series[pl.ds(32 * r + 8 * i + j, STN, stride=64), :] for i in range(PER)]
             right.append(jnp.concatenate(rows, 0))
         right = jnp.concatenate(right, 1).astype(BF16)
-        tile = lax.dot_general(left, right, NT, preferred_element_type=F32) / FRAMES
+        tile = lax.dot_general(left, right, NT, preferred_element_type=F32) * (1.0 / FRAMES)
         tile = tile.reshape(STN, 8, 128)
         plain[:, 8 * j : 8 * j + 8, :] = tile
         most = jnp.maximum(most, jnp.max(jnp.abs(tile), 0))

time: 128 us -> 128 us (level)
  no operation moved by 1% of the time
where the time goes in v12:
time: 128 us
  blocking collectives  84 us (66%)
  starting transfers between devices  20.7 us (16%)
  waiting for transfers between devices  12.6 us (10%)
  Pallas kernels  8.05 us (6%)
  local copies, waits for them, and re-layouts  1.61 us (1%)
    all_to_all x1, blocking collectives, shards(): spectra = lax.all_to_all(spectra, ('stn', 'zh'), 0, 0, tiled=True)  38.5 us
    all_to_all x1, blocking collectives, shards(): lax.all_to_all(products.astype(jnp.float16), 'stn', 0, 0, tiled=True)  33.1 us
    all_to_all x1, blocking collectives, shards(): lax.all_to_all(spectra.reshape(Q, 2 * N2 // Q, N1 * BLOCK), ('x', 'c'), 0...  12.4 us
    ppermute x3, starting transfers between devices, half_of_input(): pieces.append(lax.ppermute(piece, ('x', 'c'), pairs) if p else piece)  9.87 us
    ppermute x4, waiting for transfers between devices, last_frames(): rounds.append(lax.ppermute(piece, ('zh', 'x', 'c'), pairs))  9.51 us
    ppermute x4, starting transfers between devices, last_frames(): rounds.append(lax.ppermute(piece, ('zh', 'x', 'c'), pairs))  4.54 us
    pallas_call x2, Pallas kernels, kernel(): pl.pallas_call(body, out_shape=out_shape, in_specs=[pl.BlockSpec(memory_s...  4.41 us
    ppermute x1, starting transfers between devices, last_frames(): lax.ppermute(last, ('zh', 'x', 'c'), [(Q // X * x, Q + Q // X * x) for x...  4.38 us
  transfers between devices with their start and end apart: 9, of which 4 were waited for; matrix products, arithmetic and copies ran while one was open for 0% of the time, Pallas kernels for 2%

profile of v12, /device:TPU:2, one launch (start us, length us, event | category | flops | bytes accessed | tf_op | source)
XLA Modules:
  0.0 127.7 jit_solution(9466548322694633995)
XLA Ops:
  0.0 1.4 %reshape.32 = bf16[2,4,6,32,128]{4,3,2,1,0:T(8,128)(2,1)S(1)} reshape(bf16[2,4,24576]{2,1,0:T(4,128)(2,1)} %param.5) | data formatting | bytes 786432 | tf_op jit(solution)/shard_map/reshape | solution.py:298
  1.5 1.3 %collective-permute-start.4 = (bf16[2,6,32,128]{3,2,1,0:T(8,128)(2,1)S(1)}, bf16[2,6,32,128]{3,2,1,0:T(8,128)(2,1)S(1)}, u32[]{:S(2)}, u32[]{:S(2)}) collective-permute-start(bf16[2,6,32,128]{3,2,1,0:T(8,128)(2,1)S(1)} %get-tuple-element.12), channel_id=1, source_target_pairs={{5,2},{6,4},{7,6},{21,18},{22,20},{23,22},{37,34},{38,36},{39,38},... | collective-permute-start | bytes 294920 | tf_op jit(solution)/shard_map/ppermute | solution.py:276
  2.8 0.7 collective-permute-start.5
  3.5 1.3 %collective-permute-start.6 = (bf16[2,6,32,128]{3,2,1,0:T(8,128)(2,1)S(1)}, bf16[2,6,32,128]{3,2,1,0:T(8,128)(2,1)S(1)}, u32[]{:S(2)}, u32[]{:S(2)}) collective-permute-start(bf16[2,6,32,128]{3,2,1,0:T(8,128)(2,1)S(1)} %get-tuple-element.14), channel_id=1, source_target_pairs={{5,6},{6,0},{7,2},{21,22},{22,16},{23,18},{37,38},{38,32},{39,34},... | collective-permute-start | bytes 294920 | tf_op jit(solution)/shard_map/ppermute | solution.py:276
  4.8 1.3 %collective-permute-start.7 = (bf16[2,6,32,128]{3,2,1,0:T(8,128)(2,1)S(1)}, bf16[2,6,32,128]{3,2,1,0:T(8,128)(2,1)S(1)}, u32[]{:S(2)}, u32[]{:S(2)}) collective-permute-start(bf16[2,6,32,128]{3,2,1,0:T(8,128)(2,1)S(1)} %get-tuple-element.15), channel_id=1, source_target_pairs={{5,0},{6,2},{7,4},{21,16},{22,18},{23,20},{37,32},{38,34},{39,36},... | collective-permute-start | bytes 294920 | tf_op jit(solution)/shard_map/ppermute | solution.py:276
  6.1 1.9 %collective-permute-start = (bf16[2,4,6,32,128]{4,3,2,0,1:T(8,128)(2,1)S(1)}, bf16[2,4,6,32,128]{4,3,2,0,1:T(8,128)(2,1)S(1)}, u32[]{:S(2)}, u32[]{:S(2)}) collective-permute-start(bf16[2,4,6,32,128]{4,3,2,0,1:T(8,128)(2,1)S(1)} %copy.6), channel_id=1, source_target_pairs={{0,1},{1,0},{2,3},{3,2},{4,5},{6,7},{8,9},{9,8},{10,11},{11,10},{1... | collective-permute-start | bytes 1179656 | tf_op jit(solution)/shard_map/ppermute | solution.py:287
  8.2 0.0 collective-permute-done.4
  8.2 0.0 collective-permute-done.5
  8.2 7.2 %collective-permute-done.6 = bf16[2,6,32,128]{3,2,1,0:T(8,128)(2,1)S(1)} collective-permute-done((bf16[2,6,32,128]{3,2,1,0:T(8,128)(2,1)S(1)}, bf16[2,6,32,128]{3,2,1,0:T(8,128)(2,1)S(1)}, u32[]{:S(2)}, u32[]{:S(2)}) %collective-permute-start.6) | collective-permute-done | bytes 98336 | tf_op jit(solution)/shard_map/ppermute | solution.py:276
  15.3 2.4 %collective-permute-done.7 = bf16[2,6,32,128]{3,2,1,0:T(8,128)(2,1)S(1)} collective-permute-done((bf16[2,6,32,128]{3,2,1,0:T(8,128)(2,1)S(1)}, bf16[2,6,32,128]{3,2,1,0:T(8,128)(2,1)S(1)}, u32[]{:S(2)}, u32[]{:S(2)}) %collective-permute-start.7) | collective-permute-done | bytes 98336 | tf_op jit(solution)/shard_map/ppermute | solution.py:276
  17.7 0.1 pad_maximum_fusion
  17.8 4.4 %collective-permute-start.8 = (bf16[2,15,32,128]{3,2,1,0:T(8,128)(2,1)S(1)}, bf16[2,15,32,128]{3,2,1,0:T(8,128)(2,1)S(1)}, u32[]{:S(2)}, u32[]{:S(2)}) collective-permute-start(bf16[2,15,32,128]{3,2,1,0:T(8,128)(2,1)S(1)} %pad_maximum_fusion.1), channel_id=1, source_target_pairs={{0,8},{2,10},{4,12},{6,14},{16,24},{18,26},{20,28},{22,30},{32,40}... | collective-permute-start | bytes 737288 | tf_op jit(solution)/shard_map/ppermute | solution.py:282
  22.2 0.0 collective-permute-done
  22.3 3.9 %collective-permute-start.1 = (bf16[2,2,6,32,128]{4,3,2,1,0:T(8,128)(2,1)S(1)}, bf16[2,2,6,32,128]{4,3,2,1,0:T(8,128)(2,1)S(1)}, u32[]{:S(2)}, u32[]{:S(2)}) collective-permute-start(bf16[2,2,6,32,128]{4,3,2,1,0:T(8,128)(2,1)S(1)} %pad_maximum_fusion.3), channel_id=1, source_target_pairs={{0,4},{1,5},{2,6},{3,7},{5,1},{7,3},{8,12},{9,13},{10,14},{11,15},... | collective-permute-start | bytes 589832 | tf_op jit(solution)/shard_map/ppermute | solution.py:293
  26.2 1.9 %collective-permute-start.2 = (bf16[2,2,6,32,128]{4,3,2,1,0:T(8,128)(2,1)S(1)}, bf16[2,2,6,32,128]{4,3,2,1,0:T(8,128)(2,1)S(1)}, u32[]{:S(2)}, u32[]{:S(2)}) collective-permute-start(bf16[2,2,6,32,128]{4,3,2,1,0:T(8,128)(2,1)S(1)} %pad_maximum_fusion.4), channel_id=1, source_target_pairs={{0,2},{1,3},{2,4},{3,5},{5,7},{7,1},{8,10},{9,11},{10,12},{11,13},... | collective-permute-start | bytes 589832 | tf_op jit(solution)/shard_map/ppermute | solution.py:293
  28.2 0.0 copy-start.1
  28.2 0.0 copy-start
  28.2 4.1 %collective-permute-start.3 = (bf16[2,2,6,32,128]{4,3,2,1,0:T(8,128)(2,1)S(1)}, bf16[2,2,6,32,128]{4,3,2,1,0:T(8,128)(2,1)S(1)}, u32[]{:S(2)}, u32[]{:S(2)}) collective-permute-start(bf16[2,2,6,32,128]{4,3,2,1,0:T(8,128)(2,1)S(1)} %pad_maximum_fusion.5), channel_id=1, source_target_pairs={{0,6},{1,7},{2,0},{3,1},{5,3},{7,5},{8,14},{9,15},{10,8},{11,9},{1... | collective-permute-start | bytes 589832 | tf_op jit(solution)/shard_map/ppermute | solution.py:293
  32.3 0.0 copy-start.2
  32.3 0.0 copy-start.3
  32.3 0.0 collective-permute-done.1.refs_1_
  32.4 1.4 %collective-permute-done.2.refs_2_ = bf16[2,2,6,32,128]{4,3,2,1,0:T(8,128)(2,1)S(1)} collective-permute-done((bf16[2,2,6,32,128]{4,3,2,1,0:T(8,128)(2,1)S(1)}, bf16[2,2,6,32,128]{4,3,2,1,0:T(8,128)(2,1)S(1)}, u32[]{:S(2)}, u32[]{:S(2)}) %collective-permute-start.2) | collective-permute-done | bytes 196640 | tf_op jit(solution)/shard_map/ppermute | solution.py:293
  33.8 1.7 %collective-permute-done.3.refs_3_ = bf16[2,2,6,32,128]{4,3,2,1,0:T(8,128)(2,1)S(1)} collective-permute-done((bf16[2,2,6,32,128]{4,3,2,1,0:T(8,128)(2,1)S(1)}, bf16[2,2,6,32,128]{4,3,2,1,0:T(8,128)(2,1)S(1)}, u32[]{:S(2)}, u32[]{:S(2)}) %collective-permute-start.3) | collective-permute-done | bytes 196640 | tf_op jit(solution)/shard_map/ppermute | solution.py:293
  35.4 0.0 copy-done.1
  35.5 0.0 copy-done
  35.5 0.0 copy-done.2
  35.5 0.0 copy-done.3
  35.5 2.2 %early.1 = (f32[2,16,32,128]{3,2,1,0:T(8,128)S(1)}, bf16[256,256]{1,0:T(8,128)(2,1)S(1)}) custom-call(s32[1]{0:T(128)} %bitcast.1.core, s32[1]{0:T(128)} %bitcast.2.column, s32[1]{0:T(128)} %bitcast.station, bf16[2,2,6,32,128]{4,3,2,1,0:T(8,128)(2,1)S(1)} %pad_maximum_fusion.2.refs_0_, bf16[2,2,6,32,128]{4,3,2,1,0:T(8,128)(2,1)S(1)} %collective-permute-done.1.refs_1_, ...), custom_call_target="tpu_custom_call" | custom-call | tf_op jit(solution)/shard_map/early/pallas_call | solution.py:137
  37.7 0.0 collective-permute-done.8.hist
  37.7 2.2 %rest.1 = bf16[256,768]{1,0:T(8,128)(2,1)S(1)} custom-call(s32[1]{0:T(128)} %bitcast.1.core, s32[1]{0:T(128)} %bitcast.2.column, s32[1]{0:T(128)} %bitcast.station, f32[2,16,32,128]{3,2,1,0:T(8,128)S(1)} %get-tuple-element.7.sums, bf16[2,15,32,128]{3,2,1,0:T(8,128)(2,1)S(1)} %collective-permute-done.8.hist, bf16[256,256]{1,0:T(8,128)(2,1)S(1)} %get-tuple-element.8.done, ...), custom_call_target="tpu_custom_call" | custom-call | tf_op jit(solution)/shard_map/rest/pallas_call | solution.py:137
  39.9 12.4 %all_to_all.15.x = bf16[8,32,768]{2,1,0:T(8,128)(2,1)S(1)} all-to-all(bf16[8,32,768]{2,1,0:T(8,128)(2,1)S(1)} %bitcast.42), channel_id=1, replica_groups=mesh['stn'=32,'zh'=2,'x'=4,'c'=2] {'x','c'}, dimensions={0} | all-to-all | bytes 786432 | tf_op jit(solution)/shard_map/all_to_all | solution.py:303
  52.3 0.2 regroup.1
  52.4 38.5 %all_to_all.16 = bf16[64,24,128]{2,1,0:T(8,128)(2,1)S(1)} all-to-all(bf16[64,24,128]{2,1,0:T(8,128)(2,1)S(1)} %bitcast.40), channel_id=1, replica_groups=mesh['stn'=32,'zh'=2,'x'=4,'c'=2] {'stn','zh'}, dimensions={0} | all-to-all | bytes 786432 | tf_op jit(solution)/shard_map/all_to_all | solution.py:305
  91.0 1.6 %correlate.1 = f32[32,64,128]{2,1,0:T(8,128)S(1)} custom-call(bf16[32,2,24,128]{3,2,1,0:T(8,128)(2,1)S(1)} %bitcast.41), custom_call_target="tpu_custom_call" | custom-call | tf_op jit(solution)/shard_map/correlate/pallas_call | solution.py:221
  92.6 0.1 convert_element_type.6
  92.7 33.1 %all_to_all.17 = f16[32,64,128]{2,1,0:T(8,128)(2,1)S(1)} all-to-all(f16[32,64,128]{2,1,0:T(8,128)(2,1)S(1)} %convert_element_type.6), channel_id=1, replica_groups=mesh['stn'=32,'zh'=2,'x'=4,'c'=2] {'stn'}, dimensions={0} | all-to-all | bytes 1048576 | tf_op jit(solution)/shard_map/all_to_all | solution.py:307
  125.8 0.1 convert_element_type.7.x
  125.8 1.9 %deliver.1 = f32[2,4,128,256]{3,2,1,0:T(8,128)} custom-call(s32[1]{0:T(128)} %bitcast.station, f32[32,64,128]{2,1,0:T(8,128)S(1)} %convert_element_type.7.x), custom_call_target="tpu_custom_call" | custom-call | tf_op jit(solution)/shard_map/deliver/pallas_call | solution.py:258
  (11 shorter events, 0.3 us)
Async XLA Ops:
  1.5 6.7 %collective-permute-start.4 = (bf16[2,6,32,128]{3,2,1,0:T(8,128)(2,1)S(1)}, bf16[2,6,32,128]{3,2,1,0:T(8,128)(2,1)S(1)}, u32[]{:S(2)}, u32[]{:S(2)}) collective-permute-start(bf16[2,6,32,128]{3,2,1,0:T(8,128)(2,1)S(1)} %get-tuple-element.12), channel_id=1, source_target_pairs={{5,2},{6,4},{7,6},{21,18},{22,20},{23,22},{37,34},{38,36},{39,38},... | collective-permute-start | bytes 294920 | tf_op jit(solution)/shard_map/ppermute | solution.py:276
  2.8 5.4 %collective-permute-start.5 = (bf16[2,6,32,128]{3,2,1,0:T(8,128)(2,1)S(1)}, bf16[2,6,32,128]{3,2,1,0:T(8,128)(2,1)S(1)}, u32[]{:S(2)}, u32[]{:S(2)}) collective-permute-start(bf16[2,6,32,128]{3,2,1,0:T(8,128)(2,1)S(1)} %get-tuple-element.13), channel_id=1, source_target_pairs={{5,4},{6,6},{7,0},{21,20},{22,22},{23,16},{37,36},{38,38},{39,32},... | collective-permute-start | bytes 294920 | tf_op jit(solution)/shard_map/ppermute | solution.py:276
  3.5 11.9 %collective-permute-start.6 = (bf16[2,6,32,128]{3,2,1,0:T(8,128)(2,1)S(1)}, bf16[2,6,32,128]{3,2,1,0:T(8,128)(2,1)S(1)}, u32[]{:S(2)}, u32[]{:S(2)}) collective-permute-start(bf16[2,6,32,128]{3,2,1,0:T(8,128)(2,1)S(1)} %get-tuple-element.14), channel_id=1, source_target_pairs={{5,6},{6,0},{7,2},{21,22},{22,16},{23,18},{37,38},{38,32},{39,34},... | collective-permute-start | bytes 294920 | tf_op jit(solution)/shard_map/ppermute | solution.py:276
  4.8 12.9 %collective-permute-start.7 = (bf16[2,6,32,128]{3,2,1,0:T(8,128)(2,1)S(1)}, bf16[2,6,32,128]{3,2,1,0:T(8,128)(2,1)S(1)}, u32[]{:S(2)}, u32[]{:S(2)}) collective-permute-start(bf16[2,6,32,128]{3,2,1,0:T(8,128)(2,1)S(1)} %get-tuple-element.15), channel_id=1, source_target_pairs={{5,0},{6,2},{7,4},{21,16},{22,18},{23,20},{37,32},{38,34},{39,36},... | collective-permute-start | bytes 294920 | tf_op jit(solution)/shard_map/ppermute | solution.py:276
  6.1 16.1 %collective-permute-start = (bf16[2,4,6,32,128]{4,3,2,0,1:T(8,128)(2,1)S(1)}, bf16[2,4,6,32,128]{4,3,2,0,1:T(8,128)(2,1)S(1)}, u32[]{:S(2)}, u32[]{:S(2)}) collective-permute-start(bf16[2,4,6,32,128]{4,3,2,0,1:T(8,128)(2,1)S(1)} %copy.6), channel_id=1, source_target_pairs={{0,1},{1,0},{2,3},{3,2},{4,5},{6,7},{8,9},{9,8},{10,11},{11,10},{1... | collective-permute-start | bytes 1179656 | tf_op jit(solution)/shard_map/ppermute | solution.py:287
  17.8 19.9 %collective-permute-start.8 = (bf16[2,15,32,128]{3,2,1,0:T(8,128)(2,1)S(1)}, bf16[2,15,32,128]{3,2,1,0:T(8,128)(2,1)S(1)}, u32[]{:S(2)}, u32[]{:S(2)}) collective-permute-start(bf16[2,15,32,128]{3,2,1,0:T(8,128)(2,1)S(1)} %pad_maximum_fusion.1), channel_id=1, source_target_pairs={{0,8},{2,10},{4,12},{6,14},{16,24},{18,26},{20,28},{22,30},{32,40}... | collective-permute-start | bytes 737288 | tf_op jit(solution)/shard_map/ppermute | solution.py:282
  22.3 10.0 %collective-permute-start.1 = (bf16[2,2,6,32,128]{4,3,2,1,0:T(8,128)(2,1)S(1)}, bf16[2,2,6,32,128]{4,3,2,1,0:T(8,128)(2,1)S(1)}, u32[]{:S(2)}, u32[]{:S(2)}) collective-permute-start(bf16[2,2,6,32,128]{4,3,2,1,0:T(8,128)(2,1)S(1)} %pad_maximum_fusion.3), channel_id=1, source_target_pairs={{0,4},{1,5},{2,6},{3,7},{5,1},{7,3},{8,12},{9,13},{10,14},{11,15},... | collective-permute-start | bytes 589832 | tf_op jit(solution)/shard_map/ppermute | solution.py:293
  26.2 7.6 %collective-permute-start.2 = (bf16[2,2,6,32,128]{4,3,2,1,0:T(8,128)(2,1)S(1)}, bf16[2,2,6,32,128]{4,3,2,1,0:T(8,128)(2,1)S(1)}, u32[]{:S(2)}, u32[]{:S(2)}) collective-permute-start(bf16[2,2,6,32,128]{4,3,2,1,0:T(8,128)(2,1)S(1)} %pad_maximum_fusion.4), channel_id=1, source_target_pairs={{0,2},{1,3},{2,4},{3,5},{5,7},{7,1},{8,10},{9,11},{10,12},{11,13},... | collective-permute-start | bytes 589832 | tf_op jit(solution)/shard_map/ppermute | solution.py:293
  28.2 7.3 %copy-start.1 = (f32[16,32,128]{2,1,0:T(8,128)S(1)}, f32[16,32,128]{2,1,0:T(8,128)}, u32[]{:S(2)}) copy-start(f32[16,32,128]{2,1,0:T(8,128)} %constant.123.clone.refs_4_.taps) | copy-start | bytes 786436
  28.2 7.3 %copy-start = (bf16[512,256]{1,0:T(8,128)(2,1)S(1)}, bf16[512,256]{1,0:T(8,128)(2,1)}, u32[]{:S(2)}) copy-start(bf16[512,256]{1,0:T(8,128)(2,1)} %constant.125.clone.refs_6_.second) | copy-start | bytes 786436
  28.2 7.2 %collective-permute-start.3 = (bf16[2,2,6,32,128]{4,3,2,1,0:T(8,128)(2,1)S(1)}, bf16[2,2,6,32,128]{4,3,2,1,0:T(8,128)(2,1)S(1)}, u32[]{:S(2)}, u32[]{:S(2)}) collective-permute-start(bf16[2,2,6,32,128]{4,3,2,1,0:T(8,128)(2,1)S(1)} %pad_maximum_fusion.5), channel_id=1, source_target_pairs={{0,6},{1,7},{2,0},{3,1},{5,3},{7,5},{8,14},{9,15},{10,8},{11,9},{1... | collective-permute-start | bytes 589832 | tf_op jit(solution)/shard_map/ppermute | solution.py:293
  32.3 3.2 %copy-start.2 = (f32[2,32,128]{2,1,0:T(8,128)S(1)}, f32[2,32,128]{2,1,0:T(8,128)}, u32[]{:S(2)}) copy-start(f32[2,32,128]{2,1,0:T(8,128)} %constant.126.clone.refs_7_.twiddle) | copy-start | bytes 98308
  32.3 3.2 %copy-start.3 = (bf16[128,64]{1,0:T(8,128)(2,1)S(1)}, bf16[128,64]{1,0:T(8,128)(2,1)}, u32[]{:S(2)}) copy-start(bf16[128,64]{1,0:T(8,128)(2,1)} %constant.124.clone.refs_5_.first) | copy-start | bytes 49156
